TPU v7x, 32 devices: a whole 2x2x4 slice. The times are simulated.
32 devices in a mesh: rep: 4 (over y, x), ep: 8 (over z, core).
Axes of the slice: x: 2, y: 2, z: 4, core: 2. Of those that a mesh axis runs over, the one named last changes fastest.
Arguments:
- tokens: bfloat16 [8192, 768], P(('rep', 'ep')), may hold values from -6 to 6
- segment_ids: int32 [4, 2048], P('rep', 'ep'), may hold values from 0 to 3, never falling along the last dimension, each value on 1 to 1024 neighbouring positions
- routes: int32 [8192, 2], P(('rep', 'ep')), may hold values from 0 to 7, all different within a row; in each aligned block of 256 rows (0 to 255, 256 to 511, ...) at most 128 rows name the same one
- norm1_gain: bfloat16 [768], P(('rep', 'ep')), may hold values from 0.5 to 1.5
- w_query: bfloat16 [768, 768], P(('rep', 'ep')), may hold values from -0.3125 to 0.3125
- w_key: bfloat16 [768, 768], P(('rep', 'ep')), may hold values from -0.3125 to 0.3125
- w_value: bfloat16 [768, 768], P(('rep', 'ep')), may hold values from -0.21875 to 0.21875
- w_out: bfloat16 [768, 768], P(('rep', 'ep')), may hold values from -1.25 to 1.25
- norm2_gain: bfloat16 [768], P(('rep', 'ep')), may hold values from 0.5 to 1.5
- w_router: bfloat16 [768, 8], P(('rep', 'ep')), may hold values from -0.15625 to 0.15625
- shared_gate: bfloat16 [768, 2048], P(('rep', 'ep')), may hold values from -0.21875 to 0.21875
- shared_up: bfloat16 [768, 2048], P(('rep', 'ep')), may hold values from -0.21875 to 0.21875
- shared_down: bfloat16 [2048, 768], P(('rep', 'ep')), may hold values from -0.1875 to 0.1875
- expert_gate: bfloat16 [8, 768, 2048], P('ep'), may hold values from -0.21875 to 0.21875
- expert_up: bfloat16 [8, 768, 2048], P('ep'), may hold values from -0.21875 to 0.21875
- expert_down: bfloat16 [8, 2048, 768], P('ep'), may hold values from -1.5 to 1.5
- out_grad: bfloat16 [8192, 768], P(('rep', 'ep')), may hold values from -6 to 6
Outputs:
- layer_out: bfloat16 [8192, 768], P(('rep', 'ep'))
- tokens_grad: float32 [8192, 768], P(('rep', 'ep'))
- norm1_gain_grad: float32 [768], P(('rep', 'ep'))
- w_query_grad: float32 [768, 768], P(('rep', 'ep'))
- w_key_grad: float32 [768, 768], P(('rep', 'ep'))
- w_value_grad: float32 [768, 768], P(('rep', 'ep'))
- w_out_grad: float32 [768, 768], P(('rep', 'ep'))
- norm2_gain_grad: float32 [768], P(('rep', 'ep'))
- w_router_grad: float32 [768, 8], P(('rep', 'ep'))
- shared_gate_grad: float32 [768, 2048], P(('rep', 'ep'))
- shared_up_grad: float32 [768, 2048], P(('rep', 'ep'))
- shared_down_grad: float32 [2048, 768], P(('rep', 'ep'))
- expert_gate_grad: float32 [8, 768, 2048], P('ep', None, 'rep')
- expert_up_grad: float32 [8, 768, 2048], P('ep', None, 'rep')
- expert_down_grad: float32 [8, 2048, 768], P('ep', None, 'rep')
Inputs may be any that keep to these rules, and one draw needn't show every extreme that they name: `segment_ids`: along each pack of 2048 places the document number never falls; every document has 1 to 1024 places, and one has exactly 1024. `routes`: each token names 2 different experts. Among the 256 tokens of one device no expert is named more than 128 times, and in some device's tokens one expert is named exactly 128 times.
All inputs are finite; a program needn't handle non-finite values.
Results may differ from a plain program's by a relative error of at most 0.03.
Values may be sent and summed in bfloat16 or wider, within the bound.
No kernel may reach another device: no remote copies, remote signals or barrier semaphores. Data moves between devices by JAX's collectives and lax.ppermute only.
A program may use at most 256 MiB of HBM per device.

v0:
```python
import math

import jax
import jax.numpy as jnp
from jax import lax
from jax.sharding import PartitionSpec as P

HEADS = 12
BLOCK = 256


EPSILON = 1e-06
NEG_LARGE = -1e30


def times_transposed(former, latter):
    return lax.dot_general(
        former, latter, (((1,), (1,)), ((), ())), preferred_element_type=jnp.float32
    )


def transposed_times(former, latter):
    return lax.dot_general(
        former, latter, (((0,), (0,)), ((), ())), preferred_element_type=jnp.float32
    )


def rms_scale(values):
    return lax.rsqrt(jnp.mean(values * values, axis=1, keepdims=True) + EPSILON)


def norm_back(grad_normed, normed, scale_rows):
    return scale_rows * (
        grad_normed - normed * jnp.mean(grad_normed * normed, axis=1, keepdims=True)
    )


def silu_value(values):
    return values * jax.nn.sigmoid(values)


def silu_slope(values):
    logistic = jax.nn.sigmoid(values)
    return logistic * (1.0 + values * (1.0 - logistic))


def rotate(values, cosine_table, sine_table):
    halfway = values.shape[-1] // 2
    front_half = values[..., :halfway]
    back_half = values[..., halfway:]
    return jnp.concatenate(
        [
            front_half * cosine_table - back_half * sine_table,
            back_half * cosine_table + front_half * sine_table,
        ],
        axis=-1,
    )


def turn_tables(places, head_dim):
    halfway = head_dim // 2
    inverse = jnp.exp(
        jnp.arange(halfway).astype(jnp.float32) * (-2.0 * math.log(10000.0) / head_dim)
    )
    turned = places.astype(jnp.float32)[:, None] * inverse[None, :]
    return (jnp.cos(turned)[:, None, :], jnp.sin(turned)[:, None, :])


def allowed_pairs(query_segment, query_places, key_segment, key_places):
    same_doc = query_segment[:, None] == key_segment[None, :]
    earlier = key_places[None, :] // BLOCK <= query_places[:, None] // BLOCK
    return jnp.logical_and(same_doc, earlier)[None]


def shards(
    tokens,
    segment_ids,
    routes,
    norm1_gain,
    w_query,
    w_key,
    w_value,
    w_out,
    norm2_gain,
    w_router,
    shared_gate,
    shared_up,
    shared_down,
    expert_gate,
    expert_up,
    expert_down,
    out_grad,
):
    (
        first_norm_gain,
        query_matrix,
        key_matrix,
        value_matrix,
        output_matrix,
        second_norm_gain,
        router_matrix,
        shared_gate_full,
        shared_up_full,
        shared_down_full,
    ) = (
        lax.all_gather(norm1_gain, ("rep", "ep"), axis=0, tiled=True),
        lax.all_gather(w_query, ("rep", "ep"), axis=0, tiled=True),
        lax.all_gather(w_key, ("rep", "ep"), axis=0, tiled=True),
        lax.all_gather(w_value, ("rep", "ep"), axis=0, tiled=True),
        lax.all_gather(w_out, ("rep", "ep"), axis=0, tiled=True),
        lax.all_gather(norm2_gain, ("rep", "ep"), axis=0, tiled=True),
        lax.all_gather(w_router, ("rep", "ep"), axis=0, tiled=True),
        lax.all_gather(shared_gate, ("rep", "ep"), axis=0, tiled=True),
        lax.all_gather(shared_up, ("rep", "ep"), axis=0, tiled=True),
        lax.all_gather(shared_down, ("rep", "ep"), axis=0, tiled=True),
    )
    token_rows = tokens.shape[0]
    model_width = tokens.shape[1]
    head_count = HEADS
    head_dim = model_width // head_count
    score_scale = head_dim ** (-0.5)
    group_size = lax.axis_size("ep")
    whole_rows = token_rows * group_size
    step_rows = math.gcd(whole_rows, 512)
    top_count = routes.shape[1]
    experts = router_matrix.shape[1]
    local_experts = expert_gate.shape[0]
    capacity = 2 * token_rows * top_count // experts
    choice_count = token_rows * top_count
    places = lax.axis_index("ep") * token_rows + jnp.arange(token_rows, dtype=jnp.int32)
    cosine_table, sine_table = turn_tables(places, head_dim)
    own_segment = segment_ids.reshape(token_rows)
    layer_inputs = tokens.astype(jnp.float32)
    scale_first = rms_scale(layer_inputs)
    normed_first = layer_inputs * scale_first
    gain_first = first_norm_gain.astype(jnp.float32)
    hidden_first = (normed_first * gain_first).astype(jnp.bfloat16)
    query_raw = jnp.dot(hidden_first, query_matrix, preferred_element_type=jnp.float32).reshape(
        token_rows, head_count, head_dim
    )
    queries = rotate(query_raw, cosine_table, sine_table).astype(jnp.bfloat16)
    key_raw = jnp.dot(hidden_first, key_matrix, preferred_element_type=jnp.float32).reshape(
        token_rows, head_count, head_dim
    )
    keys_local = rotate(key_raw, cosine_table, sine_table).astype(jnp.bfloat16)
    values_local = (
        jnp.dot(hidden_first, value_matrix, preferred_element_type=jnp.float32)
        .astype(jnp.bfloat16)
        .reshape(token_rows, head_count, head_dim)
    )
    keys_flat = keys_local.reshape(token_rows, model_width)
    values_flat = values_local.reshape(token_rows, model_width)

    def key_update(carried, key_block, value_block, segment_block, block_start):
        running_max, running_total, running_acc = carried
        key_places = block_start + jnp.arange(key_block.shape[0], dtype=jnp.int32)
        allowed = allowed_pairs(own_segment, places, segment_block, key_places)
        scores = (
            jnp.einsum("qhd,khd->hqk", queries, key_block, preferred_element_type=jnp.float32)
            * score_scale
        )
        scores = jnp.where(allowed, scores, NEG_LARGE)
        new_max = jnp.maximum(running_max, jnp.max(scores, axis=2))
        factor = jnp.exp(running_max - new_max)
        weights = jnp.where(allowed, jnp.exp(scores - new_max[:, :, None]), 0.0)
        running_total = running_total * factor + jnp.sum(weights, axis=2)
        running_acc = running_acc * factor[:, :, None] + jnp.einsum(
            "hqk,khd->hqd",
            weights.astype(jnp.bfloat16),
            value_block,
            preferred_element_type=jnp.float32,
        )
        return (new_max, running_total, running_acc)

    start_state = (
        jnp.full((head_count, token_rows), NEG_LARGE, jnp.float32),
        jnp.zeros((head_count, token_rows), jnp.float32),
        jnp.zeros((head_count, token_rows, head_dim), jnp.float32),
    )
    carried = start_state
    key_piece = lax.all_gather(keys_flat, "ep", axis=0, tiled=True)
    value_piece = lax.all_gather(values_flat, "ep", axis=0, tiled=True)
    segment_piece = lax.all_gather(own_segment, "ep", axis=0, tiled=True)
    piece_rows = key_piece.shape[0]
    inner_rows = math.gcd(piece_rows, 512)

    def inner_step(inner_carried, block_index):
        offset = block_index * inner_rows
        key_block = lax.dynamic_slice_in_dim(key_piece, offset, inner_rows, 0).reshape(
            inner_rows, head_count, head_dim
        )
        value_block = lax.dynamic_slice_in_dim(value_piece, offset, inner_rows, 0).reshape(
            inner_rows, head_count, head_dim
        )
        segment_block = lax.dynamic_slice_in_dim(segment_piece, offset, inner_rows, 0)
        return (key_update(inner_carried, key_block, value_block, segment_block, offset), None)

    carried, unused = lax.scan(
        inner_step, carried, jnp.arange(piece_rows // inner_rows, dtype=jnp.int32)
    )
    final_max, final_total, final_acc = carried
    log_total = final_max + jnp.log(final_total)
    attended = final_acc / final_total[:, :, None]
    attended_low = (
        jnp.transpose(attended, (1, 0, 2)).reshape(token_rows, model_width).astype(jnp.bfloat16)
    )
    attn_result = jnp.dot(attended_low, output_matrix, preferred_element_type=jnp.float32)
    middle = layer_inputs + attn_result
    scale_second = rms_scale(middle)
    normed_second = middle * scale_second
    gain_second = second_norm_gain.astype(jnp.float32)
    hidden_second = (normed_second * gain_second).astype(jnp.bfloat16)
    logits = jnp.dot(hidden_second, router_matrix, preferred_element_type=jnp.float32)
    shifted = jnp.exp(logits - jnp.max(logits, axis=1, keepdims=True))
    router_probs = shifted / jnp.sum(shifted, axis=1, keepdims=True)
    route_table = (
        routes[:, :, None] == jnp.arange(experts, dtype=jnp.int32)[None, None, :]
    ).astype(jnp.float32)
    gate_values = jnp.sum(router_probs[:, None, :] * route_table, axis=2)
    shared_pre = jnp.dot(hidden_second, shared_gate_full, preferred_element_type=jnp.float32)
    shared_lin = jnp.dot(hidden_second, shared_up_full, preferred_element_type=jnp.float32)
    shared_hidden = (silu_value(shared_pre) * shared_lin).astype(jnp.bfloat16)
    shared_result = jnp.dot(shared_hidden, shared_down_full, preferred_element_type=jnp.float32)
    flat_routes = routes.reshape(choice_count)
    onehot = (flat_routes[:, None] == jnp.arange(experts, dtype=jnp.int32)[None, :]).astype(
        jnp.int32
    )
    own_rank = jnp.sum((jnp.cumsum(onehot, axis=0) - 1) * onehot, axis=1)
    slot_of_choice = flat_routes * capacity + own_rank
    slot_source = (
        jnp.full((experts * capacity,), choice_count, jnp.int32)
        .at[slot_of_choice]
        .set(jnp.arange(choice_count, dtype=jnp.int32))
    )
    slot_token_row = jnp.where(slot_source < choice_count, slot_source // top_count, token_rows)
    padded_rows = jnp.concatenate(
        [hidden_second, jnp.zeros((1, model_width), jnp.bfloat16)], axis=0
    )
    outgoing = padded_rows[slot_token_row].reshape(group_size, local_experts, capacity, model_width)
    received = lax.all_to_all(outgoing, "ep", split_axis=0, concat_axis=0, tiled=True)
    gate_pre = jnp.einsum(
        "sjcd,jdf->sjcf", received, expert_gate, preferred_element_type=jnp.float32
    )
    up_pre = jnp.einsum("sjcd,jdf->sjcf", received, expert_up, preferred_element_type=jnp.float32)
    expert_hidden = (silu_value(gate_pre) * up_pre).astype(jnp.bfloat16)
    expert_result = jnp.einsum(
        "sjcf,jfd->sjcd", expert_hidden, expert_down, preferred_element_type=jnp.float32
    ).astype(jnp.bfloat16)
    returned = lax.all_to_all(expert_result, "ep", split_axis=0, concat_axis=0, tiled=True).reshape(
        experts * capacity, model_width
    )
    picked = returned[slot_of_choice].reshape(token_rows, top_count, model_width)
    mixture = jnp.sum(gate_values[:, :, None] * picked.astype(jnp.float32), axis=1)
    layer_out = (middle + shared_result + mixture).astype(jnp.bfloat16)
    grad_output = out_grad.astype(jnp.float32)
    shared_hidden_grad = times_transposed(out_grad, shared_down_full)
    shared_pre_grad = (shared_hidden_grad * shared_lin * silu_slope(shared_pre)).astype(
        jnp.bfloat16
    )
    shared_lin_grad = (shared_hidden_grad * silu_value(shared_pre)).astype(jnp.bfloat16)
    choice_grad = (
        (gate_values[:, :, None] * grad_output[:, None, :])
        .astype(jnp.bfloat16)
        .reshape(choice_count, model_width)
    )
    padded_grads = jnp.concatenate([choice_grad, jnp.zeros((1, model_width), jnp.bfloat16)], axis=0)
    grads_outgoing = padded_grads[slot_source].reshape(
        group_size, local_experts, capacity, model_width
    )
    grads_received = lax.all_to_all(grads_outgoing, "ep", split_axis=0, concat_axis=0, tiled=True)
    expert_hidden_grad = jnp.einsum(
        "sjcd,jfd->sjcf", grads_received, expert_down, preferred_element_type=jnp.float32
    )
    gate_pre_grad = (expert_hidden_grad * up_pre * silu_slope(gate_pre)).astype(jnp.bfloat16)
    up_pre_grad = (expert_hidden_grad * silu_value(gate_pre)).astype(jnp.bfloat16)
    row_grads = (
        jnp.einsum("sjcf,jdf->sjcd", gate_pre_grad, expert_gate, preferred_element_type=jnp.float32)
        + jnp.einsum("sjcf,jdf->sjcd", up_pre_grad, expert_up, preferred_element_type=jnp.float32)
    ).astype(jnp.bfloat16)
    expert_gate_term = jnp.einsum(
        "sjcd,sjcf->jdf", received, gate_pre_grad, preferred_element_type=jnp.float32
    )
    expert_up_term = jnp.einsum(
        "sjcd,sjcf->jdf", received, up_pre_grad, preferred_element_type=jnp.float32
    )
    expert_down_term = jnp.einsum(
        "sjcf,sjcd->jfd", expert_hidden, grads_received, preferred_element_type=jnp.float32
    )
    rows_back = lax.all_to_all(row_grads, "ep", split_axis=0, concat_axis=0, tiled=True).reshape(
        experts * capacity, model_width
    )
    gate_grad = jnp.sum(grad_output[:, None, :] * picked.astype(jnp.float32), axis=2)
    prob_grad = jnp.sum(gate_grad[:, :, None] * route_table, axis=1)
    logit_grad = (
        router_probs * (prob_grad - jnp.sum(router_probs * prob_grad, axis=1, keepdims=True))
    ).astype(jnp.bfloat16)
    second_grad = (
        times_transposed(shared_pre_grad, shared_gate_full)
        + times_transposed(shared_lin_grad, shared_up_full)
        + times_transposed(logit_grad, router_matrix)
    )
    second_grad = second_grad + jnp.sum(
        rows_back[slot_of_choice].reshape(token_rows, top_count, model_width).astype(jnp.float32),
        axis=1,
    )
    router_term = transposed_times(hidden_second, logit_grad)
    shared_gate_term = transposed_times(hidden_second, shared_pre_grad)
    shared_up_term = transposed_times(hidden_second, shared_lin_grad)
    shared_down_term = transposed_times(shared_hidden, out_grad)
    gain_second_term = jnp.sum(second_grad * normed_second, axis=0)
    middle_grad = grad_output + norm_back(second_grad * gain_second, normed_second, scale_second)
    attn_grad = middle_grad.astype(jnp.bfloat16)
    output_term = transposed_times(attended_low, attn_grad)
    attended_grad = times_transposed(attn_grad, output_matrix).astype(jnp.bfloat16)
    grad_heads = attended_grad.reshape(token_rows, head_count, head_dim)
    row_delta = jnp.einsum("qhd,hqd->hq", grad_heads.astype(jnp.float32), attended)
    key_whole, value_whole, segment_whole = (
        lax.all_gather(keys_flat, "ep", axis=0, tiled=True),
        lax.all_gather(values_flat, "ep", axis=0, tiled=True),
        lax.all_gather(own_segment, "ep", axis=0, tiled=True),
    )

    def key_back(query_acc, block_index):
        offset = block_index * step_rows
        key_block = lax.dynamic_slice_in_dim(key_whole, offset, step_rows, 0).reshape(
            step_rows, head_count, head_dim
        )
        value_block = lax.dynamic_slice_in_dim(value_whole, offset, step_rows, 0).reshape(
            step_rows, head_count, head_dim
        )
        segment_block = lax.dynamic_slice_in_dim(segment_whole, offset, step_rows, 0)
        key_places = offset + jnp.arange(step_rows, dtype=jnp.int32)
        allowed = allowed_pairs(own_segment, places, segment_block, key_places)
        scores = (
            jnp.einsum("qhd,khd->hqk", queries, key_block, preferred_element_type=jnp.float32)
            * score_scale
        )
        probs_exact = jnp.where(allowed, jnp.exp(scores - log_total[:, :, None]), 0.0)
        prob_grads = jnp.einsum(
            "qhd,khd->hqk", grad_heads, value_block, preferred_element_type=jnp.float32
        )
        score_grads = (probs_exact * (prob_grads - row_delta[:, :, None])).astype(jnp.bfloat16)
        query_acc = query_acc + jnp.einsum(
            "hqk,khd->qhd", score_grads, key_block, preferred_element_type=jnp.float32
        )
        key_part = jnp.einsum(
            "hqk,qhd->khd", score_grads, queries, preferred_element_type=jnp.float32
        ).reshape(step_rows, model_width)
        value_part = jnp.einsum(
            "hqk,qhd->khd",
            probs_exact.astype(jnp.bfloat16),
            grad_heads,
            preferred_element_type=jnp.float32,
        ).reshape(step_rows, model_width)
        return (query_acc, jnp.concatenate([key_part, value_part], axis=1))

    query_acc, key_terms = lax.scan(
        key_back,
        jnp.zeros((token_rows, head_count, head_dim), jnp.float32),
        jnp.arange(whole_rows // step_rows, dtype=jnp.int32),
    )
    key_value_sum = lax.psum_scatter(
        key_terms.reshape(whole_rows, 2 * model_width).astype(jnp.bfloat16),
        "ep",
        scatter_dimension=0,
        tiled=True,
    ).astype(jnp.float32)
    query_sum = query_acc.reshape(token_rows, model_width)
    key_sum = key_value_sum[:, :model_width]
    value_sum = key_value_sum[:, model_width:]
    query_grad = (
        rotate(
            (query_sum * score_scale).reshape(token_rows, head_count, head_dim),
            cosine_table,
            -sine_table,
        )
        .astype(jnp.bfloat16)
        .reshape(token_rows, model_width)
    )
    key_grad = (
        rotate(
            (key_sum * score_scale).reshape(token_rows, head_count, head_dim),
            cosine_table,
            -sine_table,
        )
        .astype(jnp.bfloat16)
        .reshape(token_rows, model_width)
    )
    value_grad = value_sum.astype(jnp.bfloat16)
    first_grad = (
        times_transposed(query_grad, query_matrix)
        + times_transposed(key_grad, key_matrix)
        + times_transposed(value_grad, value_matrix)
    )
    query_term = transposed_times(hidden_first, query_grad)
    key_term = transposed_times(hidden_first, key_grad)
    value_term = transposed_times(hidden_first, value_grad)
    gain_first_term = jnp.sum(first_grad * normed_first, axis=0)
    tokens_grad = middle_grad + norm_back(first_grad * gain_first, normed_first, scale_first)
    dense_grads = (
        lax.psum_scatter(gain_first_term, ("rep", "ep"), scatter_dimension=0, tiled=True),
        lax.psum_scatter(query_term, ("rep", "ep"), scatter_dimension=0, tiled=True),
        lax.psum_scatter(key_term, ("rep", "ep"), scatter_dimension=0, tiled=True),
        lax.psum_scatter(value_term, ("rep", "ep"), scatter_dimension=0, tiled=True),
        lax.psum_scatter(output_term, ("rep", "ep"), scatter_dimension=0, tiled=True),
        lax.psum_scatter(gain_second_term, ("rep", "ep"), scatter_dimension=0, tiled=True),
        lax.psum_scatter(router_term, ("rep", "ep"), scatter_dimension=0, tiled=True),
        lax.psum_scatter(shared_gate_term, ("rep", "ep"), scatter_dimension=0, tiled=True),
        lax.psum_scatter(shared_up_term, ("rep", "ep"), scatter_dimension=0, tiled=True),
        lax.psum_scatter(shared_down_term, ("rep", "ep"), scatter_dimension=0, tiled=True),
    )
    expert_grads = (
        lax.psum_scatter(
            expert_gate_term.astype(jnp.bfloat16), "rep", scatter_dimension=2, tiled=True
        ).astype(jnp.float32),
        lax.psum_scatter(
            expert_up_term.astype(jnp.bfloat16), "rep", scatter_dimension=2, tiled=True
        ).astype(jnp.float32),
        lax.psum_scatter(
            expert_down_term.astype(jnp.bfloat16), "rep", scatter_dimension=2, tiled=True
        ).astype(jnp.float32),
    )
    return (
        layer_out,
        tokens_grad,
        dense_grads[0],
        dense_grads[1],
        dense_grads[2],
        dense_grads[3],
        dense_grads[4],
        dense_grads[5],
        dense_grads[6],
        dense_grads[7],
        dense_grads[8],
        dense_grads[9],
        expert_grads[0],
        expert_grads[1],
        expert_grads[2],
    )


def solution(mesh):
    return jax.shard_map(
        shards,
        mesh=mesh,
        in_specs=(
            P(("rep", "ep"), None),
            P("rep", "ep"),
            P(("rep", "ep"), None),
            P(("rep", "ep")),
            P(("rep", "ep"), None),
            P(("rep", "ep"), None),
            P(("rep", "ep"), None),
            P(("rep", "ep"), None),
            P(("rep", "ep")),
            P(("rep", "ep"), None),
            P(("rep", "ep"), None),
            P(("rep", "ep"), None),
            P(("rep", "ep"), None),
            P("ep", None, None),
            P("ep", None, None),
            P("ep", None, None),
            P(("rep", "ep"), None),
        ),
        out_specs=(
            P(("rep", "ep"), None),
            P(("rep", "ep"), None),
            P(("rep", "ep")),
            P(("rep", "ep"), None),
            P(("rep", "ep"), None),
            P(("rep", "ep"), None),
            P(("rep", "ep"), None),
            P(("rep", "ep")),
            P(("rep", "ep"), None),
            P(("rep", "ep"), None),
            P(("rep", "ep"), None),
            P(("rep", "ep"), None),
            P("ep", None, "rep"),
            P("ep", None, "rep"),
            P("ep", None, "rep"),
        ),
        check_vma=False,
    )
```

profile of v0, /device:TPU:9, one launch (start us, length us, event | category | flops | bytes accessed | tf_op | source)
XLA Modules:
  0.0 1669.5 jit_solution(3728425969518155587)
XLA Ops:
  11.2 40.1 %all-reduce.8 = (bf16[768]{0:T(1024)(128)(2,1)S(1)}, bf16[768]{0:T(1024)(128)(2,1)}) all-reduce(bf16[768]{0:T(1024)(128)(2,1)S(1)} %dynamic-update-slice, bf16[768]{0:T(1024)(128)(2,1)S(1)} %dynamic-update-slice.1), channel_id=1, replica_groups=mesh['rep'=4,'ep'=8] {'rep','ep'}, use_global_device_ids=true, to_apply=%add.2 | all-reduce | flops 1536 | bytes 6144
  52.5 13.4 all-gather.18.cloned.1.call-done
  69.5 52.6 %all-gather.16.cloned.1.call-done = bf16[768,768]{1,0:T(8,128)(2,1)} async-done(((bf16[24,768]{1,0:T(8,128)(2,1)}), bf16[768,768]{1,0:T(8,128)(2,1)}) %all-gather.16.cloned.1.call-update) | async-done | bytes 1179664 | tf_op jit(solution)/shard_map/all_gather | solution.py:107
  124.9 53.4 %all-gather.12.cloned.1.call-done = bf16[768,768]{1,0:T(8,128)(2,1)} async-done(((bf16[24,768]{1,0:T(8,128)(2,1)}), bf16[768,768]{1,0:T(8,128)(2,1)}) %all-gather.12.cloned.1.call-update) | async-done | bytes 1179664 | tf_op jit(solution)/shard_map/all_gather | solution.py:108
  206.7 40.1 %all-gather.1 = bf16[32,24,8]{1,2,0:T(8,128)(2,1)S(1)} all-gather(bf16[1,24,8]{1,2,0:T(8,128)(2,1)S(1)} %bitcast.382), channel_id=1, replica_groups=mesh['rep'=4,'ep'=8] {'rep','ep'}, dimensions={0}, use_global_device_ids=true | all-gather | bytes 12672 | tf_op jit(solution)/shard_map/all_gather | solution.py:112
  259.0 83.7 %while.38 = (s32[]{:T(128)}, f32[12,256]{1,0:T(8,128)S(1)}, f32[12,256]{1,0:T(8,128)}, f32[12,256,64]{1,2,0:T(8,128)}, s32[1,256]{1,0:T(1,128)}, /*index=5*/s32[...) while((s32[]{:T(128)}, f32[12,256]{1,0:T(8,128)S(1)}, ...), condition=%wide.region_4.5_spmd.clone.clone.clone, body=%wide.region_1.4_spmd.clone.clone.clone.sunk | while | flops 424111616 | bytes 52608892 | solution.py:198
  374.8 31.0 %all-to-all-done.2 = bf16[8,1,128,768]{3,2,1,0:T(8,128)(2,1)} async-done(((bf16[8,1,128,768]{3,2,1,0:T(8,128)(2,1)}), bf16[8,1,128,768]{3,2,1,0:T(8,128)(2,1)}, u32[]{:S(2)}, u32[]{:S(2)}) %all-to-all-start.2) | async-done | bytes 1572896 | tf_op jit(solution)/shard_map/all_to_all | solution.py:270
  423.8 36.0 %all-to-all-done = bf16[8,1,128,768]{3,2,1,0:T(8,128)(2,1)} async-done(((bf16[8,1,128,768]{3,2,1,0:T(8,128)(2,1)}), bf16[8,1,128,768]{3,2,1,0:T(8,128)(2,1)}, u32[]{:S(2)}, u32[]{:S(2)}) %all-to-all-start) | async-done | bytes 1572896 | tf_op jit(solution)/shard_map/all_to_all | solution.py:240
  465.6 12.8 fusion.54
  503.8 34.2 %all-to-all-done.1 = bf16[8,1,128,768]{3,2,1,0:T(8,128)(2,1)} async-done(((bf16[8,1,128,768]{3,2,1,0:T(8,128)(2,1)}), bf16[8,1,128,768]{3,2,1,0:T(8,128)(2,1)}, u32[]{:S(2)}, u32[]{:S(2)}) %all-to-all-start.1) | async-done | bytes 1572896 | tf_op jit(solution)/shard_map/all_to_all | solution.py:249
  597.9 77.5 %while.39 = (s32[]{:T(128)}, f32[256,12,64]{0,2,1:T(8,128)}, bf16[4,512,1536]{2,1,0:T(8,128)(2,1)}, s32[4]{0:T(128)S(1)}, bf16[2048,768]{0,1:T(8,128)(2,1)}, /*i...) while((s32[]{:T(128)}, f32[256,12,64]{0,2,1:T(8,128)}, ...), condition=%wide.region_20.21_spmd.clone.clone.clone, body=%wide.region_19.20_spmd.clone.clone.clone.sunk | while | flops 1026306560 | bytes 81072312 | solution.py:357
  681.7 11.6 copy.164
  733.8 11.0 reduce-scatter.15.cloned.1.call-done
  758.7 33.0 %reduce-scatter.35.cloned.1.call-done = bf16[192,2048]{1,0:T(8,128)(2,1)} async-done(((bf16[768,2048]{1,0:T(8,128)(2,1)}), bf16[192,2048]{1,0:T(8,128)(2,1)}) %reduce-scatter.35.cloned.1.call-update) | async-done | bytes 786448
  797.2 41.3 %reduce-scatter.31.cloned.1.call-done = bf16[1,768,512]{2,1,0:T(8,128)(2,1)} async-done(((bf16[1,768,2048]{2,1,0:T(8,128)(2,1)}), bf16[1,768,512]{2,1,0:T(8,128)(2,1)}) %reduce-scatter.31.cloned.1.call-update) | async-done | bytes 786448 | tf_op jit(solution)/shard_map/reduce_scatter | solution.py:413
  841.0 44.5 %reduce-scatter.33.cloned.1.call-done = bf16[1,768,512]{2,1,0:T(8,128)(2,1)} async-done(((bf16[1,768,2048]{2,1,0:T(8,128)(2,1)}), bf16[1,768,512]{2,1,0:T(8,128)(2,1)}) %reduce-scatter.33.cloned.1.call-update) | async-done | bytes 786448 | tf_op jit(solution)/shard_map/reduce_scatter | solution.py:416
  892.6 39.5 %all-reduce.7 = (f32[768]{0:T(1024)}, f32[768]{0:T(1024)}, f32[768,8]{0,1:T(8,128)}) all-reduce(f32[768]{0:T(1024)S(1)} %get-tuple-element.848, f32[768]{0:T(1024)S(1)} %copy-done.66, f32[768,8]{0,1:T(8,128)} %fusion.150), channel_id=4, replica_groups=mesh['rep'=4,'ep'=8] {'rep','ep'}, use_global_device_ids=true, to_apply=%region_24.25.clone | all-reduce | flops 7680 | bytes 61440
  939.2 65.2 %reduce-scatter.25.cloned.1.call-done = f32[24,2048]{1,0:T(8,128)} async-done(((f32[768,2048]{1,0:T(8,128)}), f32[24,2048]{1,0:T(8,128)}) %reduce-scatter.25.cloned.1.call-update) | async-done | bytes 196624 | tf_op jit(solution)/shard_map/reduce_scatter | solution.py:408
  1004.4 120.9 %reduce-scatter.27.cloned.1.call-done = f32[24,2048]{1,0:T(8,128)} async-done(((f32[768,2048]{1,0:T(8,128)}), f32[24,2048]{1,0:T(8,128)}) %reduce-scatter.27.cloned.1.call-update) | async-done | bytes 196624 | tf_op jit(solution)/shard_map/reduce_scatter | solution.py:409
  1125.3 119.8 %reduce-scatter.29.cloned.1.call-done = f32[64,768]{1,0:T(8,128)} async-done(((f32[2048,768]{1,0:T(8,128)}), f32[64,768]{1,0:T(8,128)}) %reduce-scatter.29.cloned.1.call-update) | async-done | bytes 196624 | tf_op jit(solution)/shard_map/reduce_scatter | solution.py:410
  1245.1 104.7 %reduce-scatter.23.cloned.1.call-done = f32[24,768]{1,0:T(8,128)} async-done(((f32[768,768]{1,0:T(8,128)}), f32[24,768]{1,0:T(8,128)}) %reduce-scatter.23.cloned.1.call-update) | async-done | bytes 73744 | tf_op jit(solution)/shard_map/reduce_scatter | solution.py:405
  1349.8 103.8 %reduce-scatter.17.cloned.1.call-done = f32[24,768]{1,0:T(8,128)} async-done(((f32[768,768]{1,0:T(8,128)}), f32[24,768]{1,0:T(8,128)}) %reduce-scatter.17.cloned.1.call-update) | async-done | bytes 73744 | tf_op jit(solution)/shard_map/reduce_scatter | solution.py:402
  1453.6 104.8 %reduce-scatter.19.cloned.1.call-done = f32[24,768]{1,0:T(8,128)} async-done(((f32[768,768]{1,0:T(8,128)}), f32[24,768]{1,0:T(8,128)}) %reduce-scatter.19.cloned.1.call-update) | async-done | bytes 73744 | tf_op jit(solution)/shard_map/reduce_scatter | solution.py:403
  1558.4 103.8 %reduce-scatter.21.cloned.1.call-done = f32[24,768]{1,0:T(8,128)} async-done(((f32[768,768]{1,0:T(8,128)}), f32[24,768]{1,0:T(8,128)}) %reduce-scatter.21.cloned.1.call-update) | async-done | bytes 73744 | tf_op jit(solution)/shard_map/reduce_scatter | solution.py:404
  (560 shorter events, 429.8 us)
Async XLA Ops:
  7.2 58.7 %all-gather.18.cloned.1.call-start = ((), (), s32[]{:S(2)}) async-start(), calls=%async_computation.18 | async-start | bytes 1216512 | tf_op jit(solution)/shard_map/all_gather | solution.py:109
  7.9 114.1 %all-gather.16.cloned.1.call-start = ((), (), s32[]{:S(2)}) async-start(), calls=%async_computation.17 | async-start | bytes 1216512 | tf_op jit(solution)/shard_map/all_gather | solution.py:107
  8.7 169.6 %all-gather.12.cloned.1.call-start = ((), (), s32[]{:S(2)}) async-start(), calls=%async_computation.15 | async-start | bytes 1216512 | tf_op jit(solution)/shard_map/all_gather | solution.py:108
  9.4 244.3 %all-gather.20.cloned.1.call-start = ((), (), s32[]{:S(2)}) async-start(), calls=%async_computation.19 | async-start | bytes 3538944 | tf_op jit(solution)/shard_map/all_gather | solution.py:182
  68.6 189.9 %all-gather.14.cloned.1.call-start = ((), (), s32[]{:S(2)}) async-start(), calls=%async_computation.16 | async-start | bytes 3538944 | tf_op jit(solution)/shard_map/all_gather | solution.py:181
  183.1 161.7 %all-gather.22.cloned.1.call-start = ((), (), s32[]{:S(2)}) async-start(), calls=%async_computation.20 | async-start | bytes 1216512 | tf_op jit(solution)/shard_map/all_gather | solution.py:110
  183.7 362.3 %all-gather.24.cloned.1.call-start = ((), (), s32[]{:S(2)}) async-start(), calls=%async_computation.21 | async-start | bytes 3244032 | tf_op jit(solution)/shard_map/all_gather | solution.py:113
  184.5 365.7 %all-gather.26.cloned.1.call-start = ((), (), s32[]{:S(2)}) async-start(), calls=%async_computation.22 | async-start | bytes 3244032 | tf_op jit(solution)/shard_map/all_gather | solution.py:114
  363.2 42.6 %all-to-all-start.2 = ((bf16[8,1,128,768]{3,2,1,0:T(8,128)(2,1)}), bf16[8,1,128,768]{3,2,1,0:T(8,128)(2,1)}, u32[]{:S(2)}, u32[]{:S(2)}) async-start(bf16[8,1,128,768]{3,2,1,0:T(8,128)(2,1)} %bitcast.364), calls=%async_computation.2 | async-start | bytes 3145728 | tf_op jit(solution)/shard_map/all_to_all | solution.py:270
  405.8 54.0 %all-to-all-start = ((bf16[8,1,128,768]{3,2,1,0:T(8,128)(2,1)}), bf16[8,1,128,768]{3,2,1,0:T(8,128)(2,1)}, u32[]{:S(2)}, u32[]{:S(2)}) async-start(bf16[8,1,128,768]{3,2,1,0:T(8,128)(2,1)} %bitcast.363), calls=%async_computation | async-start | bytes 3145728 | tf_op jit(solution)/shard_map/all_to_all | solution.py:240
  414.0 140.5 %all-gather.28.cloned.1.call-start = ((), (), s32[]{:S(2)}) async-start(), calls=%async_computation.23 | async-start | bytes 3244032 | tf_op jit(solution)/shard_map/all_gather | solution.py:115
  485.2 52.8 %all-to-all-start.1 = ((bf16[8,1,128,768]{3,2,1,0:T(8,128)(2,1)}), bf16[8,1,128,768]{3,2,1,0:T(8,128)(2,1)}, u32[]{:S(2)}, u32[]{:S(2)}) async-start(bf16[8,1,128,768]{3,2,1,0:T(8,128)(2,1)} %fusion.89), calls=%async_computation.1 | async-start | bytes 3145728 | tf_op jit(solution)/shard_map/all_to_all | solution.py:249
  538.0 41.5 %all-to-all-start.3 = ((bf16[8,1,128,768]{3,2,1,0:T(8,128)(2,1)}), bf16[8,1,128,768]{3,2,1,0:T(8,128)(2,1)S(1)}, u32[]{:S(2)}, u32[]{:S(2)}) async-start(bf16[8,1,128,768]{3,2,1,0:T(8,128)(2,1)} %fusion.92), calls=%async_computation.3 | async-start | bytes 3145728 | tf_op jit(solution)/shard_map/all_to_all | solution.py:289
  545.2 199.6 %reduce-scatter.15.cloned.1.call-start = ((), (), s32[]{:S(2)}) async-start(), calls=%async_computation.24 | async-start | bytes 7077888 | tf_op jit(solution)/shard_map/reduce_scatter | solution.py:362
  675.4 116.2 %reduce-scatter.35.cloned.1.call-start = ((), (), s32[]{:S(2)}) async-start(), calls=%async_computation.34 | async-start | bytes 3932160
  699.7 138.7 %reduce-scatter.31.cloned.1.call-start = ((), (), s32[]{:S(2)}) async-start(), calls=%async_computation.32 | async-start | bytes 3932160 | tf_op jit(solution)/shard_map/reduce_scatter | solution.py:413
  707.7 177.8 %reduce-scatter.33.cloned.1.call-start = ((), (), s32[]{:S(2)}) async-start(), calls=%async_computation.33 | async-start | bytes 3932160 | tf_op jit(solution)/shard_map/reduce_scatter | solution.py:416
  715.6 288.8 %reduce-scatter.25.cloned.1.call-start = ((), (), s32[]{:S(2)}) async-start(), calls=%async_computation.29 | async-start | bytes 6488064 | tf_op jit(solution)/shard_map/reduce_scatter | solution.py:408
  720.6 404.7 %reduce-scatter.27.cloned.1.call-start = ((), (), s32[]{:S(2)}) async-start(), calls=%async_computation.30 | async-start | bytes 6488064 | tf_op jit(solution)/shard_map/reduce_scatter | solution.py:409
  725.5 519.5 %reduce-scatter.29.cloned.1.call-start = ((), (), s32[]{:S(2)}) async-start(), calls=%async_computation.31 | async-start | bytes 6488064 | tf_op jit(solution)/shard_map/reduce_scatter | solution.py:410
  730.6 619.3 %reduce-scatter.23.cloned.1.call-start = ((), (), s32[]{:S(2)}) async-start(), calls=%async_computation.28 | async-start | bytes 2433024 | tf_op jit(solution)/shard_map/reduce_scatter | solution.py:405
  733.7 719.9 %reduce-scatter.17.cloned.1.call-start = ((), (), s32[]{:S(2)}) async-start(), calls=%async_computation.25 | async-start | bytes 2433024 | tf_op jit(solution)/shard_map/reduce_scatter | solution.py:402
  748.6 809.8 %reduce-scatter.19.cloned.1.call-start = ((), (), s32[]{:S(2)}) async-start(), calls=%async_computation.26 | async-start | bytes 2433024 | tf_op jit(solution)/shard_map/reduce_scatter | solution.py:403
  750.7 911.5 %reduce-scatter.21.cloned.1.call-start = ((), (), s32[]{:S(2)}) async-start(), calls=%async_computation.27 | async-start | bytes 2433024 | tf_op jit(solution)/shard_map/reduce_scatter | solution.py:404
  (134 other events, 2610.5 us)
Sparse Core Ops, SparseCore 0:
  11.1 54.7 all-gather.17
  68.9 53.1 all-gather.15
  125.1 53.1 all-gather.11
  180.3 37.3 all-gather.19
  219.7 38.7 all-gather.13
  261.4 52.0 all-gather.21
  316.5 58.8 all-gather.23
  378.4 82.3 all-gather.25
  463.8 74.0 all-gather.27
  675.6 69.2 reduce-scatter.14
  747.8 43.8 reduce-scatter.34
  794.5 43.9 reduce-scatter.30
  841.5 43.9 reduce-scatter.32
  891.5 112.8 reduce-scatter.24
  1011.4 113.8 reduce-scatter.26
  1131.3 113.7 reduce-scatter.28
  1251.6 98.1 reduce-scatter.22
  1355.5 98.0 reduce-scatter.16
  1460.3 98.0 reduce-scatter.18
  1564.1 98.0 reduce-scatter.20
where the time goes:
time: 1680 us; the launch traced here: 1670 us
  waiting for transfers between devices  1080 us (64%)
  matrix products  209 us (12%)
  blocking collectives  130 us (8%)
  local copies, waits for them, and re-layouts  126 us (8%)
  other arithmetic  67.8 us (4%)
  starting transfers between devices  30.4 us (2%)
    reduce_scatter x1, waiting for transfers between devices, shards(): lax.psum_scatter(shared_up_term, ('rep', 'ep'), scatter_dimension=0, tile...  121 us
    reduce_scatter x1, waiting for transfers between devices, shards(): lax.psum_scatter(shared_down_term, ('rep', 'ep'), scatter_dimension=0, ti...  120 us
    reduce_scatter x1, waiting for transfers between devices, shards(): lax.psum_scatter(key_term, ('rep', 'ep'), scatter_dimension=0, tiled=True)  105 us
    reduce_scatter x1, waiting for transfers between devices, shards(): lax.psum_scatter(output_term, ('rep', 'ep'), scatter_dimension=0, tiled=T...  105 us
    reduce_scatter x1, waiting for transfers between devices, shards(): lax.psum_scatter(query_term, ('rep', 'ep'), scatter_dimension=0, tiled=True)  104 us
    reduce_scatter x1, waiting for transfers between devices, shards(): lax.psum_scatter(value_term, ('rep', 'ep'), scatter_dimension=0, tiled=True)  104 us
    unnamed x2, blocking collectives  79.6 us
    reduce_scatter x1, waiting for transfers between devices, shards(): lax.psum_scatter(shared_gate_term, ('rep', 'ep'), scatter_dimension=0, ti...  65.2 us
  transfers between devices with their start and end apart: 24, of which 18 were waited for; matrix products, arithmetic and copies ran while one was open for 18% of the time, Pallas kernels for 0%

commit v1 on v0

v1 whole, which is shorter than its diff:
```python
import functools
import math

import jax
import jax.numpy as jnp
from jax import lax
from jax.experimental import pallas as pl
from jax.experimental.pallas import tpu as pltpu
from jax.sharding import PartitionSpec as P

HEADS = 12
EPSILON = 1e-06
NEG_LARGE = -1e30
BF = jnp.bfloat16
F32 = jnp.float32
VMEM_LIMIT = 58 * 1024 * 1024


def nn(a, b):
    return lax.dot_general(a, b, (((1,), (0,)), ((), ())), preferred_element_type=F32)


def nt(a, b):
    return lax.dot_general(a, b, (((1,), (1,)), ((), ())), preferred_element_type=F32)


def tn(a, b):
    return lax.dot_general(a, b, (((0,), (0,)), ((), ())), preferred_element_type=F32)


def rms_scale(values):
    return lax.rsqrt(jnp.mean(values * values, axis=1, keepdims=True) + EPSILON)


def lanes(shape):
    return lax.broadcasted_iota(jnp.int32, shape, len(shape) - 1)


def turned(x):
    front = lanes(x.shape) % 64 < 32
    return jnp.where(front, -pltpu.roll(x, 96, 1), pltpu.roll(x, 32, 1))


def vmem(n):
    return [pl.BlockSpec(memory_space=pltpu.VMEM)] * n


def params(**kw):
    return pltpu.CompilerParams(vmem_limit_bytes=VMEM_LIMIT, **kw)


def whole(shape):
    return pl.BlockSpec(shape, lambda *_: (0,) * len(shape))


def qkv_kernel(chips, rows, c_ref, *refs):
    own, par = refs[:chips], refs[chips : 2 * chips]
    wq, wk, wv, cos, sin, gain, h1, keys, vals, quer = refs[2 * chips :]
    c = c_ref[0]
    pairs = keys.shape[0]
    scale = 0.125
    for s in range(chips):
        for p, src in ((0, own[s]), (1, par[s])):
            core = c if p == 0 else 1 - c
            slot = 2 * (chips - 1 - s) + core
            x = src[0:rows, :].astype(F32)
            h = (x * rms_scale(x) * gain[...]).astype(BF)
            h1[slot] = h
            co, si = cos[slot], sin[slot]
            k = nn(h, wk[...])
            v = nn(h, wv[...])
            for i in range(pairs):
                kp = k[:, 128 * i : 128 * i + 128]
                keys[i, slot] = (kp * co + turned(kp) * si).astype(BF)
                vals[i, slot] = v[:, 128 * i : 128 * i + 128].astype(BF)
            if s == 0:
                q = nn(h, wq[...])
                for i in range(pairs):
                    qp = q[:, 128 * i : 128 * i + 128]
                    quer[i, core] = ((qp * co + turned(qp) * si) * scale).astype(BF)


def attend_kernel(first, count, rows, q_ref, k_ref, v_ref, sq_ref, sk_ref, o_ref, ol_ref, lse_ref, s_scr):
    low = lanes((rows, 128)) < 64
    for qi in range(2):
        qpair = q_ref[0, qi * rows : (qi + 1) * rows, :]
        sq = sq_ref[qi * rows : (qi + 1) * rows, 0:1]
        outs, lses = [], []
        for hh in range(2):
            keep = low if hh == 0 else jnp.logical_not(low)
            q = jnp.where(keep, qpair, jnp.zeros_like(qpair))
            m = jnp.full((rows, 128), NEG_LARGE, F32)
            for j in range(count):
                at = (first + qi + j) * rows
                s = nt(q, k_ref[0, at : at + rows, :])
                s = jnp.where(sq == sk_ref[0:1, at : at + rows], s, NEG_LARGE)
                s_scr[:, j * rows : (j + 1) * rows] = s
                for g in range(rows // 128):
                    m = jnp.maximum(m, s[:, g * 128 : (g + 1) * 128])
            m = jnp.max(m, axis=1, keepdims=True)
            total = jnp.zeros((rows, 128), F32)
            acc = jnp.zeros((rows, 128), F32)
            for j in range(count):
                at = (first + qi + j) * rows
                e = jnp.exp(s_scr[:, j * rows : (j + 1) * rows] - m)
                for g in range(rows // 128):
                    total = total + e[:, g * 128 : (g + 1) * 128]
                acc = acc + nn(e.astype(BF), v_ref[0, at : at + rows, :])
            total = jnp.sum(total, axis=1, keepdims=True)
            outs.append(acc / total)
            lses.append(m + jnp.log(total))
        o = jnp.where(low, outs[0], outs[1])
        o_ref[0, qi * rows : (qi + 1) * rows, :] = o
        ol_ref[0, qi * rows : (qi + 1) * rows, :] = o.astype(BF)
        both = jnp.where(lanes((rows, 128)) == 0, lses[0], lses[1])
        lse_ref[0, :, qi * rows : (qi + 1) * rows] = both.T[0:8, :]


def mid_kernel(a_ref, w_ref, x_ref, g_ref, mid_ref, h_ref):
    mid = x_ref[...].astype(F32) + nn(a_ref[...], w_ref[...])
    mid_ref[...] = mid
    h_ref[...] = (mid * rms_scale(mid) * g_ref[...]).astype(BF)


def pre_kernel(nblk, rows, *refs):
    og = refs[:nblk]
    p_ref, wd, wsd, dehid, ogx_t, dsh, ogx = refs[nblk:]
    cap = p_ref.shape[1]

    @pl.when(pl.program_id(0) == 0)
    def _():
        for b in range(nblk):
            block = og[b][0:rows, :]
            ogx[b * cap : (b + 1) * cap, :] = nn(p_ref[b], block).astype(BF)
            dsh[b * rows : (b + 1) * rows, :] = nt(block, wsd[...]).astype(BF)
        ogx_t[...] = ogx[...].T

    dehid[...] = nt(ogx[...], wd[...]).astype(BF)


def act(g, u, dh):
    s = jax.nn.sigmoid(g)
    silu = g * s
    hid = (silu * u).astype(BF)
    dg = (dh * u * (s * (1.0 + g * (1.0 - s)))).astype(BF)
    du = (dh * silu).astype(BF)
    return hid, dg, du


def split_nn(a, col):
    wide = jnp.broadcast_to(col, (col.shape[0], 128))
    high = wide.astype(BF)
    return nn(a, high) + nn(a, (wide - high.astype(F32)).astype(BF))


def expert_kernel(nblk, rows, experts, e_ref, *refs):
    g_refs = refs[:nblk]
    (p_ref, pt_ref, wr, wr_t, wsg, wsu, dsh, wg, wu, dehid) = refs[nblk : nblk + 10]
    (x_out, ehid, degate, deup, gate_slot, gate_tok, shid, dsg, dsu, tg, rgrad) = refs[nblk + 10 : nblk + 21]
    x_scr, row_scr, tg_scr, pg_scr, prob_scr, gs_scr = refs[nblk + 21 :]
    cap = p_ref.shape[1]
    step = pl.program_id(0)
    own = lanes((rows, 128)) == e_ref[0]

    @pl.when(step == 0)
    def _():
        row_scr[...] = jnp.zeros_like(row_scr)
        pg_scr[...] = jnp.zeros_like(pg_scr)
        for b in range(nblk):
            block = g_refs[b][...]
            x = nn(p_ref[b], block).astype(BF)
            x_scr[b * cap : (b + 1) * cap, :] = x
            x_out[b * cap : (b + 1) * cap, :] = x
            logits = jnp.where(lanes((rows, 128)) < experts, nn(block, wr[...]), NEG_LARGE)
            shifted = jnp.exp(logits - jnp.max(logits, axis=1, keepdims=True))
            probs = shifted / jnp.sum(shifted, axis=1, keepdims=True)
            prob_scr[b] = probs
            gate = jnp.sum(jnp.where(own, probs, 0.0), axis=1, keepdims=True)
            gate_tok[b] = jnp.broadcast_to(gate, (rows, 128))
            slot = split_nn(p_ref[b], gate)
            gs_scr[b * cap : (b + 1) * cap, :] = slot
            gate_slot[b * cap : (b + 1) * cap, :] = slot
            at = b * rows
            hid, dg, du = act(nn(block, wsg[...]), nn(block, wsu[...]), dsh[at : at + rows, :].astype(F32))
            shid[at : at + rows, :] = hid
            dsg[at : at + rows, :] = dg
            dsu[at : at + rows, :] = du
            tg_scr[at : at + rows, :] = nt(dg, wsg[...]) + nt(du, wsu[...])

    raw = dehid[...].astype(F32)
    hid, dg, du = act(nn(x_scr[...], wg[0]), nn(x_scr[...], wu[0]), raw * gs_scr[:, 0:1])
    ehid[...] = hid
    degate[...] = dg
    deup[...] = du
    row_scr[...] += nt(dg, wg[0]) + nt(du, wu[0])
    pg_scr[...] += jnp.sum(hid.astype(F32) * raw, axis=1, keepdims=True)

    @pl.when(step == pl.num_programs(0) - 1)
    def _():
        total = jnp.zeros_like(rgrad)
        for b in range(nblk):
            at = b * rows
            pg = split_nn(pt_ref[b], pg_scr[b * cap : (b + 1) * cap, 0:1])
            probs = prob_scr[b]
            gate = jnp.sum(jnp.where(own, probs, 0.0), axis=1, keepdims=True)
            lgrad = (pg * probs * (own.astype(F32) - gate)).astype(BF)
            total += tn(lgrad, g_refs[b][...])
            back = nn(pt_ref[b], row_scr[b * cap : (b + 1) * cap, :].astype(BF))
            tg[b] = (tg_scr[at : at + rows, :] + back + nn(lgrad, wr_t[...])).astype(BF)
        rgrad[...] = total


def wgrad_kernel(x_ref, ogx_t, gate_slot, ehid, degate, deup, gu, dn, x_t):
    @pl.when(pl.program_id(0) == 0)
    def _():
        x_t[...] = x_ref[...].T

    gu[0, 0] = nn(x_t[...], degate[...]).astype(BF)
    gu[0, 1] = nn(x_t[...], deup[...]).astype(BF)
    dn[...] = nn(ogx_t[...], (ehid[...].astype(F32) * gate_slot[:, 0:1]).astype(BF)).astype(BF)


def result_kernel(nblk, rows, *refs):
    g_refs, og = refs[:nblk], refs[nblk : 2 * nblk]
    (pt_ref, gate_tok, shid, dsg, dsu, wsd, ehid, wd) = refs[2 * nblk : 2 * nblk + 8]
    mix, sgu, sd, acc = refs[2 * nblk + 8 :]
    cap = pt_ref.shape[2]
    step = pl.program_id(0)

    @pl.when(step == 0)
    def _():
        acc[...] = jnp.zeros_like(acc)
        dg_sum = jnp.zeros((sgu.shape[0], dsg.shape[1]), F32)
        du_sum = jnp.zeros_like(dg_sum)
        sd_sum = jnp.zeros(sd.shape, F32)
        for b in range(nblk):
            at = b * rows
            g_t = g_refs[b][...].T
            dg_sum += nn(g_t, dsg[at : at + rows, :])
            du_sum += nn(g_t, dsu[at : at + rows, :])
            sd_sum += tn(shid[at : at + rows, :], og[b][0:rows, :])
        width = dsg.shape[1]
        sgu[:, :width] = dg_sum.astype(BF)
        sgu[:, width:] = du_sum.astype(BF)
        sd[...] = sd_sum.astype(BF)

    acc[...] += nn(ehid[...], wd[0])

    @pl.when(step == pl.num_programs(0) - 1)
    def _():
        for b in range(nblk):
            at = b * rows
            res = acc[b * cap : (b + 1) * cap, :].astype(BF)
            picked = nn(pt_ref[b], res) * gate_tok[b][:, 0:1]
            mix[b] = (picked + nn(shid[at : at + rows, :], wsd[...])).astype(BF)


def mid_back_kernel(count, *refs):
    pieces = refs[:count]
    mid_ref, g_ref, og_ref, w_ref, mg_ref, ag_ref, da_ref, gg_ref = refs[count:]
    two = pieces[0][...].astype(F32)
    for piece in pieces[1:]:
        two += piece[...].astype(F32)
    mid = mid_ref[...]
    scale = rms_scale(mid)
    mn = mid * scale
    gg_ref[...] = jnp.broadcast_to(jnp.sum(two * mn, axis=0, keepdims=True), gg_ref.shape)
    dn = two * g_ref[...]
    mg = og_ref[...].astype(F32) + scale * (dn - mn * jnp.mean(dn * mn, axis=1, keepdims=True))
    mg_ref[...] = mg
    ag = mg.astype(BF)
    ag_ref[...] = ag
    da = nt(ag, w_ref[...]).astype(BF)
    for i in range(da_ref.shape[0]):
        da_ref[i] = da[:, 128 * i : 128 * i + 128]


def attend_back_kernel(first, count, rows, q_ref, k_ref, v_ref, o_ref, do_ref, lse_ref, sq_ref, sk_ref, cos, sin,
                       h1_ref, wq, wk, wv, gain, grads, og1, gg, h1_t, k_t, dk, dv, og_scr):
    step = pl.program_id(0)
    low = lanes((rows, 128)) < 64
    kv_rows = k_ref.shape[1]
    base = kv_rows - 2 * rows

    @pl.when(step == 0)
    def _():
        h1_t[...] = h1_ref[...].T
        og_scr[...] = jnp.zeros_like(og_scr)

    k_t[...] = k_ref[0].T
    dk[...] = jnp.zeros_like(dk)
    dv[...] = jnp.zeros_like(dv)
    dqs = []
    for qi in range(2):
        at_q = qi * rows
        qpair = q_ref[0, at_q : at_q + rows, :]
        dopair = do_ref[0, at_q : at_q + rows, :]
        prod = dopair.astype(F32) * o_ref[0, at_q : at_q + rows, :]
        d0 = jnp.sum(jnp.where(low, prod, 0.0), axis=1, keepdims=True)
        d1 = jnp.sum(jnp.where(low, 0.0, prod), axis=1, keepdims=True)
        delta = jnp.where(lanes((rows, 128)) == 0, d0, d1).T
        sq = sq_ref[0:1, at_q : at_q + rows]
        halves = []
        for hh in range(2):
            keep = low if hh == 0 else jnp.logical_not(low)
            q = jnp.where(keep, qpair, jnp.zeros_like(qpair))
            do = jnp.where(keep, dopair, jnp.zeros_like(dopair))
            lse_row = lse_ref[0, hh : hh + 1, at_q : at_q + rows]
            delta_row = delta[hh : hh + 1, :]
            dq = jnp.zeros((64, rows), F32)
            for j in range(count):
                at = (first + qi + j) * rows
                same = sk_ref[at : at + rows, 0:1] == sq
                s = nt(k_ref[0, at : at + rows, :], q)
                p = jnp.where(same, jnp.exp(s - lse_row), 0.0)
                dp = nt(v_ref[0, at : at + rows, :], do)
                ds = (p * (dp - delta_row)).astype(BF)
                dv[at : at + rows, :] += nn(p.astype(BF), do)
                dk[at : at + rows, :] += nn(ds, q)
                dq += nn(k_t[64 * hh : 64 * hh + 64, at : at + rows], ds)
            halves.append(dq)
        dq = jnp.concatenate(halves, axis=0).T * 0.125
        at = base + at_q
        dq = dq * cos[at : at + rows, :] - turned(dq) * sin[at : at + rows, :]
        dqs.append(dq.astype(BF))
    dq = jnp.concatenate(dqs, axis=0)
    dkv = dk[...]
    dkb = (dkv * cos[...] - turned(dkv) * sin[...]).astype(BF)
    dvb = dv[...].astype(BF)
    grads[0] = nn(h1_t[:, base:], dq).astype(BF)
    grads[1] = nn(h1_t[...], dkb).astype(BF)
    grads[2] = nn(h1_t[...], dvb).astype(BF)
    og_scr[...] += nt(dkb, wk[...]) + nt(dvb, wv[...])
    og_scr[base:, :] += nt(dq, wq[...])

    @pl.when(step == pl.num_programs(0) - 1)
    def _():
        one = og_scr[...]
        og1[...] = one.astype(BF)
        total = jnp.sum(one * h1_ref[...].astype(F32), axis=0, keepdims=True) / gain[...]
        gg[...] = jnp.broadcast_to(total, gg.shape)


def last_kernel(count, *refs):
    pieces = refs[:count]
    x_ref, g_ref, mg_ref, out = refs[count:]
    one = pieces[0][...].astype(F32)
    for piece in pieces[1:]:
        one += piece[...].astype(F32)
    x = x_ref[...].astype(F32)
    scale = rms_scale(x)
    xn = x * scale
    dn = one * g_ref[...]
    out[...] = mg_ref[...] + scale * (dn - xn * jnp.mean(dn * xn, axis=1, keepdims=True))


def shape(dims, dtype=BF):
    return jax.ShapeDtypeStruct(dims, dtype)


def shards(
    R,
    E,
    tokens,
    segment_ids,
    routes,
    norm1_gain,
    w_query,
    w_key,
    w_value,
    w_out,
    norm2_gain,
    w_router,
    shared_gate,
    shared_up,
    shared_down,
    expert_gate,
    expert_up,
    expert_down,
    out_grad,
):
    Z = E // 2
    T, D = tokens.shape
    FF = shared_gate.shape[1]
    topk = routes.shape[1]
    experts = w_router.shape[1]
    assert expert_gate.shape[0] == 1 and experts == E
    half = D // 2
    pairs = half // 128
    wrow = w_query.shape[0]
    hrow = 2 * wrow
    cap = 2 * T * topk // experts
    slots = E * cap
    fs = FF // E
    drow = shared_down.shape[0]
    longest = E * T // 2
    back = -(-(longest - 1) // T)
    nb = -(-back // 2)
    chips = nb + 1
    kvb = 2 * chips
    first = 2 * nb - back
    count = back + 1
    r = lax.axis_index("rep")
    e = lax.axis_index("ep")
    z, c = e // 2, e % 2
    is0 = c == 0
    c_arr = jnp.reshape(c, (1,)).astype(jnp.int32)
    e_arr = jnp.reshape(e, (1,)).astype(jnp.int32)

    def swap(x):
        return lax.ppermute(x, "ep", [(i, i ^ 1) for i in range(E)])

    def ring(x, s):
        return lax.ppermute(x, "ep", [(i, (i + 2 * s) % E) for i in range(E)])

    def line(x, s):
        return lax.ppermute(x, "ep", [(i, i + 2 * s) for i in range(E) if 0 <= i + 2 * s < E])

    def cross(x, s):
        return lax.ppermute(x, "rep", [(i, i ^ s) for i in range(R)])

    def ordered(mine, other):
        return jnp.where(is0, mine, other), jnp.where(is0, other, mine)

    def put(buf, x, i):
        return lax.dynamic_update_index_in_dim(buf, x, i, 0)

    def chip_pack(mats, extra):
        stacked = jnp.stack(mats).reshape(len(mats) * wrow, D)
        mine, other = ordered(stacked[:, :half], stacked[:, half:])
        ext = jnp.pad(extra.reshape(1, -1), ((0, 0), (0, half - extra.size)))
        got = swap(jnp.concatenate([other, ext], axis=0))
        a, b = ordered(mine, got[:-1])
        ea, eb = ordered(ext, got[-1:])
        rows = jnp.stack([a.reshape(-1, wrow, half), b.reshape(-1, wrow, half)], axis=1).reshape(-1, half)
        rows = jnp.concatenate([rows, ea, eb], axis=0)
        return jnp.pad(rows, ((0, -rows.shape[0] % 16), (0, 0)))

    def gather_z(pack):
        buf = put(jnp.zeros((Z,) + pack.shape, BF), pack, z)
        for s in range(1, Z):
            buf = put(buf, ring(pack, s), (z - s) % Z)
        return buf

    def gather_rep(part):
        buf = put(jnp.zeros((R,) + part.shape, BF), part, r)
        for s in range(1, R):
            buf = put(buf, cross(part, s), r ^ s)
        return buf

    def unpack(full, i):
        return full[:, :, i * hrow : (i + 1) * hrow, :].reshape(D, half)

    pack1 = chip_pack([w_query, w_key, w_value], norm1_gain)
    full1 = gather_rep(gather_z(pack1))
    wq, wk, wv = (unpack(full1, i) for i in range(3))
    gain1 = full1[:, :, 3 * hrow : 3 * hrow + 2, :wrow].reshape(1, D).astype(F32)

    seg_row = jnp.pad(segment_ids.reshape(1, T).astype(BF), ((0, 7), (0, D - T)))
    tok_pack = jnp.concatenate([tokens, seg_row], axis=0)
    own_tok = [tok_pack] + [line(tok_pack, s) for s in range(1, chips)]
    par_tok = [swap(x) for x in own_tok]

    seg_blocks = [None] * kvb
    for s in range(chips):
        valid = z - s >= 0
        a, b = ordered(own_tok[s][T, :T], par_tok[s][T, :T])
        seg_blocks[2 * (nb - s)] = jnp.where(valid, a.astype(F32), -1.0)
        seg_blocks[2 * (nb - s) + 1] = jnp.where(valid, b.astype(F32), -1.0)
    segs = jnp.stack(seg_blocks)
    kv_rows = kvb * T
    seg_flat = segs.reshape(1, kv_rows)
    seg_wide = jnp.broadcast_to(segs.reshape(kv_rows, 1), (kv_rows, 128))

    inverse = jnp.exp(jnp.arange(32).astype(F32) * (-2.0 * math.log(10000.0) / 64))
    inverse = jnp.tile(inverse, 4)
    places = (z - nb) * (2 * T) + jnp.arange(kv_rows, dtype=jnp.int32)
    angle = places.astype(F32)[:, None] * inverse[None, :]
    cos, sin = jnp.cos(angle), jnp.sin(angle)

    h1, keys, vals, quer = pl.pallas_call(
        functools.partial(qkv_kernel, chips, T),
        in_specs=[pl.BlockSpec(memory_space=pltpu.SMEM)] + vmem(2 * chips + 6),
        out_specs=tuple(vmem(4)),
        out_shape=(
            shape((kvb, T, D)),
            shape((pairs, kvb, T, 128)),
            shape((pairs, kvb, T, 128)),
            shape((pairs, 2, T, 128)),
        ),
        compiler_params=params(),
        name="qkv",
    )(c_arr, *own_tok, *par_tok, wq, wk, wv, cos.reshape(kvb, T, 128), sin.reshape(kvb, T, 128), gain1)
    h1 = h1.reshape(kv_rows, D)
    keys = keys.reshape(pairs, kv_rows, 128)
    vals = vals.reshape(pairs, kv_rows, 128)
    quer = quer.reshape(pairs, 2 * T, 128)

    tok_done = own_tok[-1]
    og_pack = jnp.concatenate(
        [out_grad, jnp.pad(routes.reshape(1, topk * T).astype(BF), ((0, 7), (0, D - topk * T)))], axis=0
    )
    og_pack, full1_dep, tok_done = lax.optimization_barrier((og_pack, full1[0, 0, 0], tok_done))

    def gather_ep(x):
        lane = [x] + [ring(x, s) for s in range(1, Z)]
        blocks = []
        for item in lane:
            blocks += [item, swap(item)]
        return blocks

    pack2 = chip_pack([w_out], jnp.concatenate([norm2_gain, w_router.reshape(-1)]))
    full2 = gather_rep(gather_z(pack2))
    wo_half = unpack(full2, 0)
    wo = jnp.concatenate(ordered(wo_half, swap(wo_half)), axis=1)
    ext2 = full2[:, :, hrow : hrow + 2, :].reshape(R * E, half)
    gain2 = ext2[:, :wrow].reshape(1, D).astype(F32)
    router = ext2[:, wrow : wrow + wrow * experts].reshape(D, experts)
    router = jnp.pad(router, ((0, 0), (0, 128 - experts)))
    router_t = router.T

    def by_unit(w):
        return w.reshape(wrow, R, E, drow).transpose(2, 0, 1, 3).reshape(E, wrow, fs)

    gu = jnp.concatenate([by_unit(shared_gate), by_unit(shared_up)], axis=2)
    gu = lax.all_to_all(gu, "ep", split_axis=0, concat_axis=0, tiled=True).reshape(E * wrow, 2 * fs)
    gu = gather_rep(gu).reshape(D, 2 * fs)
    wsg, wsu = gu[:, :fs], gu[:, fs:]
    wsd = gather_rep(shared_down).reshape(fs, D)

    og_blocks = gather_ep(og_pack)
    table = jnp.stack([x[T, : topk * T] for x in og_blocks]).reshape(E, T, topk)
    hit = jnp.any(table == e.astype(F32).astype(BF), axis=2).astype(F32)
    rank = jnp.cumsum(hit, axis=1) - hit
    rank = jnp.where(hit > 0, rank, -1.0)
    slot_ids = jnp.arange(cap).astype(F32)
    pick = (rank[:, None, :] == slot_ids[None, :, None]).astype(BF)
    pick_t = (rank[:, :, None] == slot_ids[None, None, :]).astype(BF)

    one = lambda *dims: pl.BlockSpec((1,) + dims, lambda i: (i, 0, 0))
    att, att_low, lse = pl.pallas_call(
        functools.partial(attend_kernel, first, count, T),
        grid=(pairs,),
        in_specs=[
            one(2 * T, 128),
            one(kv_rows, 128),
            one(kv_rows, 128),
            whole((2 * T, 128)),
            whole((1, kv_rows)),
        ],
        out_specs=(one(2 * T, 128), one(2 * T, 128), one(8, 2 * T)),
        out_shape=(
            shape((pairs, 2 * T, 128), F32),
            shape((pairs, 2 * T, 128)),
            shape((pairs, 8, 2 * T), F32),
        ),
        scratch_shapes=[pltpu.VMEM((T, count * T), F32)],
        compiler_params=params(),
        name="attend",
    )(quer, keys, vals, seg_wide[-2 * T :], seg_flat)

    def joined(mine, other):
        both = jnp.where(is0, jnp.concatenate([mine, other]), jnp.concatenate([other, mine]))
        return both.transpose(1, 0, 2).reshape(T, D)

    att_own, att_other = ordered(att_low[:, :T], att_low[:, T:])
    attended = joined(att_own, swap(att_other))
    mid, h2 = pl.pallas_call(
        mid_kernel,
        in_specs=vmem(4),
        out_specs=tuple(vmem(2)),
        out_shape=(shape((T, D), F32), shape((T, D))),
        compiler_params=params(),
        name="mid",
    )(attended, wo, tokens, gain2)

    ft = min(256, FF // R)
    steps = FF // ft
    per = FF // R // ft
    col = lambda n: pl.BlockSpec((n, ft), lambda i: (0, i))
    wcol = pl.BlockSpec((1, D, ft), lambda i: (0, 0, i))
    wdn = pl.BlockSpec((1, ft, D), lambda i: (0, i, 0))
    dehid, ogx_t, dsh = pl.pallas_call(
        functools.partial(pre_kernel, E, T),
        grid=(steps,),
        in_specs=[whole((T + 8, D))] * E
        + [whole((E, cap, T)), pl.BlockSpec((ft, D), lambda i: (i, 0)), whole((fs, D))],
        out_specs=(col(slots), whole((D, slots)), whole((E * T, fs))),
        out_shape=(shape((slots, FF)), shape((D, slots)), shape((E * T, fs))),
        scratch_shapes=[pltpu.VMEM((slots, D), BF)],
        compiler_params=params(),
        name="pre",
    )(*og_blocks, pick, expert_down.reshape(FF, D), wsd)

    h2_blocks = gather_ep(h2)
    (x_rows, ehid, degate, deup, gate_slot, gate_tok, shid, dsg, dsu, tg, rgrad) = pl.pallas_call(
        functools.partial(expert_kernel, E, T, experts),
        grid=(steps,),
        in_specs=[pl.BlockSpec(memory_space=pltpu.SMEM)]
        + [whole((T, D))] * E
        + [
            whole((E, cap, T)),
            whole((E, T, cap)),
            whole((D, 128)),
            whole((128, D)),
            whole((D, fs)),
            whole((D, fs)),
            whole((E * T, fs)),
            wcol,
            wcol,
            col(slots),
        ],
        out_specs=(
            whole((slots, D)),
            col(slots),
            col(slots),
            col(slots),
            whole((slots, 128)),
            whole((E, T, 128)),
            whole((E * T, fs)),
            whole((E * T, fs)),
            whole((E * T, fs)),
            whole((E, T, D)),
            whole((128, D)),
        ),
        out_shape=(
            shape((slots, D)),
            shape((slots, FF)),
            shape((slots, FF)),
            shape((slots, FF)),
            shape((slots, 128), F32),
            shape((E, T, 128), F32),
            shape((E * T, fs)),
            shape((E * T, fs)),
            shape((E * T, fs)),
            shape((E, T, D)),
            shape((128, D), F32),
        ),
        scratch_shapes=[
            pltpu.VMEM((slots, D), BF),
            pltpu.VMEM((slots, D), F32),
            pltpu.VMEM((E * T, D), F32),
            pltpu.VMEM((slots, 128), F32),
            pltpu.VMEM((E, T, 128), F32),
            pltpu.VMEM((slots, 128), F32),
        ],
        compiler_params=params(),
        name="expert",
    )(e_arr, *h2_blocks, pick, pick_t, router, router_t, wsg, wsu, dsh, expert_gate, expert_up, dehid)

    def scatter_ep(blocks):
        lane = [blocks[2 * s] + swap(blocks[2 * s + 1]) for s in range(Z)]
        return [lane[0]] + [ring(lane[s], -s) for s in range(1, Z)]

    two_parts = scatter_ep(tg)

    gu_grad, dn_grad = pl.pallas_call(
        wgrad_kernel,
        grid=(steps,),
        in_specs=[whole((slots, D)), whole((D, slots)), whole((slots, 128)), col(slots), col(slots), col(slots)],
        out_specs=(
            pl.BlockSpec((1, 2, D, ft), lambda i: (i // per, 0, 0, i % per)),
            col(D),
        ),
        out_shape=(shape((R, 2, D, FF // R)), shape((D, FF))),
        scratch_shapes=[pltpu.VMEM((D, slots), BF)],
        compiler_params=params(),
        name="wgrad",
    )(x_rows, ogx_t, gate_slot, ehid, degate, deup)
    gu_sum = lax.psum_scatter(gu_grad.reshape(-1, FF // R), "rep", scatter_dimension=0, tiled=True)
    gu_sum = gu_sum.reshape(1, 2, D, FF // R)
    dn_sum = lax.psum_scatter(dn_grad, "rep", scatter_dimension=0, tiled=True)

    mix, sgu_grad, sd_grad = pl.pallas_call(
        functools.partial(result_kernel, E, T),
        grid=(steps,),
        in_specs=[whole((T, D))] * E
        + [whole((T + 8, D))] * E
        + [
            whole((E, T, cap)),
            whole((E, T, 128)),
            whole((E * T, fs)),
            whole((E * T, fs)),
            whole((E * T, fs)),
            whole((fs, D)),
            col(slots),
            wdn,
        ],
        out_specs=(whole((E, T, D)), whole((D, 2 * fs)), whole((fs, D))),
        out_shape=(shape((E, T, D)), shape((D, 2 * fs)), shape((fs, D))),
        scratch_shapes=[pltpu.VMEM((slots, D), F32)],
        compiler_params=params(),
        name="result",
    )(*h2_blocks, *og_blocks, pick_t, gate_tok, shid, dsg, dsu, wsd, ehid, expert_down)

    mid_grad, attn_grad, att_grad, gain2_part = pl.pallas_call(
        functools.partial(mid_back_kernel, Z),
        in_specs=vmem(Z + 4),
        out_specs=tuple(vmem(4)),
        out_shape=(shape((T, D), F32), shape((T, D)), shape((2 * pairs, T, 128)), shape((8, D), F32)),
        compiler_params=params(),
        name="mid_back",
    )(*two_parts, mid, gain2, out_grad, wo)

    ag_own, ag_other = ordered(att_grad[:pairs], att_grad[pairs:])
    do_a, do_b = ordered(ag_own, swap(ag_other))
    do = jnp.concatenate([do_a, do_b], axis=1)

    grads, og1, gain1_part = pl.pallas_call(
        functools.partial(attend_back_kernel, first, count, T),
        grid=(pairs,),
        in_specs=[
            one(2 * T, 128),
            one(kv_rows, 128),
            one(kv_rows, 128),
            one(2 * T, 128),
            one(2 * T, 128),
            one(8, 2 * T),
            whole((1, 2 * T)),
            whole((kv_rows, 128)),
            whole((kv_rows, 128)),
            whole((kv_rows, 128)),
            whole((kv_rows, D)),
            pl.BlockSpec((D, 128), lambda i: (0, i)),
            pl.BlockSpec((D, 128), lambda i: (0, i)),
            pl.BlockSpec((D, 128), lambda i: (0, i)),
            whole((1, D)),
        ],
        out_specs=(
            pl.BlockSpec((3, D, 128), lambda i: (0, 0, i)),
            whole((kv_rows, D)),
            whole((8, D)),
        ),
        out_shape=(shape((3, D, half)), shape((kv_rows, D)), shape((8, D), F32)),
        scratch_shapes=[
            pltpu.VMEM((D, kv_rows), BF),
            pltpu.VMEM((128, kv_rows), BF),
            pltpu.VMEM((kv_rows, 128), F32),
            pltpu.VMEM((kv_rows, 128), F32),
            pltpu.VMEM((kv_rows, D), F32),
        ],
        compiler_params=params(),
        name="attend_back",
    )(quer, keys, vals, att, do, lse, seg_flat[:, -2 * T :], seg_wide, cos, sin, h1, wq, wk, wv, gain1)

    og1 = og1.reshape(chips, 2, T, D)
    mine, other = ordered(og1[:, 0], og1[:, 1])
    lane = mine + swap(other)
    one_parts = [lane[nb]] + [line(lane[nb - s], -s) for s in range(1, chips)]
    tokens_grad = pl.pallas_call(
        functools.partial(last_kernel, chips),
        in_specs=vmem(chips + 3),
        out_specs=vmem(1)[0],
        out_shape=shape((T, D), F32),
        compiler_params=params(),
        name="last",
    )(*one_parts, tokens, gain1, mid_grad)

    mix_parts = scatter_ep(mix)
    layer_out = mid
    for part in mix_parts:
        layer_out = layer_out + part.astype(F32)
    layer_out = layer_out.astype(BF)

    def reduce_rep(x):
        total = lax.dynamic_index_in_dim(x, r, 0, keepdims=False).astype(F32)
        for s in range(1, R):
            total += cross(lax.dynamic_index_in_dim(x, r ^ s, 0, keepdims=False), s).astype(F32)
        return total

    def reduce_z(x):
        total = lax.dynamic_index_in_dim(x, z, 0, keepdims=False).astype(F32)
        for s in range(1, Z):
            total += ring(lax.dynamic_index_in_dim(x, (z + s) % Z, 0, keepdims=False), s).astype(F32)
        return total

    wo_part = tn(attended, attn_grad).astype(BF)
    wo_mine, wo_other = ordered(wo_part[:, :half], wo_part[:, half:])
    wo_lane = wo_mine + swap(wo_other)
    n_chip = R * Z
    ext = jnp.concatenate(
        [
            gain1_part[0].reshape(n_chip, hrow),
            gain2_part[0].reshape(n_chip, hrow),
            rgrad[:experts].reshape(experts, n_chip, hrow).transpose(1, 0, 2).reshape(n_chip, experts * hrow),
        ],
        axis=1,
    ).astype(BF)
    ext = jnp.pad(ext, ((0, 0), (0, -ext.shape[1] % half))).reshape(n_chip, -1, half)
    dense = jnp.concatenate([grads, wo_lane[None]]).reshape(4, n_chip, hrow, half).transpose(1, 0, 2, 3)
    dense = jnp.concatenate([dense.reshape(n_chip, 4 * hrow, half), ext], axis=1)
    dense = reduce_rep(dense.reshape((R, Z) + dense.shape[1:])).astype(BF)
    dense = reduce_z(dense)
    mats = dense[: 4 * hrow].reshape(4, 2, wrow, half)
    mats_mine, mats_other = ordered(mats[:, 0], mats[:, 1])
    ext = dense[4 * hrow :]
    got = swap(jnp.concatenate([mats_other.reshape(4 * wrow, half), ext], axis=0).astype(BF)).astype(F32)
    left, right = ordered(mats_mine, got[: 4 * wrow].reshape(4, wrow, half))
    mats = jnp.concatenate([left, right], axis=2)
    ext = (ext + got[4 * wrow :]).reshape(-1)[: (2 + experts) * hrow].reshape(2 + experts, 2, wrow)
    ext = jnp.where(is0, ext[:, 0], ext[:, 1])

    sgu = reduce_rep(sgu_grad.reshape(R, D // R, 2 * fs)).astype(BF)
    sd_sum = reduce_rep(sd_grad.reshape(R, drow, D))
    sgu = lax.all_to_all(sgu.reshape(E, wrow, 2 * fs), "ep", split_axis=0, concat_axis=0, tiled=True)

    def units_back(x):
        return x.astype(F32).reshape(E, wrow, R, drow).transpose(1, 2, 0, 3).reshape(wrow, FF)

    return (
        layer_out,
        tokens_grad,
        ext[0],
        mats[0],
        mats[1],
        mats[2],
        mats[3],
        ext[1],
        ext[2:].T,
        units_back(sgu[:, :, :fs]),
        units_back(sgu[:, :, fs:]),
        sd_sum,
        gu_sum[0, 0][None].astype(F32),
        gu_sum[0, 1][None].astype(F32),
        dn_sum.T[None].astype(F32),
    )


def solution(mesh):
    rows = P(("rep", "ep"), None)
    flat = P(("rep", "ep"))
    expert = P("ep", None, None)
    expert_out = P("ep", None, "rep")
    return jax.shard_map(
        functools.partial(shards, mesh.shape["rep"], mesh.shape["ep"]),
        mesh=mesh,
        in_specs=(rows, P("rep", "ep"), rows, flat, rows, rows, rows, rows, flat)
        + (rows,) * 4
        + (expert,) * 3
        + (rows,),
        out_specs=(rows, rows, flat, rows, rows, rows, rows, flat)
        + (rows,) * 4
        + (expert_out,) * 3,
        check_vma=False,
    )
```

time: 1680 us -> 531 us (0.32)
  the two profiles are of different devices: /device:TPU:9 before, /device:TPU:0 now
where the time goes in v1:
time: 531 us; the launch traced here: 524 us
  waiting for transfers between devices  147 us (28%)
  Pallas kernels  145 us (27%)
  starting transfers between devices  120 us (23%)
  other arithmetic  47 us (9%)
  local copies, waits for them, and re-layouts  46.8 us (9%)
  between operations  15.6 us (3%)
    ppermute x21, waiting for transfers between devices, ring(): return lax.ppermute(x, 'ep', [(i, (i + 2 * s) % E) for i in range(E)])  66.2 us
    ppermute x21, starting transfers between devices, ring(): return lax.ppermute(x, 'ep', [(i, (i + 2 * s) % E) for i in range(E)])  65.4 us
    ppermute x21, waiting for transfers between devices, cross(): return lax.ppermute(x, 'rep', [(i, i ^ s) for i in range(R)])  55.3 us
    pallas_call x1, Pallas kernels, shards(): pl.pallas_call(functools.partial(expert_kernel, E, T, experts), grid=(ste...  38.3 us
    pallas_call x1, Pallas kernels, shards(): pl.pallas_call(functools.partial(attend_back_kernel, first, count, T), gr...  31.5 us
    ppermute x21, starting transfers between devices, cross(): return lax.ppermute(x, 'rep', [(i, i ^ s) for i in range(R)])  27.8 us
    ppermute x4, waiting for transfers between devices, line(): lax.ppermute(x, 'ep', [(i, i + 2 * s) for i in range(E) if 0 <= i + 2 * s...  23.9 us
    pallas_call x1, Pallas kernels, shards(): pl.pallas_call(functools.partial(result_kernel, E, T), grid=(steps,), in_...  18.7 us
  transfers between devices with their start and end apart: 77, of which 24 were waited for; matrix products, arithmetic and copies ran while one was open for 16% of the time, Pallas kernels for 17%

profile of v1, /device:TPU:0, one launch (start us, length us, event | category | flops | bytes accessed | tf_op | source)
XLA Modules:
  0.0 523.6 jit_solution(10840687813601655418)
XLA Ops:
  9.8 5.7 %collective-permute-start = (bf16[264,768]{1,0:T(8,128)(2,1)}, bf16[264,768]{1,0:T(8,128)(2,1)}, u32[]{:S(2)}, u32[]{:S(2)}) collective-permute-start(bf16[264,768]{1,0:T(8,128)(2,1)} %fusion.15.refs_0_), channel_id=1, source_target_pairs={{0,2},{1,3},{2,4},{3,5},{4,6},{5,7},{8,10},{9,11},{10,12},{11,13},... | collective-permute-start | bytes 1216520 | tf_op jit(solution)/shard_map/ppermute | solution.py:417
  42.8 7.0 %collective-permute-start.15 = (bf16[64,384]{1,0:T(8,128)(2,1)S(1)}, bf16[64,384]{1,0:T(8,128)(2,1)S(1)}, u32[]{:S(2)}, u32[]{:S(2)}) collective-permute-start(bf16[64,384]{1,0:T(8,128)(2,1)S(1)} %fusion.41), channel_id=1, source_target_pairs={{0,4},{1,5},{2,6},{3,7},{4,0},{5,1},{6,2},{7,3},{8,12},{9,13},{10,... | collective-permute-start | bytes 147464 | tf_op jit(solution)/shard_map/ppermute | solution.py:414
  82.8 5.7 %collective-permute-done.19 = bf16[4,64,384]{2,1,0:T(8,128)(2,1)S(1)} collective-permute-done((bf16[4,64,384]{2,1,0:T(8,128)(2,1)S(1)}, bf16[4,64,384]{2,1,0:T(8,128)(2,1)S(1)}, u32[]{:S(2)}, u32[]{:S(2)}) %collective-permute-start.19) | collective-permute-done | bytes 196640 | tf_op jit(solution)/shard_map/ppermute | solution.py:420
  95.8 5.2 %collective-permute-done.35 = bf16[192,512]{1,0:T(8,128)(2,1)S(1)} collective-permute-done((bf16[192,512]{1,0:T(8,128)(2,1)S(1)}, bf16[192,512]{1,0:T(8,128)(2,1)S(1)}, u32[]{:S(2)}, u32[]{:S(2)}) %collective-permute-start.35) | collective-permute-done | bytes 196640 | tf_op jit(solution)/shard_map/ppermute | solution.py:420
  102.6 10.6 %collective-permute-done.36 = bf16[192,512]{1,0:T(8,128)(2,1)S(1)} collective-permute-done((bf16[192,512]{1,0:T(8,128)(2,1)S(1)}, bf16[192,512]{1,0:T(8,128)(2,1)S(1)}, u32[]{:S(2)}, u32[]{:S(2)}) %collective-permute-start.36) | collective-permute-done | bytes 196640 | tf_op jit(solution)/shard_map/ppermute | solution.py:420
  114.8 4.9 collective-permute-done.37
  132.7 8.0 %qkv.1 = (bf16[6,256,768]{2,1,0:T(8,128)(2,1)}, bf16[3,6,256,128]{3,2,1,0:T(8,128)(2,1)}, bf16[3,6,256,128]{3,2,1,0:T(8,128)(2,1)}, bf16[3,2,256,128]{3,2,1,0:T(8,128)(2,1)}) custom-call(s32[1]{0:T(128)} %bitcast.c_ref, bf16[264,768]{1,0:T(8,128)(2,1)} %fusion.15.refs_0_, bf16[264,768]{1,0:T(8,128)(2,1)} %collective-permute-done.refs_1_, ...), custom_call_target="tpu_custom_call" | custom-call | tf_op jit(solution)/shard_map/qkv/pallas_call | solution.py:481
  141.5 10.2 %attend.1 = (f32[3,512,128]{2,1,0:T(8,128)}, bf16[3,512,128]{2,1,0:T(8,128)(2,1)}, f32[3,8,512]{2,1,0:T(8,128)}) custom-call(bf16[3,512,128]{2,1,0:T(8,128)(2,1)} %bitcast.280, bf16[3,1536,128]{2,1,0:T(8,128)(2,1)} %bitcast.265, bf16[3,1536,128]{2,1,0:T(8,128)(2,1)} %bitcast.267, f32[512,128]{1,0:T(8,128)} %broadcast_in_dim.136.sq_ref, f32[1,1536]{1,0:T(1,128)} %bitcast.311), custom_call_target="tpu_custom_call" | custom-call | tf_op jit(solution)/shard_map/attend/pallas_call | solution.py:541
  161.8 8.1 %collective-permute-start.22 = (bf16[256,768]{1,0:T(8,128)(2,1)}, bf16[256,768]{1,0:T(8,128)(2,1)S(1)}, u32[]{:S(2)}, u32[]{:S(2)}) collective-permute-start(bf16[256,768]{1,0:T(8,128)(2,1)} %get-tuple-element.56.refs_0_), channel_id=1, source_target_pairs={{0,2},{1,3},{2,4},{3,5},{4,6},{5,7},{6,0},{7,1},{8,10},{9,11},{10,... | collective-permute-start | bytes 1179656 | tf_op jit(solution)/shard_map/ppermute | solution.py:414
  174.4 6.1 %collective-permute-done.22.refs_2_ = bf16[256,768]{1,0:T(8,128)(2,1)S(1)} collective-permute-done((bf16[256,768]{1,0:T(8,128)(2,1)}, bf16[256,768]{1,0:T(8,128)(2,1)S(1)}, u32[]{:S(2)}, u32[]{:S(2)}) %collective-permute-start.22) | collective-permute-done | bytes 393248 | tf_op jit(solution)/shard_map/ppermute | solution.py:414
  180.5 16.4 %collective-permute-done.24.refs_4_ = bf16[256,768]{1,0:T(8,128)(2,1)} collective-permute-done((bf16[256,768]{1,0:T(8,128)(2,1)}, bf16[256,768]{1,0:T(8,128)(2,1)}, u32[]{:S(2)}, u32[]{:S(2)}) %collective-permute-start.24) | collective-permute-done | bytes 393248 | tf_op jit(solution)/shard_map/ppermute | solution.py:414
  198.3 11.7 %pre.1 = (bf16[1024,2048]{1,0:T(8,128)(2,1)}, bf16[768,1024]{1,0:T(8,128)(2,1)}, bf16[2048,256]{1,0:T(8,128)(2,1)}) custom-call(bf16[264,768]{1,0:T(8,128)(2,1)} %copy-done.1, bf16[264,768]{1,0:T(8,128)(2,1)} %collective-permute-done.28.refs_1_.refs_9_, bf16[264,768]{1,0:T(8,128)(2,1)} %collective-permute-done.29.refs_2_.refs_10_, ...), custom_call_target="tpu_custom_call" | custom-call | tf_op jit(solution)/shard_map/pre/pallas_call | solution.py:583
  212.4 38.3 %expert.1 = (bf16[1024,768]{1,0:T(8,128)(2,1)}, bf16[1024,2048]{1,0:T(8,128)(2,1)}, bf16[1024,2048]{1,0:T(8,128)(2,1)}, bf16[1024,2048]{1,0:T(8,128)(2,1)}, f32[...) custom-call(s32[1]{0:T(128)} %bitcast.39.e_ref, ...), custom_call_target="tpu_custom_call" | custom-call | tf_op jit(solution)/shard_map/expert/pallas_call | solution.py:596
  250.7 17.0 %wgrad.1 = (bf16[4,2,768,512]{3,2,1,0:T(8,128)(2,1)}, bf16[768,2048]{1,0:T(8,128)(2,1)}) custom-call(bf16[1024,768]{1,0:T(8,128)(2,1)} %get-tuple-element.80.x_ref, bf16[768,1024]{1,0:T(8,128)(2,1)} %get-tuple-element.81.ogx_t, f32[1024,128]{1,0:T(8,128)} %get-tuple-element.82.gate_slot, bf16[1024,2048]{1,0:T(8,128)(2,1)} %get-tuple-element.64.refs_22_.ehid, ...), custom_call_target="tpu_custom_call" | custom-call | tf_op jit(solution)/shard_map/wgrad/pallas_call | solution.py:657
  280.7 18.7 %result.1 = (bf16[8,256,768]{2,1,0:T(8,128)(2,1)}, bf16[768,512]{1,0:T(8,128)(2,1)}, bf16[256,768]{1,0:T(8,128)(2,1)}) custom-call(bf16[256,768]{1,0:T(8,128)(2,1)} %get-tuple-element.56.refs_0_, bf16[256,768]{1,0:T(8,128)(2,1)} %copy-done.13, bf16[256,768]{1,0:T(8,128)(2,1)} %copy-done.14, bf16[256,768]{1,0:T(8,128)(2,1)} %copy-done.16, ...), custom_call_target="tpu_custom_call" | custom-call | tf_op jit(solution)/shard_map/result/pallas_call | solution.py:674
  316.0 6.7 %collective-permute-done.71 = bf16[64,768]{1,0:T(8,128)(2,1)S(1)} collective-permute-done((bf16[64,768]{1,0:T(8,128)(2,1)S(1)}, bf16[64,768]{1,0:T(8,128)(2,1)S(1)}, u32[]{:S(2)}, u32[]{:S(2)}) %collective-permute-start.71) | collective-permute-done | bytes 98336 | tf_op jit(solution)/shard_map/ppermute | solution.py:420
  322.7 11.3 %collective-permute-start.50 = (bf16[256,768]{1,0:T(8,128)(2,1)}, bf16[256,768]{1,0:T(8,128)(2,1)S(1)}, u32[]{:S(2)}, u32[]{:S(2)}) collective-permute-start(bf16[256,768]{1,0:T(8,128)(2,1)} %get-tuple-element.89), channel_id=1, source_target_pairs={{0,6},{1,7},{2,0},{3,1},{4,2},{5,3},{6,4},{7,5},{8,14},{9,15},{10,... | collective-permute-start | bytes 1179656 | tf_op jit(solution)/shard_map/ppermute | solution.py:414
  343.8 27.3 %collective-permute-done.52.refs_2_ = bf16[256,768]{1,0:T(8,128)(2,1)S(1)} collective-permute-done((bf16[256,768]{1,0:T(8,128)(2,1)}, bf16[256,768]{1,0:T(8,128)(2,1)S(1)}, u32[]{:S(2)}, u32[]{:S(2)}) %collective-permute-start.52) | collective-permute-done | bytes 393248 | tf_op jit(solution)/shard_map/ppermute | solution.py:414
  382.1 31.5 %attend_back.1 = (bf16[3,768,384]{2,1,0:T(8,128)(2,1)}, bf16[1536,768]{1,0:T(8,128)(2,1)}, f32[8,768]{1,0:T(8,128)}) custom-call(bf16[3,512,128]{2,1,0:T(8,128)(2,1)} %bitcast.281, bf16[3,1536,128]{2,1,0:T(8,128)(2,1)} %bitcast.266, bf16[3,1536,128]{2,1,0:T(8,128)(2,1)} %bitcast.268, f32[3,512,128]{2,1,0:T(8,128)} %get-tuple-element.66.o_ref, ...), custom_call_target="tpu_custom_call" | custom-call | tf_op jit(solution)/shard_map/attend_back/pallas_call | solution.py:709
  430.3 4.9 collective-permute-done.62
  437.5 10.0 %collective-permute-done.61 = bf16[4,194,384]{2,0,1:T(4,128)(2,1)} collective-permute-done((bf16[4,194,384]{2,0,1:T(4,128)(2,1)}, bf16[4,194,384]{2,0,1:T(4,128)(2,1)}, u32[]{:S(2)}, u32[]{:S(2)}) %collective-permute-start.61) | collective-permute-done | bytes 596000 | tf_op jit(solution)/shard_map/ppermute | solution.py:420
  455.5 14.8 %collective-permute-start.63 = (bf16[194,384]{1,0:T(8,128)(2,1)S(1)}, bf16[194,384]{1,0:T(8,128)(2,1)S(1)}, u32[]{:S(2)}, u32[]{:S(2)}) collective-permute-start(bf16[194,384]{1,0:T(8,128)(2,1)S(1)} %get-tuple-element.124), channel_id=1, source_target_pairs={{0,2},{1,3},{2,4},{3,5},{4,6},{5,7},{6,0},{7,1},{8,10},{9,11},{10,... | collective-permute-start | bytes 446984 | tf_op jit(solution)/shard_map/ppermute | solution.py:414
  483.0 10.0 %collective-permute-done.57.refs_1_ = bf16[256,768]{1,0:T(8,128)(2,1)S(1)} collective-permute-done((bf16[256,768]{1,0:T(8,128)(2,1)S(1)}, bf16[256,768]{1,0:T(8,128)(2,1)S(1)}, u32[]{:S(2)}, u32[]{:S(2)}) %collective-permute-start.57) | collective-permute-done | bytes 393248 | tf_op jit(solution)/shard_map/ppermute | solution.py:417
  493.1 13.9 %collective-permute-done.58.refs_2_ = bf16[256,768]{1,0:T(8,128)(2,1)S(1)} collective-permute-done((bf16[256,768]{1,0:T(8,128)(2,1)S(1)}, bf16[256,768]{1,0:T(8,128)(2,1)S(1)}, u32[]{:S(2)}, u32[]{:S(2)}) %collective-permute-start.58) | collective-permute-done | bytes 393248 | tf_op jit(solution)/shard_map/ppermute | solution.py:417
  (404 shorter events, 204.1 us)
Async XLA Ops:
  9.8 113.7 %collective-permute-start = (bf16[264,768]{1,0:T(8,128)(2,1)}, bf16[264,768]{1,0:T(8,128)(2,1)}, u32[]{:S(2)}, u32[]{:S(2)}) collective-permute-start(bf16[264,768]{1,0:T(8,128)(2,1)} %fusion.15.refs_0_), channel_id=1, source_target_pairs={{0,2},{1,3},{2,4},{3,5},{4,6},{5,7},{8,10},{9,11},{10,12},{11,13},... | collective-permute-start | bytes 1216520 | tf_op jit(solution)/shard_map/ppermute | solution.py:417
  15.5 79.3 %collective-permute-start.1 = (bf16[264,768]{1,0:T(8,128)(2,1)}, bf16[264,768]{1,0:T(8,128)(2,1)}, u32[]{:S(2)}, u32[]{:S(2)}) collective-permute-start(bf16[264,768]{1,0:T(8,128)(2,1)} %fusion.15.refs_0_), channel_id=1, source_target_pairs={{0,4},{1,5},{2,6},{3,7},{8,12},{9,13},{10,14},{11,15},{16,20},{17,... | collective-permute-start | bytes 1216520 | tf_op jit(solution)/shard_map/ppermute | solution.py:417
  20.0 72.5 %collective-permute-start.2 = (bf16[264,768]{1,0:T(8,128)(2,1)}, bf16[264,768]{1,0:T(8,128)(2,1)}, u32[]{:S(2)}, u32[]{:S(2)}) collective-permute-start(bf16[264,768]{1,0:T(8,128)(2,1)} %fusion.15.refs_0_), channel_id=1, source_target_pairs={{0,1},{1,0},{2,3},{3,2},{4,5},{5,4},{6,7},{7,6},{8,9},{9,8},{10,11... | collective-permute-start | bytes 1216520 | tf_op jit(solution)/shard_map/ppermute | solution.py:411
  25.5 66.9 %all-to-all-start = ((bf16[8,24,512]{2,1,0:T(8,128)(2,1)}), bf16[8,24,512]{2,1,0:T(8,128)(2,1)S(1)}, u32[]{:S(2)}, u32[]{:S(2)}) async-start(bf16[8,24,512]{2,1,0:T(8,128)(2,1)} %pad_maximum_fusion.3), calls=%async_computation | async-start | bytes 393216 | tf_op jit(solution)/shard_map/all_to_all | solution.py:526
  28.9 481.7 %reduce-scatter.5.cloned.1.call-start = ((), (), s32[]{:S(2)}) async-start(), calls=%async_computation.5 | async-start | bytes 3932160 | tf_op jit(solution)/shard_map/reduce_scatter | solution.py:672
  82.2 38.5 %collective-permute-start.9 = (bf16[4,160,384]{2,1,0:T(8,128)(2,1)}, bf16[4,160,384]{2,1,0:T(8,128)(2,1)}, u32[]{:S(2)}, u32[]{:S(2)}) collective-permute-start(bf16[4,160,384]{2,1,0:T(8,128)(2,1)} %bitcast_dynamic-update-slice_fusion.12), channel_id=1, source_target_pairs={{0,8},{8,0},{16,24},{24,16},{1,9},{9,1},{17,25},{25,17},{2,10},{10... | collective-permute-start | bytes 1474568 | tf_op jit(solution)/shard_map/ppermute | solution.py:420
  88.5 33.8 %collective-permute-start.10 = (bf16[4,160,384]{2,1,0:T(8,128)(2,1)}, bf16[4,160,384]{2,1,0:T(8,128)(2,1)}, u32[]{:S(2)}, u32[]{:S(2)}) collective-permute-start(bf16[4,160,384]{2,1,0:T(8,128)(2,1)} %bitcast_dynamic-update-slice_fusion.12), channel_id=1, source_target_pairs={{0,16},{8,24},{16,0},{24,8},{1,17},{9,25},{17,1},{25,9},{2,18},{10... | collective-permute-start | bytes 1474568 | tf_op jit(solution)/shard_map/ppermute | solution.py:420
  119.7 35.6 %collective-permute-start.20 = (bf16[768,384]{1,0:T(8,128)(2,1)S(1)}, bf16[768,384]{1,0:T(8,128)(2,1)}, u32[]{:S(2)}, u32[]{:S(2)}) collective-permute-start(bf16[768,384]{1,0:T(8,128)(2,1)S(1)} %bitcast.276), channel_id=1, source_target_pairs={{0,1},{1,0},{2,3},{3,2},{4,5},{5,4},{6,7},{7,6},{8,9},{9,8},{10,11... | collective-permute-start | bytes 1769480 | tf_op jit(solution)/shard_map/ppermute | solution.py:411
  120.7 33.4 %collective-permute-start.28 = (bf16[264,768]{1,0:T(8,128)(2,1)S(1)}, bf16[264,768]{1,0:T(8,128)(2,1)}, u32[]{:S(2)}, u32[]{:S(2)}) collective-permute-start(bf16[264,768]{1,0:T(8,128)(2,1)S(1)} %fusion.16.refs_0_.refs_8_), channel_id=1, source_target_pairs={{0,1},{1,0},{2,3},{3,2},{4,5},{5,4},{6,7},{7,6},{8,9},{9,8},{10,11... | collective-permute-start | bytes 1216520 | tf_op jit(solution)/shard_map/ppermute | solution.py:411
  161.8 49.5 %collective-permute-start.21 = (bf16[256,768]{1,0:T(8,128)(2,1)}, bf16[256,768]{1,0:T(8,128)(2,1)S(1)}, u32[]{:S(2)}, u32[]{:S(2)}) collective-permute-start(bf16[256,768]{1,0:T(8,128)(2,1)} %get-tuple-element.56.refs_0_), channel_id=1, source_target_pairs={{0,1},{1,0},{2,3},{3,2},{4,5},{5,4},{6,7},{7,6},{8,9},{9,8},{10,11... | collective-permute-start | bytes 1179656 | tf_op jit(solution)/shard_map/ppermute | solution.py:411
  180.5 30.8 %collective-permute-start.23 = (bf16[256,768]{1,0:T(8,128)(2,1)S(1)}, bf16[256,768]{1,0:T(8,128)(2,1)S(1)}, u32[]{:S(2)}, u32[]{:S(2)}) collective-permute-start(bf16[256,768]{1,0:T(8,128)(2,1)S(1)} %collective-permute-done.22.refs_2_), channel_id=1, source_target_pairs={{0,1},{1,0},{2,3},{3,2},{4,5},{5,4},{6,7},{7,6},{8,9},{9,8},{10,11... | collective-permute-start | bytes 1179656 | tf_op jit(solution)/shard_map/ppermute | solution.py:411
  267.7 245.4 %reduce-scatter.3.cloned.1.call-start = ((), (), s32[]{:S(2)}) async-start(), calls=%async_computation.4 | async-start | bytes 7864320 | tf_op jit(solution)/shard_map/reduce_scatter | solution.py:670
  276.0 31.1 %collective-permute-start.51 = (bf16[256,768]{1,0:T(8,128)(2,1)}, bf16[256,768]{1,0:T(8,128)(2,1)}, u32[]{:S(2)}, u32[]{:S(2)}) collective-permute-start(bf16[256,768]{1,0:T(8,128)(2,1)} %get-tuple-element.92), channel_id=1, source_target_pairs={{0,1},{1,0},{2,3},{3,2},{4,5},{5,4},{6,7},{7,6},{8,9},{9,8},{10,11... | collective-permute-start | bytes 1179656 | tf_op jit(solution)/shard_map/ppermute | solution.py:411
  276.5 30.8 %collective-permute-start.49 = (bf16[256,768]{1,0:T(8,128)(2,1)}, bf16[256,768]{1,0:T(8,128)(2,1)}, u32[]{:S(2)}, u32[]{:S(2)}) collective-permute-start(bf16[256,768]{1,0:T(8,128)(2,1)} %get-tuple-element.93), channel_id=1, source_target_pairs={{0,1},{1,0},{2,3},{3,2},{4,5},{5,4},{6,7},{7,6},{8,9},{9,8},{10,11... | collective-permute-start | bytes 1179656 | tf_op jit(solution)/shard_map/ppermute | solution.py:411
  276.6 32.7 %collective-permute-start.48 = (bf16[256,768]{1,0:T(8,128)(2,1)}, bf16[256,768]{1,0:T(8,128)(2,1)}, u32[]{:S(2)}, u32[]{:S(2)}) collective-permute-start(bf16[256,768]{1,0:T(8,128)(2,1)} %get-tuple-element.94), channel_id=1, source_target_pairs={{0,1},{1,0},{2,3},{3,2},{4,5},{5,4},{6,7},{7,6},{8,9},{9,8},{10,11... | collective-permute-start | bytes 1179656 | tf_op jit(solution)/shard_map/ppermute | solution.py:411
  300.6 33.3 %collective-permute-start.69 = (bf16[192,512]{1,0:T(8,128)(2,1)S(1)}, bf16[192,512]{1,0:T(8,128)(2,1)S(1)}, u32[]{:S(2)}, u32[]{:S(2)}) collective-permute-start(bf16[192,512]{1,0:T(8,128)(2,1)S(1)} %get-tuple-element.120), channel_id=1, source_target_pairs={{0,24},{8,16},{16,8},{24,0},{1,25},{9,17},{17,9},{25,1},{2,26},{10... | collective-permute-start | bytes 589832 | tf_op jit(solution)/shard_map/ppermute | solution.py:420
  333.9 37.2 %collective-permute-start.52 = (bf16[256,768]{1,0:T(8,128)(2,1)}, bf16[256,768]{1,0:T(8,128)(2,1)S(1)}, u32[]{:S(2)}, u32[]{:S(2)}) collective-permute-start(bf16[256,768]{1,0:T(8,128)(2,1)} %get-tuple-element.88), channel_id=1, source_target_pairs={{0,4},{1,5},{2,6},{3,7},{4,0},{5,1},{6,2},{7,3},{8,12},{9,13},{10,... | collective-permute-start | bytes 1179656 | tf_op jit(solution)/shard_map/ppermute | solution.py:414
  334.0 37.2 %collective-permute-start.54 = (bf16[256,768]{1,0:T(8,128)(2,1)}, bf16[256,768]{1,0:T(8,128)(2,1)S(1)}, u32[]{:S(2)}, u32[]{:S(2)}) collective-permute-start(bf16[256,768]{1,0:T(8,128)(2,1)} %get-tuple-element.87), channel_id=1, source_target_pairs={{0,2},{1,3},{2,4},{3,5},{4,6},{5,7},{6,0},{7,1},{8,10},{9,11},{10,... | collective-permute-start | bytes 1179656 | tf_op jit(solution)/shard_map/ppermute | solution.py:414
  336.1 84.6 %collective-permute-start.42 = (bf16[256,768]{1,0:T(8,128)(2,1)}, bf16[256,768]{1,0:T(8,128)(2,1)}, u32[]{:S(2)}, u32[]{:S(2)}) collective-permute-start(bf16[256,768]{1,0:T(8,128)(2,1)} %get-tuple-element.98), channel_id=1, source_target_pairs={{0,1},{1,0},{2,3},{3,2},{4,5},{5,4},{6,7},{7,6},{8,9},{9,8},{10,11... | collective-permute-start | bytes 1179656 | tf_op jit(solution)/shard_map/ppermute | solution.py:411
  336.1 86.5 %collective-permute-start.46 = (bf16[256,768]{1,0:T(8,128)(2,1)}, bf16[256,768]{1,0:T(8,128)(2,1)}, u32[]{:S(2)}, u32[]{:S(2)}) collective-permute-start(bf16[256,768]{1,0:T(8,128)(2,1)} %get-tuple-element.96), channel_id=1, source_target_pairs={{0,1},{1,0},{2,3},{3,2},{4,5},{5,4},{6,7},{7,6},{8,9},{9,8},{10,11... | collective-permute-start | bytes 1179656 | tf_op jit(solution)/shard_map/ppermute | solution.py:411
  338.4 87.5 %all-to-all-start.1 = ((bf16[8,24,512]{2,1,0:T(8,128)(2,1)}), bf16[8,24,512]{2,1,0:T(8,128)(2,1)S(1)}, u32[]{:S(2)}, u32[]{:S(2)}) async-start(bf16[8,24,512]{2,1,0:T(8,128)(2,1)} %bitcast.109), calls=%async_computation.1 | async-start | bytes 393216 | tf_op jit(solution)/shard_map/all_to_all | solution.py:805
  343.8 79.4 %collective-permute-start.44 = (bf16[256,768]{1,0:T(8,128)(2,1)}, bf16[256,768]{1,0:T(8,128)(2,1)}, u32[]{:S(2)}, u32[]{:S(2)}) collective-permute-start(bf16[256,768]{1,0:T(8,128)(2,1)} %get-tuple-element.97), channel_id=1, source_target_pairs={{0,1},{1,0},{2,3},{3,2},{4,5},{5,4},{6,7},{7,6},{8,9},{9,8},{10,11... | collective-permute-start | bytes 1179656 | tf_op jit(solution)/shard_map/ppermute | solution.py:411
  371.1 78.3 %collective-permute-start.41 = (bf16[256,768]{1,0:T(8,128)(2,1)}, bf16[256,768]{1,0:T(8,128)(2,1)}, u32[]{:S(2)}, u32[]{:S(2)}) collective-permute-start(bf16[256,768]{1,0:T(8,128)(2,1)} %get-tuple-element.95), channel_id=1, source_target_pairs={{0,1},{1,0},{2,3},{3,2},{4,5},{5,4},{6,7},{7,6},{8,9},{9,8},{10,11... | collective-permute-start | bytes 1179656 | tf_op jit(solution)/shard_map/ppermute | solution.py:411
  380.0 34.6 %collective-permute-start.59 = (bf16[768,384]{1,0:T(8,128)(2,1)S(1)}, bf16[768,384]{1,0:T(8,128)(2,1)S(1)}, u32[]{:S(2)}, u32[]{:S(2)}) collective-permute-start(bf16[768,384]{1,0:T(8,128)(2,1)S(1)} %broadcast_select_fusion), channel_id=1, source_target_pairs={{0,1},{1,0},{2,3},{3,2},{4,5},{5,4},{6,7},{7,6},{8,9},{9,8},{10,11... | collective-permute-start | bytes 1769480 | tf_op jit(solution)/shard_map/ppermute | solution.py:411
  (91 other events, 1432.6 us)
Sparse Core Ops, SparseCore 0:
  267.8 58.9 reduce-scatter.4
  329.8 74.3 reduce-scatter.2

commit v2 on v1

--- a/solution.py
+++ b/solution.py
@@ -47,6 +47,14 @@
 
 def params(**kw):
     return pltpu.CompilerParams(vmem_limit_bytes=VMEM_LIMIT, **kw)
+
+
+def cost(micros):
+    return pl.CostEstimate(flops=int(micros * 1.1e9), bytes_accessed=int(micros * 1e5), transcendentals=0)
+
+
+def after(x, *deps):
+    return lax.optimization_barrier((x,) + deps)[0]
 
 
 def whole(shape):
@@ -122,17 +130,14 @@
     h_ref[...] = (mid * rms_scale(mid) * g_ref[...]).astype(BF)
 
 
-def pre_kernel(nblk, rows, *refs):
-    og = refs[:nblk]
-    p_ref, wd, wsd, dehid, ogx_t, dsh, ogx = refs[nblk:]
+def pre_kernel(nblk, rows, ix, og, p_ref, wd, dehid, ogx_t, ogx):
     cap = p_ref.shape[1]
 
     @pl.when(pl.program_id(0) == 0)
     def _():
         for b in range(nblk):
-            block = og[b][0:rows, :]
-            ogx[b * cap : (b + 1) * cap, :] = nn(p_ref[b], block).astype(BF)
-            dsh[b * rows : (b + 1) * rows, :] = nt(block, wsd[...]).astype(BF)
+            block = og[ix[b], 0:rows, :]
+            ogx[b * cap : (b + 1) * cap, :] = nn(p_ref[ix[b]], block).astype(BF)
         ogx_t[...] = ogx[...].T
 
     dehid[...] = nt(ogx[...], wd[...]).astype(BF)
@@ -153,11 +158,13 @@
     return nn(a, high) + nn(a, (wide - high.astype(F32)).astype(BF))
 
 
-def expert_kernel(nblk, rows, experts, e_ref, *refs):
+def expert_kernel(nblk, rows, experts, e_ref, ix, *refs):
     g_refs = refs[:nblk]
-    (p_ref, pt_ref, wr, wr_t, wsg, wsu, dsh, wg, wu, dehid) = refs[nblk : nblk + 10]
-    (x_out, ehid, degate, deup, gate_slot, gate_tok, shid, dsg, dsu, tg, rgrad) = refs[nblk + 10 : nblk + 21]
-    x_scr, row_scr, tg_scr, pg_scr, prob_scr, gs_scr = refs[nblk + 21 :]
+    (p_ref, pt_ref, wr, wr_t, wsg, wsu, wsd, og, wg, wu, dehid) = refs[nblk : nblk + 11]
+    (x_out, ehid, degate, deup, gate_slot, gate_tok, shid, dsg, dsu, tg, tg_far, rgrad) = refs[
+        nblk + 11 : nblk + 23
+    ]
+    x_scr, row_scr, tg_scr, pg_scr, prob_scr, gs_scr = refs[nblk + 23 :]
     cap = p_ref.shape[1]
     step = pl.program_id(0)
     own = lanes((rows, 128)) == e_ref[0]
@@ -168,7 +175,7 @@
         pg_scr[...] = jnp.zeros_like(pg_scr)
         for b in range(nblk):
             block = g_refs[b][...]
-            x = nn(p_ref[b], block).astype(BF)
+            x = nn(p_ref[ix[b]], block).astype(BF)
             x_scr[b * cap : (b + 1) * cap, :] = x
             x_out[b * cap : (b + 1) * cap, :] = x
             logits = jnp.where(lanes((rows, 128)) < experts, nn(block, wr[...]), NEG_LARGE)
@@ -177,11 +184,12 @@
             prob_scr[b] = probs
             gate = jnp.sum(jnp.where(own, probs, 0.0), axis=1, keepdims=True)
             gate_tok[b] = jnp.broadcast_to(gate, (rows, 128))
-            slot = split_nn(p_ref[b], gate)
+            slot = split_nn(p_ref[ix[b]], gate)
             gs_scr[b * cap : (b + 1) * cap, :] = slot
             gate_slot[b * cap : (b + 1) * cap, :] = slot
             at = b * rows
-            hid, dg, du = act(nn(block, wsg[...]), nn(block, wsu[...]), dsh[at : at + rows, :].astype(F32))
+            dsh = nt(og[ix[b], 0:rows, :], wsd[...])
+            hid, dg, du = act(nn(block, wsg[...]), nn(block, wsu[...]), dsh)
             shid[at : at + rows, :] = hid
             dsg[at : at + rows, :] = dg
             dsu[at : at + rows, :] = du
@@ -200,30 +208,50 @@
         total = jnp.zeros_like(rgrad)
         for b in range(nblk):
             at = b * rows
-            pg = split_nn(pt_ref[b], pg_scr[b * cap : (b + 1) * cap, 0:1])
+            pg = split_nn(pt_ref[ix[b]], pg_scr[b * cap : (b + 1) * cap, 0:1])
             probs = prob_scr[b]
             gate = jnp.sum(jnp.where(own, probs, 0.0), axis=1, keepdims=True)
             lgrad = (pg * probs * (own.astype(F32) - gate)).astype(BF)
             total += tn(lgrad, g_refs[b][...])
-            back = nn(pt_ref[b], row_scr[b * cap : (b + 1) * cap, :].astype(BF))
-            tg[b] = (tg_scr[at : at + rows, :] + back + nn(lgrad, wr_t[...])).astype(BF)
+            back = nn(pt_ref[ix[b]], row_scr[b * cap : (b + 1) * cap, :].astype(BF))
+            (tg_far if b % 2 else tg)[b // 2] = (tg_scr[at : at + rows, :] + back + nn(lgrad, wr_t[...])).astype(BF)
         rgrad[...] = total
 
 
-def wgrad_kernel(x_ref, ogx_t, gate_slot, ehid, degate, deup, gu, dn, x_t):
+def wgrad_kernel(per, r_ref, x_ref, degate, deup, gate_near, gate_far, up_near, up_far, x_t):
+    step = pl.program_id(0)
+
+    @pl.when(step == 0)
+    def _():
+        x_t[...] = x_ref[...].T
+
+    @pl.when(step < 2 * per)
+    def _():
+        gate_near[0] = nn(x_t[...], degate[...]).astype(BF)
+        up_near[0] = nn(x_t[...], deup[...]).astype(BF)
+
+    @pl.when(step >= 2 * per)
+    def _():
+        gate_far[0] = nn(x_t[...], degate[...]).astype(BF)
+        up_far[0] = nn(x_t[...], deup[...]).astype(BF)
+
+
+def wgrad_all_kernel(r_ref, x_ref, degate, deup, gate, up, x_t):
     @pl.when(pl.program_id(0) == 0)
     def _():
         x_t[...] = x_ref[...].T
 
-    gu[0, 0] = nn(x_t[...], degate[...]).astype(BF)
-    gu[0, 1] = nn(x_t[...], deup[...]).astype(BF)
+    gate[0] = nn(x_t[...], degate[...]).astype(BF)
+    up[0] = nn(x_t[...], deup[...]).astype(BF)
+
+
+def down_grad_kernel(ogx_t, gate_slot, ehid, dn):
     dn[...] = nn(ogx_t[...], (ehid[...].astype(F32) * gate_slot[:, 0:1]).astype(BF)).astype(BF)
 
 
-def result_kernel(nblk, rows, *refs):
-    g_refs, og = refs[:nblk], refs[nblk : 2 * nblk]
-    (pt_ref, gate_tok, shid, dsg, dsu, wsd, ehid, wd) = refs[2 * nblk : 2 * nblk + 8]
-    mix, sgu, sd, acc = refs[2 * nblk + 8 :]
+def result_kernel(nblk, rows, ix, *refs):
+    g_refs = refs[:nblk]
+    og, pt_ref, gate_tok, shid, dsg, dsu, wsd, ehid, wd, mix, sgu, sd, acc = refs[nblk:]
     cap = pt_ref.shape[2]
     step = pl.program_id(0)
 
@@ -238,7 +266,7 @@
             g_t = g_refs[b][...].T
             dg_sum += nn(g_t, dsg[at : at + rows, :])
             du_sum += nn(g_t, dsu[at : at + rows, :])
-            sd_sum += tn(shid[at : at + rows, :], og[b][0:rows, :])
+            sd_sum += tn(shid[at : at + rows, :], og[ix[b], 0:rows, :])
         width = dsg.shape[1]
         sgu[:, :width] = dg_sum.astype(BF)
         sgu[:, width:] = du_sum.astype(BF)
@@ -251,8 +279,8 @@
         for b in range(nblk):
             at = b * rows
             res = acc[b * cap : (b + 1) * cap, :].astype(BF)
-            picked = nn(pt_ref[b], res) * gate_tok[b][:, 0:1]
-            mix[b] = (picked + nn(shid[at : at + rows, :], wsd[...])).astype(BF)
+            picked = nn(pt_ref[ix[b]], res) * gate_tok[b][:, 0:1]
+            mix[ix[b]] = (picked + nn(shid[at : at + rows, :], wsd[...])).astype(BF)
 
 
 def mid_back_kernel(count, *refs):
@@ -276,7 +304,7 @@
 
 
 def attend_back_kernel(first, count, rows, q_ref, k_ref, v_ref, o_ref, do_ref, lse_ref, sq_ref, sk_ref, cos, sin,
-                       h1_ref, wq, wk, wv, gain, grads, og1, gg, h1_t, k_t, dk, dv, og_scr):
+                       h1_ref, wq, wk, wv, gain, c_ref, grads, og_own, og_far, gg, h1_t, k_t, dk, dv, og_scr):
     step = pl.program_id(0)
     low = lanes((rows, 128)) < 64
     kv_rows = k_ref.shape[1]
@@ -336,7 +364,17 @@
     @pl.when(step == pl.num_programs(0) - 1)
     def _():
         one = og_scr[...]
-        og1[...] = one.astype(BF)
+        for slot in range(kv_rows // rows):
+            block = one[slot * rows : (slot + 1) * rows, :].astype(BF)
+
+            @pl.when(c_ref[0] == slot % 2)
+            def _():
+                og_own[slot // 2] = block
+
+            @pl.when(c_ref[0] != slot % 2)
+            def _():
+                og_far[slot // 2] = block
+
         total = jnp.sum(one * h1_ref[...].astype(F32), axis=0, keepdims=True) / gain[...]
         gg[...] = jnp.broadcast_to(total, gg.shape)
 
@@ -442,22 +480,33 @@
             buf = put(buf, ring(pack, s), (z - s) % Z)
         return buf
 
-    def gather_rep(part):
+    def gather_rep(part, *deps):
+        got = [cross(part, s) for s in range(1, R)]
+        if deps:
+            got = [after(x, *deps) for x in got]
         buf = put(jnp.zeros((R,) + part.shape, BF), part, r)
         for s in range(1, R):
-            buf = put(buf, cross(part, s), r ^ s)
+            buf = put(buf, got[s - 1], r ^ s)
         return buf
 
     def unpack(full, i):
         return full[:, :, i * hrow : (i + 1) * hrow, :].reshape(D, half)
 
-    pack1 = chip_pack([w_query, w_key, w_value], norm1_gain)
-    full1 = gather_rep(gather_z(pack1))
-    wq, wk, wv = (unpack(full1, i) for i in range(3))
-    gain1 = full1[:, :, 3 * hrow : 3 * hrow + 2, :wrow].reshape(1, D).astype(F32)
+    pack = chip_pack(
+        [w_query, w_key, w_value, w_out], jnp.concatenate([norm1_gain, norm2_gain, w_router.reshape(-1)])
+    )
+    part = gather_z(pack)
+    full = gather_rep(part)
+    wq, wk, wv, wo_half = (unpack(full, i) for i in range(4))
+    ext = full[:, :, 4 * hrow : 4 * hrow + 2, :].reshape(R * E, half)
+    gain1 = ext[:, :wrow].reshape(1, D).astype(F32)
+    gain2 = ext[:, wrow : 2 * wrow].reshape(1, D).astype(F32)
+    router = ext[:, 2 * wrow : (2 + experts) * wrow].reshape(D, experts)
+    router = jnp.pad(router, ((0, 0), (0, 128 - experts)))
+    router_t = router.T
 
     seg_row = jnp.pad(segment_ids.reshape(1, T).astype(BF), ((0, 7), (0, D - T)))
-    tok_pack = jnp.concatenate([tokens, seg_row], axis=0)
+    tok_pack = after(jnp.concatenate([tokens, seg_row], axis=0), pack)
     own_tok = [tok_pack] + [line(tok_pack, s) for s in range(1, chips)]
     par_tok = [swap(x) for x in own_tok]
 
@@ -474,9 +523,10 @@
 
     inverse = jnp.exp(jnp.arange(32).astype(F32) * (-2.0 * math.log(10000.0) / 64))
     inverse = jnp.tile(inverse, 4)
-    places = (z - nb) * (2 * T) + jnp.arange(kv_rows, dtype=jnp.int32)
+    places = after((z - nb) * (2 * T) + jnp.arange(kv_rows, dtype=jnp.int32), pack)
     angle = places.astype(F32)[:, None] * inverse[None, :]
-    cos, sin = jnp.cos(angle), jnp.sin(angle)
+    cos, sin = lax.optimization_barrier((jnp.cos(angle), jnp.sin(angle)))
+    cos, sin = cos.reshape(kvb, T, 128), sin.reshape(kvb, T, 128)
 
     h1, keys, vals, quer = pl.pallas_call(
         functools.partial(qkv_kernel, chips, T),
@@ -490,53 +540,32 @@
         ),
         compiler_params=params(),
         name="qkv",
-    )(c_arr, *own_tok, *par_tok, wq, wk, wv, cos.reshape(kvb, T, 128), sin.reshape(kvb, T, 128), gain1)
+        cost_estimate=cost(8),
+    )(c_arr, *own_tok, *par_tok, wq, wk, wv, cos, sin, gain1)
     h1 = h1.reshape(kv_rows, D)
     keys = keys.reshape(pairs, kv_rows, 128)
     vals = vals.reshape(pairs, kv_rows, 128)
     quer = quer.reshape(pairs, 2 * T, 128)
 
-    tok_done = own_tok[-1]
     og_pack = jnp.concatenate(
         [out_grad, jnp.pad(routes.reshape(1, topk * T).astype(BF), ((0, 7), (0, D - topk * T)))], axis=0
     )
-    og_pack, full1_dep, tok_done = lax.optimization_barrier((og_pack, full1[0, 0, 0], tok_done))
-
-    def gather_ep(x):
-        lane = [x] + [ring(x, s) for s in range(1, Z)]
-        blocks = []
-        for item in lane:
-            blocks += [item, swap(item)]
-        return blocks
-
-    pack2 = chip_pack([w_out], jnp.concatenate([norm2_gain, w_router.reshape(-1)]))
-    full2 = gather_rep(gather_z(pack2))
-    wo_half = unpack(full2, 0)
+    og_all = lax.all_gather(after(og_pack, pack), "ep", axis=0)
+    ix_arr = jnp.stack([((z - b // 2) % Z) * 2 + (c ^ (b % 2)) for b in range(E)]).astype(jnp.int32)
+
     wo = jnp.concatenate(ordered(wo_half, swap(wo_half)), axis=1)
-    ext2 = full2[:, :, hrow : hrow + 2, :].reshape(R * E, half)
-    gain2 = ext2[:, :wrow].reshape(1, D).astype(F32)
-    router = ext2[:, wrow : wrow + wrow * experts].reshape(D, experts)
-    router = jnp.pad(router, ((0, 0), (0, 128 - experts)))
-    router_t = router.T
 
     def by_unit(w):
         return w.reshape(wrow, R, E, drow).transpose(2, 0, 1, 3).reshape(E, wrow, fs)
 
     gu = jnp.concatenate([by_unit(shared_gate), by_unit(shared_up)], axis=2)
-    gu = lax.all_to_all(gu, "ep", split_axis=0, concat_axis=0, tiled=True).reshape(E * wrow, 2 * fs)
-    gu = gather_rep(gu).reshape(D, 2 * fs)
-    wsg, wsu = gu[:, :fs], gu[:, fs:]
-    wsd = gather_rep(shared_down).reshape(fs, D)
-
-    og_blocks = gather_ep(og_pack)
-    table = jnp.stack([x[T, : topk * T] for x in og_blocks]).reshape(E, T, topk)
-    hit = jnp.any(table == e.astype(F32).astype(BF), axis=2).astype(F32)
-    rank = jnp.cumsum(hit, axis=1) - hit
-    rank = jnp.where(hit > 0, rank, -1.0)
-    slot_ids = jnp.arange(cap).astype(F32)
-    pick = (rank[:, None, :] == slot_ids[None, :, None]).astype(BF)
-    pick_t = (rank[:, :, None] == slot_ids[None, None, :]).astype(BF)
-
+    gu = lax.all_to_all(after(gu, part), "ep", split_axis=0, concat_axis=0, tiled=True).reshape(E * wrow, 2 * fs)
+    gu = after(gu, keys)
+    wide = D // fs
+    shared = jnp.concatenate(
+        [gu[:, :fs], gu[:, fs:]] + [shared_down[:, k * fs : (k + 1) * fs] for k in range(wide)], axis=0
+    )
+    shared_got = [cross(shared, s) for s in range(1, R)]
     one = lambda *dims: pl.BlockSpec((1,) + dims, lambda i: (i, 0, 0))
     att, att_low, lse = pl.pallas_call(
         functools.partial(attend_kernel, first, count, T),
@@ -557,7 +586,8 @@
         scratch_shapes=[pltpu.VMEM((T, count * T), F32)],
         compiler_params=params(),
         name="attend",
-    )(quer, keys, vals, seg_wide[-2 * T :], seg_flat)
+        cost_estimate=cost(10),
+    )(after(quer, wo, shared), keys, vals, seg_wide[-2 * T :], seg_flat)
 
     def joined(mine, other):
         both = jnp.where(is0, jnp.concatenate([mine, other]), jnp.concatenate([other, mine]))
@@ -572,31 +602,61 @@
         out_shape=(shape((T, D), F32), shape((T, D))),
         compiler_params=params(),
         name="mid",
+        cost_estimate=cost(3),
     )(attended, wo, tokens, gain2)
 
+    shared_got = [after(x, h2) for x in shared_got]
+    shared = put(jnp.zeros((R,) + shared.shape, BF), after(shared, h2), r)
+    for i in range(1, R):
+        shared = put(shared, shared_got[i - 1], r ^ i)
+    gr = E * wrow
+    wsg = shared[:, :gr].reshape(D, fs)
+    wsu = shared[:, gr : 2 * gr].reshape(D, fs)
+    wsd = jnp.concatenate(
+        [shared[:, 2 * gr + k * drow : 2 * gr + (k + 1) * drow].reshape(fs, fs) for k in range(wide)], axis=1
+    )
+    h2_lane = [h2] + [ring(h2, s) for s in range(1, Z)]
+
+    def both_cores(lane):
+        blocks = []
+        for item in lane:
+            blocks += [item, swap(item)]
+        return blocks
+
+    og_all = after(og_all, h2)
+    table = og_all[:, T, : topk * T].reshape(E, T, topk)
+    hit = jnp.any(table == e.astype(F32).astype(BF), axis=2).astype(F32)
+    rank = jnp.cumsum(hit, axis=1) - hit
+    rank = jnp.where(hit > 0, rank, -1.0)
+    slot_ids = jnp.arange(cap).astype(F32)
+    pick = (rank[:, None, :] == slot_ids[None, :, None]).astype(BF)
+    pick_t = (rank[:, :, None] == slot_ids[None, None, :]).astype(BF)
+
+    smem = pl.BlockSpec(memory_space=pltpu.SMEM)
     ft = min(256, FF // R)
     steps = FF // ft
     per = FF // R // ft
     col = lambda n: pl.BlockSpec((n, ft), lambda i: (0, i))
     wcol = pl.BlockSpec((1, D, ft), lambda i: (0, 0, i))
     wdn = pl.BlockSpec((1, ft, D), lambda i: (0, i, 0))
-    dehid, ogx_t, dsh = pl.pallas_call(
+    dehid, ogx_t = pl.pallas_call(
         functools.partial(pre_kernel, E, T),
         grid=(steps,),
-        in_specs=[whole((T + 8, D))] * E
-        + [whole((E, cap, T)), pl.BlockSpec((ft, D), lambda i: (i, 0)), whole((fs, D))],
-        out_specs=(col(slots), whole((D, slots)), whole((E * T, fs))),
-        out_shape=(shape((slots, FF)), shape((D, slots)), shape((E * T, fs))),
+        in_specs=[smem, whole((E, T + 8, D))]
+        + [whole((E, cap, T)), pl.BlockSpec((ft, D), lambda i: (i, 0))],
+        out_specs=(col(slots), whole((D, slots))),
+        out_shape=(shape((slots, FF)), shape((D, slots))),
         scratch_shapes=[pltpu.VMEM((slots, D), BF)],
         compiler_params=params(),
         name="pre",
-    )(*og_blocks, pick, expert_down.reshape(FF, D), wsd)
-
-    h2_blocks = gather_ep(h2)
-    (x_rows, ehid, degate, deup, gate_slot, gate_tok, shid, dsg, dsu, tg, rgrad) = pl.pallas_call(
+        cost_estimate=cost(12),
+    )(ix_arr, og_all, pick, expert_down.reshape(FF, D))
+
+    h2_blocks = both_cores([after(x, dehid) for x in h2_lane])
+    (x_rows, ehid, degate, deup, gate_slot, gate_tok, shid, dsg, dsu, tg, tg_far, rgrad) = pl.pallas_call(
         functools.partial(expert_kernel, E, T, experts),
         grid=(steps,),
-        in_specs=[pl.BlockSpec(memory_space=pltpu.SMEM)]
+        in_specs=[smem, smem]
         + [whole((T, D))] * E
         + [
             whole((E, cap, T)),
@@ -605,7 +665,8 @@
             whole((128, D)),
             whole((D, fs)),
             whole((D, fs)),
-            whole((E * T, fs)),
+            whole((fs, D)),
+            whole((E, T + 8, D)),
             wcol,
             wcol,
             col(slots),
@@ -620,7 +681,8 @@
             whole((E * T, fs)),
             whole((E * T, fs)),
             whole((E * T, fs)),
-            whole((E, T, D)),
+            whole((Z, T, D)),
+            whole((Z, T, D)),
             whole((128, D)),
         ),
         out_shape=(
@@ -633,7 +695,8 @@
             shape((E * T, fs)),
             shape((E * T, fs)),
             shape((E * T, fs)),
-            shape((E, T, D)),
+            shape((Z, T, D)),
+            shape((Z, T, D)),
             shape((128, D), F32),
         ),
         scratch_shapes=[
@@ -646,37 +709,97 @@
         ],
         compiler_params=params(),
         name="expert",
-    )(e_arr, *h2_blocks, pick, pick_t, router, router_t, wsg, wsu, dsh, expert_gate, expert_up, dehid)
-
-    def scatter_ep(blocks):
-        lane = [blocks[2 * s] + swap(blocks[2 * s + 1]) for s in range(Z)]
-        return [lane[0]] + [ring(lane[s], -s) for s in range(1, Z)]
-
-    two_parts = scatter_ep(tg)
-
-    gu_grad, dn_grad = pl.pallas_call(
-        wgrad_kernel,
+        cost_estimate=cost(38),
+    )(e_arr, ix_arr, *h2_blocks, pick, pick_t, router, router_t, wsg, wsu, wsd, og_all, expert_gate, expert_up, dehid)
+
+    def core_sums(mine, other, *deps):
+        got = swap(other)
+        if deps:
+            got = after(got, *deps)
+        return [mine[s] + got[s] for s in range(Z)]
+
+
+    r_arr = jnp.reshape(r, (1,)).astype(jnp.int32)
+    wide_rep = FF // R
+    square = R == 4
+    at0 = lambda n: pl.BlockSpec(n, lambda i, q: (0,) * len(n))
+    dn_grad = pl.pallas_call(
+        down_grad_kernel,
         grid=(steps,),
-        in_specs=[whole((slots, D)), whole((D, slots)), whole((slots, 128)), col(slots), col(slots), col(slots)],
-        out_specs=(
-            pl.BlockSpec((1, 2, D, ft), lambda i: (i // per, 0, 0, i % per)),
-            col(D),
+        in_specs=[whole((D, slots)), whole((slots, 128)), col(slots)],
+        out_specs=col(D),
+        out_shape=shape((D, FF)),
+        compiler_params=params(),
+        name="dgrad",
+        cost_estimate=cost(10),
+    )(ogx_t, gate_slot, ehid)
+    dn_sum = lax.psum_scatter(dn_grad, "rep", scatter_dimension=0, tiled=True)
+    lane = core_sums(tg, tg_far, dn_grad)
+    two_parts = [lane[0]] + [ring(lane[s], -s) for s in range(1, Z)]
+
+    if square:
+
+        def rel_col(swapped):
+            def index(i, q):
+                d = i // per
+                d = (d % 2) * 2 + d // 2 if swapped else d
+                return (0, (d ^ q[0]) * per + i % per)
+
+            return pl.BlockSpec((slots, ft), index)
+
+        early = pl.BlockSpec(
+            (1, D, ft),
+            lambda i, q: (jnp.minimum(i // per, 1), 0, jnp.where(i < 2 * per, i % per, per - 1)),
+        )
+        late = pl.BlockSpec(
+            (1, D, ft),
+            lambda i, q: (jnp.maximum(i // per - 2, 0), 0, jnp.where(i < 2 * per, 0, i % per)),
+        )
+        gu_in = [rel_col(True), rel_col(False)]
+        gu_specs = (early, late, early, late)
+        gu_shapes = [(2, D, wide_rep)] * 4
+        gu_kernel = functools.partial(wgrad_kernel, per)
+    else:
+        gu_in = [pl.BlockSpec((slots, ft), lambda i, q: (0, ((i // per) ^ q[0]) * per + i % per))] * 2
+        gu_specs = (pl.BlockSpec((1, D, ft), lambda i, q: (i // per, 0, i % per)),) * 2
+        gu_shapes = [(R, D, wide_rep)] * 2
+        gu_kernel = wgrad_all_kernel
+    gu_out = pl.pallas_call(
+        gu_kernel,
+        grid_spec=pltpu.PrefetchScalarGridSpec(
+            num_scalar_prefetch=1,
+            grid=(steps,),
+            in_specs=[at0((slots, D))] + gu_in,
+            out_specs=gu_specs,
+            scratch_shapes=[pltpu.VMEM((D, slots), BF)],
         ),
-        out_shape=(shape((R, 2, D, FF // R)), shape((D, FF))),
-        scratch_shapes=[pltpu.VMEM((D, slots), BF)],
+        out_shape=tuple(shape(dims) for dims in gu_shapes),
         compiler_params=params(),
         name="wgrad",
-    )(x_rows, ogx_t, gate_slot, ehid, degate, deup)
-    gu_sum = lax.psum_scatter(gu_grad.reshape(-1, FF // R), "rep", scatter_dimension=0, tiled=True)
-    gu_sum = gu_sum.reshape(1, 2, D, FF // R)
-    dn_sum = lax.psum_scatter(dn_grad, "rep", scatter_dimension=0, tiled=True)
-
+        cost_estimate=cost(13),
+    )(r_arr, after(x_rows, *lane), degate, deup)
+
+    def pieces(x):
+        return [lax.dynamic_index_in_dim(x, r ^ s, 0, keepdims=False) for s in range(R)]
+
+    def direct(pieces, *deps):
+        total = pieces[0].astype(F32)
+        for d in range(1, R):
+            got = cross(pieces[d], d)
+            total += (after(got, *deps) if deps else got).astype(F32)
+        return total
+
+    two_parts[2::2] = [after(x, gu_out[0]) for x in two_parts[2::2]]
+    near = []
+    if square:
+        gate_a, up_a = cross(gu_out[1][0], 1), cross(gu_out[3][0], 2)
     mix, sgu_grad, sd_grad = pl.pallas_call(
         functools.partial(result_kernel, E, T),
         grid=(steps,),
-        in_specs=[whole((T, D))] * E
-        + [whole((T + 8, D))] * E
+        in_specs=[smem]
+        + [whole((T, D))] * E
         + [
+            whole((E, T + 8, D)),
             whole((E, T, cap)),
             whole((E, T, 128)),
             whole((E * T, fs)),
@@ -691,7 +814,22 @@
         scratch_shapes=[pltpu.VMEM((slots, D), F32)],
         compiler_params=params(),
         name="result",
-    )(*h2_blocks, *og_blocks, pick_t, gate_tok, shid, dsg, dsu, wsd, ehid, expert_down)
+        cost_estimate=cost(19),
+    )(ix_arr, *h2_blocks, og_all, pick_t, gate_tok, shid, dsg, dsu, wsd, after(ehid, gu_out[0], *two_parts[2::2], *near), expert_down)
+
+    sgrad = jnp.concatenate(
+        [sgu_grad[:, :fs].reshape(R, gr, fs), sgu_grad[:, fs:].reshape(R, gr, fs)]
+        + [sd_grad[:, k * fs : (k + 1) * fs].reshape(R, drow, fs) for k in range(wide)],
+        axis=1,
+    )
+    two_parts[1::2] = [after(x, mix) for x in two_parts[1::2]]
+    if square:
+        gate_a, up_a = after(gate_a, mix), after(up_a, mix)
+        two_parts[0], gate_a, up_a = lax.optimization_barrier((two_parts[0], gate_a, up_a))
+        gate_c, up_c = cross(after(gu_out[1][1], mix), 1), cross(after(gu_out[3][1], mix), 2)
+
+    mix_in = after(mix, two_parts[1], *((gate_a, up_a) if square else ()))
+    mix_sum = lax.psum_scatter(mix_in.reshape(E * T, D), "ep", scatter_dimension=0, tiled=True)
 
     mid_grad, attn_grad, att_grad, gain2_part = pl.pallas_call(
         functools.partial(mid_back_kernel, Z),
@@ -700,13 +838,28 @@
         out_shape=(shape((T, D), F32), shape((T, D)), shape((2 * pairs, T, 128)), shape((8, D), F32)),
         compiler_params=params(),
         name="mid_back",
+        cost_estimate=cost(4),
     )(*two_parts, mid, gain2, out_grad, wo)
 
     ag_own, ag_other = ordered(att_grad[:pairs], att_grad[pairs:])
     do_a, do_b = ordered(ag_own, swap(ag_other))
     do = jnp.concatenate([do_a, do_b], axis=1)
-
-    grads, og1, gain1_part = pl.pallas_call(
+    wo_part = tn(attended, after(attn_grad, ag_other)).astype(BF)
+    wo_mine, wo_other = ordered(wo_part[:, :half], wo_part[:, half:])
+    wo_got = swap(wo_other)
+    if square:
+        gate_mid = gu_out[0][1] + after(gate_c, do)
+        up_mid = gu_out[2][1] + after(up_c, do)
+        gate_b, up_b = cross(gate_mid, 2), cross(up_mid, 1)
+        sg_own, sg_near, sg_a, sg_c = pieces(after(sgrad, do))
+        sg_send = jnp.stack([sg_a, sg_c])
+        sg_got = cross(sg_send, 2)
+        do, gate_mid, up_mid, wo_other, sg_send = lax.optimization_barrier(
+            (do, gate_mid, up_mid, wo_other, sg_send)
+        )
+
+    cos2, sin2 = cos.reshape(kv_rows, 128), sin.reshape(kv_rows, 128)
+    grads, og1, og1_far, gain1_part = pl.pallas_call(
         functools.partial(attend_back_kernel, first, count, T),
         grid=(pairs,),
         in_specs=[
@@ -725,13 +878,15 @@
             pl.BlockSpec((D, 128), lambda i: (0, i)),
             pl.BlockSpec((D, 128), lambda i: (0, i)),
             whole((1, D)),
+            smem,
         ],
         out_specs=(
             pl.BlockSpec((3, D, 128), lambda i: (0, 0, i)),
-            whole((kv_rows, D)),
+            whole((chips, T, D)),
+            whole((chips, T, D)),
             whole((8, D)),
         ),
-        out_shape=(shape((3, D, half)), shape((kv_rows, D)), shape((8, D), F32)),
+        out_shape=(shape((3, D, half)), shape((chips, T, D)), shape((chips, T, D)), shape((8, D), F32)),
         scratch_shapes=[
             pltpu.VMEM((D, kv_rows), BF),
             pltpu.VMEM((128, kv_rows), BF),
@@ -741,32 +896,18 @@
         ],
         compiler_params=params(),
         name="attend_back",
-    )(quer, keys, vals, att, do, lse, seg_flat[:, -2 * T :], seg_wide, cos, sin, h1, wq, wk, wv, gain1)
-
-    og1 = og1.reshape(chips, 2, T, D)
-    mine, other = ordered(og1[:, 0], og1[:, 1])
-    lane = mine + swap(other)
+        cost_estimate=cost(30),
+    )(quer, keys, vals, att, do, lse, seg_flat[:, -2 * T :], seg_wide, cos2, sin2, h1, wq, wk, wv, gain1, c_arr)
+
+    wo_got = after(wo_got, og1)
+    if square:
+        gate_b, up_b, sg_got = after(gate_b, og1), after(up_b, og1), after(sg_got, og1)
+        og1_far, grads, gate_b, up_b, wo_got, sg_got = lax.optimization_barrier(
+            (og1_far, grads, gate_b, up_b, wo_got, sg_got)
+        )
+    lane = og1 + swap(og1_far)
     one_parts = [lane[nb]] + [line(lane[nb - s], -s) for s in range(1, chips)]
-    tokens_grad = pl.pallas_call(
-        functools.partial(last_kernel, chips),
-        in_specs=vmem(chips + 3),
-        out_specs=vmem(1)[0],
-        out_shape=shape((T, D), F32),
-        compiler_params=params(),
-        name="last",
-    )(*one_parts, tokens, gain1, mid_grad)
-
-    mix_parts = scatter_ep(mix)
-    layer_out = mid
-    for part in mix_parts:
-        layer_out = layer_out + part.astype(F32)
-    layer_out = layer_out.astype(BF)
-
-    def reduce_rep(x):
-        total = lax.dynamic_index_in_dim(x, r, 0, keepdims=False).astype(F32)
-        for s in range(1, R):
-            total += cross(lax.dynamic_index_in_dim(x, r ^ s, 0, keepdims=False), s).astype(F32)
-        return total
+    lane_all = one_parts[1:]
 
     def reduce_z(x):
         total = lax.dynamic_index_in_dim(x, z, 0, keepdims=False).astype(F32)
@@ -774,9 +915,7 @@
             total += ring(lax.dynamic_index_in_dim(x, (z + s) % Z, 0, keepdims=False), s).astype(F32)
         return total
 
-    wo_part = tn(attended, attn_grad).astype(BF)
-    wo_mine, wo_other = ordered(wo_part[:, :half], wo_part[:, half:])
-    wo_lane = wo_mine + swap(wo_other)
+    wo_lane = wo_mine + wo_got
     n_chip = R * Z
     ext = jnp.concatenate(
         [
@@ -789,8 +928,9 @@
     ext = jnp.pad(ext, ((0, 0), (0, -ext.shape[1] % half))).reshape(n_chip, -1, half)
     dense = jnp.concatenate([grads, wo_lane[None]]).reshape(4, n_chip, hrow, half).transpose(1, 0, 2, 3)
     dense = jnp.concatenate([dense.reshape(n_chip, 4 * hrow, half), ext], axis=1)
-    dense = reduce_rep(dense.reshape((R, Z) + dense.shape[1:])).astype(BF)
-    dense = reduce_z(dense)
+    dense = jnp.pad(dense, ((0, 0), (0, -dense.shape[1] % 8), (0, 0)))
+    dense_rep = direct(pieces(dense.reshape((R, Z) + dense.shape[1:])), *lane_all).astype(BF)
+    dense = reduce_z(dense_rep)
     mats = dense[: 4 * hrow].reshape(4, 2, wrow, half)
     mats_mine, mats_other = ordered(mats[:, 0], mats[:, 1])
     ext = dense[4 * hrow :]
@@ -800,12 +940,45 @@
     ext = (ext + got[4 * wrow :]).reshape(-1)[: (2 + experts) * hrow].reshape(2 + experts, 2, wrow)
     ext = jnp.where(is0, ext[:, 0], ext[:, 1])
 
-    sgu = reduce_rep(sgu_grad.reshape(R, D // R, 2 * fs)).astype(BF)
-    sd_sum = reduce_rep(sd_grad.reshape(R, drow, D))
+    if square:
+        sg_mid = cross(after(sg_near + sg_got[1], *lane_all), 1)
+        sgrad = sg_own.astype(F32) + sg_got[0].astype(F32) + after(sg_mid, dense_rep).astype(F32)
+    else:
+        sgrad = lax.psum_scatter(sgrad.reshape(-1, fs), "rep", scatter_dimension=0, tiled=True).astype(F32)
+    sd_sum = jnp.concatenate(
+        [sgrad[2 * gr + k * drow : 2 * gr + (k + 1) * drow] for k in range(wide)], axis=1
+    )
+    sgu = jnp.concatenate([sgrad[:gr], sgrad[gr : 2 * gr]], axis=1).astype(BF)
+    sgu = after(sgu, dense_rep)
     sgu = lax.all_to_all(sgu.reshape(E, wrow, 2 * fs), "ep", split_axis=0, concat_axis=0, tiled=True)
+
+    sgu = after(sgu, dense)
 
     def units_back(x):
         return x.astype(F32).reshape(E, wrow, R, drow).transpose(1, 2, 0, 3).reshape(wrow, FF)
+
+    sg_sum, su_sum = units_back(sgu[:, :, :fs]), units_back(sgu[:, :, fs:])
+
+    if square:
+        gate_sum = gu_out[0][0].astype(F32) + (gate_a.astype(F32) + after(gate_b, dense_rep).astype(F32))
+        up_sum = gu_out[2][0].astype(F32) + (up_a.astype(F32) + after(up_b, dense_rep).astype(F32))
+    else:
+        gate_sum, up_sum = (direct(x, dense_rep) for x in gu_out)
+    dn_sum = after(dn_sum, dense_rep).T.astype(F32)
+    layer_out = (mid + after(mix_sum, dense_rep).astype(F32)).astype(BF)
+
+    done = [gate_sum, up_sum, dn_sum, layer_out, sd_sum, sg_sum, su_sum]
+    one_parts[0], *done = lax.optimization_barrier((one_parts[0], *done))
+    gate_sum, up_sum, dn_sum, layer_out, sd_sum, sg_sum, su_sum = done
+    tokens_grad = pl.pallas_call(
+        functools.partial(last_kernel, chips),
+        in_specs=vmem(chips + 3),
+        out_specs=vmem(1)[0],
+        out_shape=shape((T, D), F32),
+        compiler_params=params(),
+        name="last",
+        cost_estimate=cost(3),
+    )(*one_parts, tokens, gain1, mid_grad)
 
     return (
         layer_out,
@@ -817,12 +990,12 @@
         mats[3],
         ext[1],
         ext[2:].T,
-        units_back(sgu[:, :, :fs]),
-        units_back(sgu[:, :, fs:]),
+        sg_sum,
+        su_sum,
         sd_sum,
-        gu_sum[0, 0][None].astype(F32),
-        gu_sum[0, 1][None].astype(F32),
-        dn_sum.T[None].astype(F32),
+        gate_sum[None],
+        up_sum[None],
+        dn_sum[None],
     )
 
 

time: 531 us -> 426 us (0.80)
  the two profiles are of different devices: /device:TPU:0 before, /device:TPU:9 now
where the time goes in v2:
time: 426 us; the launch traced here: 418 us
  Pallas kernels  151 us (35%)
  waiting for transfers between devices  88.1 us (21%)
  starting transfers between devices  79 us (19%)
  other arithmetic  46 us (11%)
  local copies, waits for them, and re-layouts  36.8 us (9%)
  between operations  15.2 us (4%)
    ppermute x4, waiting for transfers between devices, line(): lax.ppermute(x, 'ep', [(i, i + 2 * s) for i in range(E) if 0 <= i + 2 * s...  44 us
    pallas_call x1, Pallas kernels, shards(): pl.pallas_call(functools.partial(expert_kernel, E, T, experts), grid=(ste...  40 us
    pallas_call x1, Pallas kernels, shards(): pl.pallas_call(functools.partial(attend_back_kernel, first, count, T), gr...  31 us
    ppermute x12, waiting for transfers between devices, ring(): return lax.ppermute(x, 'ep', [(i, (i + 2 * s) % E) for i in range(E)])  24.4 us
    ppermute x15, starting transfers between devices, swap(): return lax.ppermute(x, 'ep', [(i, i ^ 1) for i in range(E)])  23.3 us
    ppermute x12, starting transfers between devices, ring(): return lax.ppermute(x, 'ep', [(i, (i + 2 * s) % E) for i in range(E)])  21.7 us
    pallas_call x1, Pallas kernels, shards(): pl.pallas_call(functools.partial(result_kernel, E, T), grid=(steps,), in_...  18.4 us
    ppermute x17, waiting for transfers between devices, cross(): return lax.ppermute(x, 'rep', [(i, i ^ s) for i in range(R)])  14.5 us
  transfers between devices with their start and end apart: 53, of which 18 were waited for; matrix products, arithmetic and copies ran while one was open for 18% of the time, Pallas kernels for 26%

profile of v2, /device:TPU:9, one launch (start us, length us, event | category | flops | bytes accessed | tf_op | source)
XLA Modules:
  0.0 417.8 jit_solution(12439499420708803873)
XLA Ops:
  24.6 3.8 collective-permute-start.3
  34.5 4.3 %multiply_sine_fusion = (f32[1536,128]{1,0:T(8,128)}, f32[1536,128]{1,0:T(8,128)}) fusion(f32[128]{0:T(128)S(1)} %mul.48, f32[1536]{0:T(1024)S(1)} %convert_element_type.209), kind=kLoop, calls=%fused_computation.14 | loop fusion | flops 196608 | bytes 1579520 | tf_op jit(solution)/shard_map/sin | solution.py:528
  40.1 5.4 %all-to-all-start = ((bf16[8,24,512]{2,1,0:T(8,128)(2,1)}), bf16[8,24,512]{2,1,0:T(8,128)(2,1)S(1)}, u32[]{:S(2)}, u32[]{:S(2)}) async-start(bf16[8,24,512]{2,1,0:T(8,128)(2,1)} %pad_maximum_fusion.5), calls=%async_computation | async-start | bytes 393216 | tf_op jit(solution)/shard_map/all_to_all | solution.py:562
  47.1 8.1 %collective-permute-done.1.refs_1_ = bf16[264,768]{1,0:T(8,128)(2,1)} collective-permute-done((bf16[264,768]{1,0:T(8,128)(2,1)}, bf16[264,768]{1,0:T(8,128)(2,1)}, u32[]{:S(2)}, u32[]{:S(2)}) %collective-permute-start.1) | collective-permute-done | bytes 405536 | tf_op jit(solution)/shard_map/ppermute | solution.py:455
  58.7 24.3 %collective-permute-done.2.refs_2_ = bf16[264,768]{1,0:T(8,128)(2,1)} collective-permute-done((bf16[264,768]{1,0:T(8,128)(2,1)}, bf16[264,768]{1,0:T(8,128)(2,1)}, u32[]{:S(2)}, u32[]{:S(2)}) %collective-permute-start.2) | collective-permute-done | bytes 405536 | tf_op jit(solution)/shard_map/ppermute | solution.py:455
  89.8 8.0 %qkv.1 = (bf16[6,256,768]{2,1,0:T(8,128)(2,1)}, bf16[3,6,256,128]{3,2,1,0:T(8,128)(2,1)}, bf16[3,6,256,128]{3,2,1,0:T(8,128)(2,1)}, bf16[3,2,256,128]{3,2,1,0:T(8,128)(2,1)}) custom-call(s32[1]{0:T(128)} %bitcast.c_ref, bf16[264,768]{1,0:T(8,128)(2,1)} %fusion.8.refs_0_, bf16[264,768]{1,0:T(8,128)(2,1)} %collective-permute-done.1.refs_1_, ...), custom_call_target="tpu_custom_call" | custom-call | flops 8800000000 | bytes 800000 | tf_op jit(solution)/shard_map/qkv/pallas_call | solution.py:531
  102.1 10.2 %attend.1 = (f32[3,512,128]{2,1,0:T(8,128)}, bf16[3,512,128]{2,1,0:T(8,128)(2,1)}, f32[3,8,512]{2,1,0:T(8,128)}) custom-call(bf16[3,512,128]{2,1,0:T(8,128)(2,1)} %bitcast.263, bf16[3,1536,128]{2,1,0:T(8,128)(2,1)} %bitcast.259, bf16[3,1536,128]{2,1,0:T(8,128)(2,1)} %bitcast.261, f32[512,128]{1,0:T(8,128)} %broadcast_in_dim.96.sq_ref, f32[1,1536]{1,0:T(1,128)} %bitcast.249), custom_call_target="tpu_custom_call" | custom-call | flops 11000000512 | bytes 1000000 | tf_op jit(solution)/shard_map/attend/pallas_call | solution.py:570
  137.8 10.6 %pre.1 = (bf16[1024,2048]{1,0:T(8,128)(2,1)}, bf16[768,1024]{1,0:T(8,128)(2,1)}) custom-call(s32[8]{0:T(128)} %stack.77.ix, bf16[8,264,768]{2,1,0:T(8,128)(2,1)} %bitcast.254, bf16[8,128,256]{2,1,0:T(8,128)(2,1)} %compare_convert_fusion.1.p_ref.refs_8_, bf16[2048,768]{1,0:T(8,128)(2,1)} %bitcast.257), custom_call_target="tpu_custom_call" | custom-call | flops 13200000000 | bytes 1200000 | tf_op jit(solution)/shard_map/pre/pallas_call | solution.py:642
  154.1 6.0 %collective-permute-done.15.refs_2_ = bf16[256,768]{1,0:T(8,128)(2,1)} collective-permute-done((bf16[256,768]{1,0:T(8,128)(2,1)}, bf16[256,768]{1,0:T(8,128)(2,1)}, u32[]{:S(2)}, u32[]{:S(2)}) %collective-permute-start.15) | collective-permute-done | bytes 393248 | tf_op jit(solution)/shard_map/ppermute | solution.py:452
  164.7 40.0 %expert.1 = (bf16[1024,768]{1,0:T(8,128)(2,1)}, bf16[1024,2048]{1,0:T(8,128)(2,1)}, bf16[1024,2048]{1,0:T(8,128)(2,1)}, bf16[1024,2048]{1,0:T(8,128)(2,1)}, f32[...) custom-call(s32[1]{0:T(128)} %bitcast.29.e_ref, ...), custom_call_target="tpu_custom_call" | custom-call | flops 41799999488 | bytes 3800000 | tf_op jit(solution)/shard_map/expert/pallas_call | solution.py:656
  208.1 9.7 %dgrad.1 = bf16[768,2048]{1,0:T(8,128)(2,1)} custom-call(bf16[768,1024]{1,0:T(8,128)(2,1)} %get-tuple-element.144.ogx_t, f32[1024,128]{1,0:T(8,128)} %get-tuple-element.145.gate_slot, bf16[1024,2048]{1,0:T(8,128)(2,1)} %get-tuple-element.159.ehid.refs_15_), custom_call_target="tpu_custom_call" | custom-call | flops 11000000512 | bytes 1000000 | tf_op jit(solution)/shard_map/dgrad/pallas_call | solution.py:726
  225.1 13.6 %wgrad.1 = (bf16[2,768,512]{2,1,0:T(8,128)(2,1)}, bf16[2,768,512]{2,1,0:T(8,128)(2,1)}, bf16[2,768,512]{2,1,0:T(8,128)(2,1)}, bf16[2,768,512]{2,1,0:T(8,128)(2,1)}) custom-call(s32[1]{0:T(128)} %bitcast.55.r_ref, bf16[1024,768]{1,0:T(8,128)(2,1)} %get-tuple-element.149.x_ref, bf16[1024,2048]{1,0:T(8,128)(2,1)} %get-tuple-element.150.degate, ...), custom_call_target="tpu_custom_call" | custom-call | flops 14300000256 | bytes 1300000 | tf_op jit(solution)/shard_map/wgrad/pallas_call | solution.py:767
  244.2 18.4 %result.1 = (bf16[8,256,768]{2,1,0:T(8,128)(2,1)}, bf16[768,512]{1,0:T(8,128)(2,1)}, bf16[256,768]{1,0:T(8,128)(2,1)}) custom-call(s32[8]{0:T(128)} %stack.77.ix, bf16[256,768]{1,0:T(8,128)(2,1)} %get-tuple-element.134.refs_0_, bf16[256,768]{1,0:T(8,128)(2,1)} %copy-done.31, bf16[256,768]{1,0:T(8,128)(2,1)} %collective-permute-done.15.refs_2_, ...), custom_call_target="tpu_custom_call" | custom-call | flops 20899999744 | bytes 1900000 | tf_op jit(solution)/shard_map/result/pallas_call | solution.py:796
  268.4 3.9 mid_back.1
  274.1 4.0 collective-permute-start.30
  292.2 31.0 %attend_back.1 = (bf16[3,768,384]{2,1,0:T(8,128)(2,1)}, bf16[3,256,768]{2,1,0:T(8,128)(2,1)}, bf16[3,256,768]{2,1,0:T(8,128)(2,1)}, f32[8,768]{1,0:T(8,128)}) custom-call(bf16[3,512,128]{2,1,0:T(8,128)(2,1)} %bitcast.264, bf16[3,1536,128]{2,1,0:T(8,128)(2,1)} %bitcast.260, bf16[3,1536,128]{2,1,0:T(8,128)(2,1)} %bitcast.262, ...), custom_call_target="tpu_custom_call" | custom-call | flops 32999999488 | bytes 3000000 | tf_op jit(solution)/shard_map/attend_back/pallas_call | solution.py:862
  335.5 5.7 %collective-permute-start.39 = (bf16[256,768]{1,0:T(8,128)(2,1)}, bf16[256,768]{1,0:T(8,128)(2,1)}, u32[]{:S(2)}, u32[]{:S(2)}) collective-permute-start(bf16[256,768]{1,0:T(8,128)(2,1)} %get-tuple-element.239), channel_id=1, source_target_pairs={{2,0},{3,1},{4,2},{5,3},{6,4},{7,5},{10,8},{11,9},{12,10},{13,11},... | collective-permute-start | bytes 1179656 | tf_op jit(solution)/shard_map/ppermute | solution.py:455
  346.1 3.7 collective-permute-done.39.refs_1_
  349.8 7.8 %collective-permute-done.40.refs_2_ = bf16[256,768]{1,0:T(8,128)(2,1)} collective-permute-done((bf16[256,768]{1,0:T(8,128)(2,1)S(1)}, bf16[256,768]{1,0:T(8,128)(2,1)}, u32[]{:S(2)}, u32[]{:S(2)}) %collective-permute-start.40) | collective-permute-done | bytes 393248 | tf_op jit(solution)/shard_map/ppermute | solution.py:455
  361.9 4.3 %collective-permute-start.44 = (bf16[200,384]{1,0:T(8,128)(2,1)S(1)}, bf16[200,384]{1,0:T(8,128)(2,1)S(1)}, u32[]{:S(2)}, u32[]{:S(2)}) collective-permute-start(bf16[200,384]{1,0:T(8,128)(2,1)S(1)} %get-tuple-element.258), channel_id=1, source_target_pairs={{0,2},{1,3},{2,4},{3,5},{4,6},{5,7},{6,0},{7,1},{8,10},{9,11},{10,... | collective-permute-start | bytes 460808 | tf_op jit(solution)/shard_map/ppermute | solution.py:452
  366.1 4.1 collective-permute-start.45
  371.7 7.4 %collective-permute-done.45 = bf16[200,384]{1,0:T(8,128)(2,1)S(1)} collective-permute-done((bf16[200,384]{1,0:T(8,128)(2,1)S(1)}, bf16[200,384]{1,0:T(8,128)(2,1)S(1)}, u32[]{:S(2)}, u32[]{:S(2)}) %collective-permute-start.45) | collective-permute-done | bytes 153632 | tf_op jit(solution)/shard_map/ppermute | solution.py:452
  379.1 3.7 collective-permute-done.46
  396.1 5.1 %all-to-all-done.1 = bf16[8,24,512]{2,1,0:T(8,128)(2,1)S(1)} async-done(((bf16[8,24,512]{2,1,0:T(8,128)(2,1)}), bf16[8,24,512]{2,1,0:T(8,128)(2,1)S(1)}, u32[]{:S(2)}, u32[]{:S(2)}) %all-to-all-start.1) | async-done | bytes 196640 | tf_op jit(solution)/shard_map/all_to_all | solution.py:953
  (335 shorter events, 159.4 us)
Async XLA Ops:
  7.2 126.9 %all-gather.3.cloned.1.call-start = ((), (), s32[]{:S(2)}) async-start(), calls=%async_computation.6 | async-start | bytes 3649536 | tf_op jit(solution)/shard_map/all_gather | solution.py:553
  20.4 34.8 %collective-permute-start.1 = (bf16[264,768]{1,0:T(8,128)(2,1)}, bf16[264,768]{1,0:T(8,128)(2,1)}, u32[]{:S(2)}, u32[]{:S(2)}) collective-permute-start(bf16[264,768]{1,0:T(8,128)(2,1)} %fusion.8.refs_0_), channel_id=1, source_target_pairs={{0,2},{1,3},{2,4},{3,5},{4,6},{5,7},{8,10},{9,11},{10,12},{11,13},... | collective-permute-start | bytes 1216520 | tf_op jit(solution)/shard_map/ppermute | solution.py:455
  22.5 60.6 %collective-permute-start.2 = (bf16[264,768]{1,0:T(8,128)(2,1)}, bf16[264,768]{1,0:T(8,128)(2,1)}, u32[]{:S(2)}, u32[]{:S(2)}) collective-permute-start(bf16[264,768]{1,0:T(8,128)(2,1)} %fusion.8.refs_0_), channel_id=1, source_target_pairs={{0,4},{1,5},{2,6},{3,7},{8,12},{9,13},{10,14},{11,15},{16,20},{17,... | collective-permute-start | bytes 1216520 | tf_op jit(solution)/shard_map/ppermute | solution.py:455
  33.3 51.8 %collective-permute-start.9 = (bf16[4,208,384]{2,1,0:T(8,128)(2,1)S(1)}, bf16[4,208,384]{2,1,0:T(8,128)(2,1)}, u32[]{:S(2)}, u32[]{:S(2)}) collective-permute-start(bf16[4,208,384]{2,1,0:T(8,128)(2,1)S(1)} %bitcast_dynamic-update-slice_fusion.8), channel_id=1, source_target_pairs={{0,8},{8,0},{16,24},{24,16},{1,9},{9,1},{17,25},{25,17},{2,10},{10... | collective-permute-start | bytes 1916936 | tf_op jit(solution)/shard_map/ppermute | solution.py:458
  38.8 47.5 %collective-permute-start.10 = (bf16[4,208,384]{2,1,0:T(8,128)(2,1)S(1)}, bf16[4,208,384]{2,1,0:T(8,128)(2,1)}, u32[]{:S(2)}, u32[]{:S(2)}) collective-permute-start(bf16[4,208,384]{2,1,0:T(8,128)(2,1)S(1)} %bitcast_dynamic-update-slice_fusion.8), channel_id=1, source_target_pairs={{0,16},{8,24},{16,0},{24,8},{1,17},{9,25},{17,1},{25,9},{2,18},{10... | collective-permute-start | bytes 1916936 | tf_op jit(solution)/shard_map/ppermute | solution.py:458
  40.1 57.7 %all-to-all-start = ((bf16[8,24,512]{2,1,0:T(8,128)(2,1)}), bf16[8,24,512]{2,1,0:T(8,128)(2,1)S(1)}, u32[]{:S(2)}, u32[]{:S(2)}) async-start(bf16[8,24,512]{2,1,0:T(8,128)(2,1)} %pad_maximum_fusion.5), calls=%async_computation | async-start | bytes 393216 | tf_op jit(solution)/shard_map/all_to_all | solution.py:562
  45.6 358.2 %reduce-scatter.3.cloned.1.call-start = ((), (), s32[]{:S(2)}) async-start(), calls=%async_computation.4 | async-start | bytes 3932160 | tf_op jit(solution)/shard_map/reduce_scatter | solution.py:736
  46.1 41.4 %collective-permute-start.11 = (bf16[4,208,384]{2,1,0:T(8,128)(2,1)S(1)}, bf16[4,208,384]{2,1,0:T(8,128)(2,1)S(1)}, u32[]{:S(2)}, u32[]{:S(2)}) collective-permute-start(bf16[4,208,384]{2,1,0:T(8,128)(2,1)S(1)} %bitcast_dynamic-update-slice_fusion.8), channel_id=1, source_target_pairs={{0,24},{8,16},{16,8},{24,0},{1,25},{9,17},{17,9},{25,1},{2,26},{10... | collective-permute-start | bytes 1916936 | tf_op jit(solution)/shard_map/ppermute | solution.py:458
  55.2 34.6 %collective-permute-start.4 = (bf16[264,768]{1,0:T(8,128)(2,1)}, bf16[264,768]{1,0:T(8,128)(2,1)}, u32[]{:S(2)}, u32[]{:S(2)}) collective-permute-start(bf16[264,768]{1,0:T(8,128)(2,1)} %collective-permute-done.1.refs_1_), channel_id=1, source_target_pairs={{0,1},{1,0},{2,3},{3,2},{4,5},{5,4},{6,7},{7,6},{8,9},{9,8},{10,11... | collective-permute-start | bytes 1216520 | tf_op jit(solution)/shard_map/ppermute | solution.py:449
  123.5 24.9 %collective-permute-start.19 = (bf16[256,768]{1,0:T(8,128)(2,1)}, bf16[256,768]{1,0:T(8,128)(2,1)S(1)}, u32[]{:S(2)}, u32[]{:S(2)}) collective-permute-start(bf16[256,768]{1,0:T(8,128)(2,1)} %get-tuple-element.134.refs_0_), channel_id=1, source_target_pairs={{0,6},{1,7},{2,0},{3,1},{4,2},{5,3},{6,4},{7,5},{8,14},{9,15},{10,... | collective-permute-start | bytes 1179656 | tf_op jit(solution)/shard_map/ppermute | solution.py:452
  123.5 28.2 %collective-permute-start.17 = (bf16[256,768]{1,0:T(8,128)(2,1)}, bf16[256,768]{1,0:T(8,128)(2,1)S(1)}, u32[]{:S(2)}, u32[]{:S(2)}) collective-permute-start(bf16[256,768]{1,0:T(8,128)(2,1)} %get-tuple-element.134.refs_0_), channel_id=1, source_target_pairs={{0,4},{1,5},{2,6},{3,7},{4,0},{5,1},{6,2},{7,3},{8,12},{9,13},{10,... | collective-permute-start | bytes 1179656 | tf_op jit(solution)/shard_map/ppermute | solution.py:452
  126.6 33.5 %collective-permute-start.15 = (bf16[256,768]{1,0:T(8,128)(2,1)}, bf16[256,768]{1,0:T(8,128)(2,1)}, u32[]{:S(2)}, u32[]{:S(2)}) collective-permute-start(bf16[256,768]{1,0:T(8,128)(2,1)} %get-tuple-element.134.refs_0_), channel_id=1, source_target_pairs={{0,2},{1,3},{2,4},{3,5},{4,6},{5,7},{6,0},{7,1},{8,10},{9,11},{10,... | collective-permute-start | bytes 1179656 | tf_op jit(solution)/shard_map/ppermute | solution.py:452
  217.9 188.3 %reduce-scatter.5.cloned.1.call-start = ((), (), s32[]{:S(2)}) async-start(), calls=%async_computation.5 | async-start | bytes 3538944 | tf_op jit(solution)/shard_map/reduce_scatter | solution.py:832
  221.7 40.8 %collective-permute-start.29 = (bf16[256,768]{1,0:T(8,128)(2,1)S(1)}, bf16[256,768]{1,0:T(8,128)(2,1)S(1)}, u32[]{:S(2)}, u32[]{:S(2)}) collective-permute-start(bf16[256,768]{1,0:T(8,128)(2,1)S(1)} %get-tuple-element.223), channel_id=1, source_target_pairs={{0,2},{1,3},{2,4},{3,5},{4,6},{5,7},{6,0},{7,1},{8,10},{9,11},{10,... | collective-permute-start | bytes 1179656 | tf_op jit(solution)/shard_map/ppermute | solution.py:452
  223.9 38.7 %collective-permute-start.28 = (bf16[256,768]{1,0:T(8,128)(2,1)S(1)}, bf16[256,768]{1,0:T(8,128)(2,1)S(1)}, u32[]{:S(2)}, u32[]{:S(2)}) collective-permute-start(bf16[256,768]{1,0:T(8,128)(2,1)S(1)} %get-tuple-element.225), channel_id=1, source_target_pairs={{0,6},{1,7},{2,0},{3,1},{4,2},{5,3},{6,4},{7,5},{8,14},{9,15},{10,... | collective-permute-start | bytes 1179656 | tf_op jit(solution)/shard_map/ppermute | solution.py:452
  240.3 27.2 %collective-permute-start.27 = (bf16[768,512]{1,0:T(8,128)(2,1)S(1)}, bf16[768,512]{1,0:T(8,128)(2,1)S(1)}, u32[]{:S(2)}, u32[]{:S(2)}) collective-permute-start(bf16[768,512]{1,0:T(8,128)(2,1)S(1)} %get-tuple-element.235), channel_id=1, source_target_pairs={{0,16},{8,24},{16,0},{24,8},{1,17},{9,25},{17,1},{25,9},{2,18},{10... | collective-permute-start | bytes 2359304 | tf_op jit(solution)/shard_map/ppermute | solution.py:458
  242.8 25.7 %collective-permute-start.25 = (bf16[768,512]{1,0:T(8,128)(2,1)S(1)}, bf16[768,512]{1,0:T(8,128)(2,1)}, u32[]{:S(2)}, u32[]{:S(2)}) collective-permute-start(bf16[768,512]{1,0:T(8,128)(2,1)S(1)} %get-tuple-element.237), channel_id=1, source_target_pairs={{0,8},{8,0},{16,24},{24,16},{1,9},{9,1},{17,25},{25,17},{2,10},{10... | collective-permute-start | bytes 2359304 | tf_op jit(solution)/shard_map/ppermute | solution.py:458
  262.6 23.8 %collective-permute-start.32 = (bf16[768,512]{1,0:T(8,128)(2,1)S(1)}, bf16[768,512]{1,0:T(8,128)(2,1)}, u32[]{:S(2)}, u32[]{:S(2)}) collective-permute-start(bf16[768,512]{1,0:T(8,128)(2,1)S(1)} %get-tuple-element.172), channel_id=1, source_target_pairs={{0,16},{8,24},{16,0},{24,8},{1,17},{9,25},{17,1},{25,9},{2,18},{10... | collective-permute-start | bytes 2359304 | tf_op jit(solution)/shard_map/ppermute | solution.py:458
  280.5 42.7 %collective-permute-start.35 = (bf16[768,384]{1,0:T(8,128)(2,1)}, bf16[768,384]{1,0:T(8,128)(2,1)}, u32[]{:S(2)}, u32[]{:S(2)}) collective-permute-start(bf16[768,384]{1,0:T(8,128)(2,1)} %broadcast_select_fusion), channel_id=1, source_target_pairs={{0,1},{1,0},{2,3},{3,2},{4,5},{5,4},{6,7},{7,6},{8,9},{9,8},{10,11... | collective-permute-start | bytes 1769480 | tf_op jit(solution)/shard_map/ppermute | solution.py:449
  285.0 38.2 %collective-permute-start.36 = (bf16[2,576,256]{2,1,0:T(8,128)(2,1)}, bf16[2,576,256]{2,1,0:T(8,128)(2,1)S(1)}, u32[]{:S(2)}, u32[]{:S(2)}) collective-permute-start(bf16[2,576,256]{2,1,0:T(8,128)(2,1)} %pad_maximum_fusion.2), channel_id=1, source_target_pairs={{0,16},{8,24},{16,0},{24,8},{1,17},{9,25},{17,1},{25,9},{2,18},{10... | collective-permute-start | bytes 1769480 | tf_op jit(solution)/shard_map/ppermute | solution.py:458
  289.0 34.2 %collective-permute-start.34 = (bf16[768,512]{1,0:T(8,128)(2,1)S(1)}, bf16[768,512]{1,0:T(8,128)(2,1)S(1)}, u32[]{:S(2)}, u32[]{:S(2)}) collective-permute-start(bf16[768,512]{1,0:T(8,128)(2,1)S(1)} %bitcast_add_fusion), channel_id=1, source_target_pairs={{0,8},{8,0},{16,24},{24,16},{1,9},{9,1},{17,25},{25,17},{2,10},{10... | collective-permute-start | bytes 2359304 | tf_op jit(solution)/shard_map/ppermute | solution.py:458
  290.7 32.5 %collective-permute-start.33 = (bf16[768,512]{1,0:T(8,128)(2,1)S(1)}, bf16[768,512]{1,0:T(8,128)(2,1)}, u32[]{:S(2)}, u32[]{:S(2)}) collective-permute-start(bf16[768,512]{1,0:T(8,128)(2,1)S(1)} %bitcast_add_fusion.1), channel_id=1, source_target_pairs={{0,16},{8,24},{16,0},{24,8},{1,17},{9,25},{17,1},{25,9},{2,18},{10... | collective-permute-start | bytes 2359304 | tf_op jit(solution)/shard_map/ppermute | solution.py:458
  330.3 27.3 %collective-permute-start.41 = (bf16[4,200,384]{2,1,0:T(8,128)(2,1)}, bf16[4,200,384]{2,1,0:T(8,128)(2,1)}, u32[]{:S(2)}, u32[]{:S(2)}) collective-permute-start(bf16[4,200,384]{2,1,0:T(8,128)(2,1)} %get-tuple-element.233), channel_id=1, source_target_pairs={{0,16},{8,24},{16,0},{24,8},{1,17},{9,25},{17,1},{25,9},{2,18},{10... | collective-permute-start | bytes 1843208 | tf_op jit(solution)/shard_map/ppermute | solution.py:458
  331.5 28.6 %collective-permute-start.42 = (bf16[4,200,384]{2,1,0:T(8,128)(2,1)}, bf16[4,200,384]{2,1,0:T(8,128)(2,1)}, u32[]{:S(2)}, u32[]{:S(2)}) collective-permute-start(bf16[4,200,384]{2,1,0:T(8,128)(2,1)} %get-tuple-element.232), channel_id=1, source_target_pairs={{0,24},{8,16},{16,8},{24,0},{1,25},{9,17},{17,9},{25,1},{2,26},{10... | collective-permute-start | bytes 1843208 | tf_op jit(solution)/shard_map/ppermute | solution.py:458
  (64 other events, 630.6 us)
Sparse Core Ops, SparseCore 0:
  39.0 48.9 all-gather.2
  218.0 54.6 reduce-scatter.2
  281.5 38.0 reduce-scatter.4

commit v3 on v2

--- a/solution.py
+++ b/solution.py
@@ -144,30 +144,23 @@
 
 
 def act(g, u, dh):
-    s = jax.nn.sigmoid(g)
+    s = 0.5 * jnp.tanh(0.5 * g) + 0.5
     silu = g * s
     hid = (silu * u).astype(BF)
-    dg = (dh * u * (s * (1.0 + g * (1.0 - s)))).astype(BF)
+    dg = (dh * u * (s + silu * (1.0 - s))).astype(BF)
     du = (dh * silu).astype(BF)
     return hid, dg, du
-
-
-def split_nn(a, col):
-    wide = jnp.broadcast_to(col, (col.shape[0], 128))
-    high = wide.astype(BF)
-    return nn(a, high) + nn(a, (wide - high.astype(F32)).astype(BF))
 
 
 def expert_kernel(nblk, rows, experts, e_ref, ix, *refs):
     g_refs = refs[:nblk]
     (p_ref, pt_ref, wr, wr_t, wsg, wsu, wsd, og, wg, wu, dehid) = refs[nblk : nblk + 11]
-    (x_out, ehid, degate, deup, gate_slot, gate_tok, shid, dsg, dsu, tg, tg_far, rgrad) = refs[
-        nblk + 11 : nblk + 23
-    ]
-    x_scr, row_scr, tg_scr, pg_scr, prob_scr, gs_scr = refs[nblk + 23 :]
+    (x_out, g_out, ghid, degate, deup, shid, dsg, dsu, tg, tg_far, rgrad) = refs[nblk + 11 : nblk + 22]
+    x_scr, row_scr, tg_scr, pg_scr, prob_scr, g_scr = refs[nblk + 22 :]
     cap = p_ref.shape[1]
+    slots = nblk * cap
     step = pl.program_id(0)
-    own = lanes((rows, 128)) == e_ref[0]
+    per = nblk // pl.num_programs(0)
 
     @pl.when(step == 0)
     def _():
@@ -175,47 +168,45 @@
         pg_scr[...] = jnp.zeros_like(pg_scr)
         for b in range(nblk):
             block = g_refs[b][...]
-            x = nn(p_ref[ix[b]], block).astype(BF)
-            x_scr[b * cap : (b + 1) * cap, :] = x
-            x_out[b * cap : (b + 1) * cap, :] = x
-            logits = jnp.where(lanes((rows, 128)) < experts, nn(block, wr[...]), NEG_LARGE)
-            shifted = jnp.exp(logits - jnp.max(logits, axis=1, keepdims=True))
-            probs = shifted / jnp.sum(shifted, axis=1, keepdims=True)
-            prob_scr[b] = probs
-            gate = jnp.sum(jnp.where(own, probs, 0.0), axis=1, keepdims=True)
-            gate_tok[b] = jnp.broadcast_to(gate, (rows, 128))
-            slot = split_nn(p_ref[ix[b]], gate)
-            gs_scr[b * cap : (b + 1) * cap, :] = slot
-            gate_slot[b * cap : (b + 1) * cap, :] = slot
-            at = b * rows
-            dsh = nt(og[ix[b], 0:rows, :], wsd[...])
-            hid, dg, du = act(nn(block, wsg[...]), nn(block, wsu[...]), dsh)
-            shid[at : at + rows, :] = hid
-            dsg[at : at + rows, :] = dg
-            dsu[at : at + rows, :] = du
-            tg_scr[at : at + rows, :] = nt(dg, wsg[...]) + nt(du, wsu[...])
-
+            g_scr[b * rows : (b + 1) * rows, :] = block
+            x_scr[b * cap : (b + 1) * cap, :] = nn(p_ref[ix[b]], block).astype(BF)
+        logits = jnp.where(lanes((slots, 128)) < experts, nn(x_scr[...], wr[...]), NEG_LARGE)
+        shifted = jnp.exp(logits - jnp.max(logits, axis=1, keepdims=True))
+        prob_scr[...] = shifted / jnp.sum(shifted, axis=1, keepdims=True)
+
+    own = lanes((slots, 128)) == e_ref[0]
+    gate = jnp.sum(jnp.where(own, prob_scr[...], 0.0), axis=1, keepdims=True)
     raw = dehid[...].astype(F32)
-    hid, dg, du = act(nn(x_scr[...], wg[0]), nn(x_scr[...], wu[0]), raw * gs_scr[:, 0:1])
-    ehid[...] = hid
+    hid, dg, du = act(nn(x_scr[...], wg[0]), nn(x_scr[...], wu[0]), raw * gate)
+    hid = hid.astype(F32)
+    ghid[...] = (hid * gate).astype(BF)
     degate[...] = dg
     deup[...] = du
     row_scr[...] += nt(dg, wg[0]) + nt(du, wu[0])
-    pg_scr[...] += jnp.sum(hid.astype(F32) * raw, axis=1, keepdims=True)
+    pg_scr[...] += jnp.sum(hid * raw, axis=1, keepdims=True)
+
+    for k in range(per):
+        b = step * per + k
+        at = pl.multiple_of(b * rows, rows)
+        block = g_scr[pl.ds(at, rows), :]
+        g_out[k * rows : (k + 1) * rows, :] = block
+        dsh = nt(og[ix[b], 0:rows, :], wsd[...])
+        sh, sg, su = act(nn(block, wsg[...]), nn(block, wsu[...]), dsh)
+        here = slice(k * rows, (k + 1) * rows)
+        shid[here, :] = sh
+        dsg[here, :] = sg
+        dsu[here, :] = su
+        tg_scr[pl.ds(at, rows), :] = nt(sg, wsg[...]) + nt(su, wsu[...])
 
     @pl.when(step == pl.num_programs(0) - 1)
     def _():
-        total = jnp.zeros_like(rgrad)
+        x_out[...] = x_scr[...]
+        lgrad = (pg_scr[:, 0:1] * prob_scr[...] * (own.astype(F32) - gate)).astype(BF)
+        rgrad[...] = tn(lgrad, x_scr[...])
+        total = (row_scr[...] + nn(lgrad, wr_t[...])).astype(BF)
         for b in range(nblk):
-            at = b * rows
-            pg = split_nn(pt_ref[ix[b]], pg_scr[b * cap : (b + 1) * cap, 0:1])
-            probs = prob_scr[b]
-            gate = jnp.sum(jnp.where(own, probs, 0.0), axis=1, keepdims=True)
-            lgrad = (pg * probs * (own.astype(F32) - gate)).astype(BF)
-            total += tn(lgrad, g_refs[b][...])
-            back = nn(pt_ref[ix[b]], row_scr[b * cap : (b + 1) * cap, :].astype(BF))
-            (tg_far if b % 2 else tg)[b // 2] = (tg_scr[at : at + rows, :] + back + nn(lgrad, wr_t[...])).astype(BF)
-        rgrad[...] = total
+            back = nn(pt_ref[ix[b]], total[b * cap : (b + 1) * cap, :])
+            (tg_far if b % 2 else tg)[b // 2] = (tg_scr[b * rows : (b + 1) * rows, :] + back).astype(BF)
 
 
 def wgrad_kernel(per, r_ref, x_ref, degate, deup, gate_near, gate_far, up_near, up_far, x_t):
@@ -245,42 +236,39 @@
     up[0] = nn(x_t[...], deup[...]).astype(BF)
 
 
-def down_grad_kernel(ogx_t, gate_slot, ehid, dn):
-    dn[...] = nn(ogx_t[...], (ehid[...].astype(F32) * gate_slot[:, 0:1]).astype(BF)).astype(BF)
-
-
-def result_kernel(nblk, rows, ix, *refs):
-    g_refs = refs[:nblk]
-    og, pt_ref, gate_tok, shid, dsg, dsu, wsd, ehid, wd, mix, sgu, sd, acc = refs[nblk:]
+def down_grad_kernel(ogx_t, ghid, dn):
+    dn[...] = nn(ogx_t[...], ghid[...]).astype(BF)
+
+
+def result_kernel(nblk, rows, ix_s, g_ref, og, pt_ref, shid, dsg, dsu, wsd, ghid, wd, mix, sgu, sd, acc, part, sg_acc, sd_acc):
     cap = pt_ref.shape[2]
     step = pl.program_id(0)
+    per = nblk // pl.num_programs(0)
+    width = dsg.shape[1]
 
     @pl.when(step == 0)
     def _():
         acc[...] = jnp.zeros_like(acc)
-        dg_sum = jnp.zeros((sgu.shape[0], dsg.shape[1]), F32)
-        du_sum = jnp.zeros_like(dg_sum)
-        sd_sum = jnp.zeros(sd.shape, F32)
-        for b in range(nblk):
-            at = b * rows
-            g_t = g_refs[b][...].T
-            dg_sum += nn(g_t, dsg[at : at + rows, :])
-            du_sum += nn(g_t, dsu[at : at + rows, :])
-            sd_sum += tn(shid[at : at + rows, :], og[ix[b], 0:rows, :])
-        width = dsg.shape[1]
-        sgu[:, :width] = dg_sum.astype(BF)
-        sgu[:, width:] = du_sum.astype(BF)
-        sd[...] = sd_sum.astype(BF)
-
-    acc[...] += nn(ehid[...], wd[0])
+        sg_acc[...] = jnp.zeros_like(sg_acc)
+        sd_acc[...] = jnp.zeros_like(sd_acc)
+
+    acc[...] += nn(ghid[...], wd[0])
+    sg_acc[:, :width] += tn(g_ref[...], dsg[...])
+    sg_acc[:, width:] += tn(g_ref[...], dsu[...])
+    for k in range(per):
+        b = step * per + k
+        here = slice(k * rows, (k + 1) * rows)
+        sd_acc[...] += tn(shid[here, :], og[ix_s[b], 0:rows, :])
+        part[pl.ds(pl.multiple_of(b * rows, rows), rows), :] = nn(shid[here, :], wsd[...])
 
     @pl.when(step == pl.num_programs(0) - 1)
     def _():
+        sgu[...] = sg_acc[...].astype(BF)
+        sd[...] = sd_acc[...].astype(BF)
+        res = acc[...].astype(BF)
         for b in range(nblk):
-            at = b * rows
-            res = acc[b * cap : (b + 1) * cap, :].astype(BF)
-            picked = nn(pt_ref[ix[b]], res) * gate_tok[b][:, 0:1]
-            mix[ix[b]] = (picked + nn(shid[at : at + rows, :], wsd[...])).astype(BF)
+            picked = nn(pt_ref[ix_s[b]], res[b * cap : (b + 1) * cap, :])
+            mix[ix_s[b]] = (picked + part[b * rows : (b + 1) * rows, :]).astype(BF)
 
 
 def mid_back_kernel(count, *refs):
@@ -355,9 +343,9 @@
     dkv = dk[...]
     dkb = (dkv * cos[...] - turned(dkv) * sin[...]).astype(BF)
     dvb = dv[...].astype(BF)
-    grads[0] = nn(h1_t[:, base:], dq).astype(BF)
-    grads[1] = nn(h1_t[...], dkb).astype(BF)
-    grads[2] = nn(h1_t[...], dvb).astype(BF)
+    grads[0, 0] = nn(h1_t[:, base:], dq).astype(BF)
+    grads[0, 1] = nn(h1_t[...], dkb).astype(BF)
+    grads[0, 2] = nn(h1_t[...], dvb).astype(BF)
     og_scr[...] += nt(dkb, wk[...]) + nt(dvb, wv[...])
     og_scr[base:, :] += nt(dq, wq[...])
 
@@ -550,7 +538,7 @@
     og_pack = jnp.concatenate(
         [out_grad, jnp.pad(routes.reshape(1, topk * T).astype(BF), ((0, 7), (0, D - topk * T)))], axis=0
     )
-    og_all = lax.all_gather(after(og_pack, pack), "ep", axis=0)
+    og_all = lax.all_gather(after(og_pack, own_tok[-1]), "ep", axis=0)
     ix_arr = jnp.stack([((z - b // 2) % Z) * 2 + (c ^ (b % 2)) for b in range(E)]).astype(jnp.int32)
 
     wo = jnp.concatenate(ordered(wo_half, swap(wo_half)), axis=1)
@@ -638,6 +626,7 @@
     per = FF // R // ft
     col = lambda n: pl.BlockSpec((n, ft), lambda i: (0, i))
     wcol = pl.BlockSpec((1, D, ft), lambda i: (0, 0, i))
+    block_of = lambda n: pl.BlockSpec((E // steps * T, n), lambda i: (i, 0))
     wdn = pl.BlockSpec((1, ft, D), lambda i: (0, i, 0))
     dehid, ogx_t = pl.pallas_call(
         functools.partial(pre_kernel, E, T),
@@ -653,7 +642,7 @@
     )(ix_arr, og_all, pick, expert_down.reshape(FF, D))
 
     h2_blocks = both_cores([after(x, dehid) for x in h2_lane])
-    (x_rows, ehid, degate, deup, gate_slot, gate_tok, shid, dsg, dsu, tg, tg_far, rgrad) = pl.pallas_call(
+    (x_rows, g_rows, ghid, degate, deup, shid, dsg, dsu, tg, tg_far, rgrad) = pl.pallas_call(
         functools.partial(expert_kernel, E, T, experts),
         grid=(steps,),
         in_specs=[smem, smem]
@@ -673,25 +662,23 @@
         ],
         out_specs=(
             whole((slots, D)),
+            block_of(D),
             col(slots),
             col(slots),
             col(slots),
-            whole((slots, 128)),
-            whole((E, T, 128)),
-            whole((E * T, fs)),
-            whole((E * T, fs)),
-            whole((E * T, fs)),
+            block_of(fs),
+            block_of(fs),
+            block_of(fs),
             whole((Z, T, D)),
             whole((Z, T, D)),
             whole((128, D)),
         ),
         out_shape=(
             shape((slots, D)),
+            shape((E * T, D)),
             shape((slots, FF)),
             shape((slots, FF)),
             shape((slots, FF)),
-            shape((slots, 128), F32),
-            shape((E, T, 128), F32),
             shape((E * T, fs)),
             shape((E * T, fs)),
             shape((E * T, fs)),
@@ -704,8 +691,8 @@
             pltpu.VMEM((slots, D), F32),
             pltpu.VMEM((E * T, D), F32),
             pltpu.VMEM((slots, 128), F32),
-            pltpu.VMEM((E, T, 128), F32),
             pltpu.VMEM((slots, 128), F32),
+            pltpu.VMEM((E * T, D), BF),
         ],
         compiler_params=params(),
         name="expert",
@@ -726,13 +713,13 @@
     dn_grad = pl.pallas_call(
         down_grad_kernel,
         grid=(steps,),
-        in_specs=[whole((D, slots)), whole((slots, 128)), col(slots)],
+        in_specs=[whole((D, slots)), col(slots)],
         out_specs=col(D),
         out_shape=shape((D, FF)),
         compiler_params=params(),
         name="dgrad",
         cost_estimate=cost(10),
-    )(ogx_t, gate_slot, ehid)
+    )(ogx_t, ghid)
     dn_sum = lax.psum_scatter(dn_grad, "rep", scatter_dimension=0, tiled=True)
     lane = core_sums(tg, tg_far, dn_grad)
     two_parts = [lane[0]] + [ring(lane[s], -s) for s in range(1, Z)]
@@ -796,26 +783,30 @@
     mix, sgu_grad, sd_grad = pl.pallas_call(
         functools.partial(result_kernel, E, T),
         grid=(steps,),
-        in_specs=[smem]
-        + [whole((T, D))] * E
-        + [
+        in_specs=[
+            smem,
+            block_of(D),
             whole((E, T + 8, D)),
             whole((E, T, cap)),
-            whole((E, T, 128)),
-            whole((E * T, fs)),
-            whole((E * T, fs)),
-            whole((E * T, fs)),
+            block_of(fs),
+            block_of(fs),
+            block_of(fs),
             whole((fs, D)),
             col(slots),
             wdn,
         ],
         out_specs=(whole((E, T, D)), whole((D, 2 * fs)), whole((fs, D))),
         out_shape=(shape((E, T, D)), shape((D, 2 * fs)), shape((fs, D))),
-        scratch_shapes=[pltpu.VMEM((slots, D), F32)],
+        scratch_shapes=[
+            pltpu.VMEM((slots, D), F32),
+            pltpu.VMEM((E * T, D), F32),
+            pltpu.VMEM((D, 2 * fs), F32),
+            pltpu.VMEM((fs, D), F32),
+        ],
         compiler_params=params(),
         name="result",
-        cost_estimate=cost(19),
-    )(ix_arr, *h2_blocks, og_all, pick_t, gate_tok, shid, dsg, dsu, wsd, after(ehid, gu_out[0], *two_parts[2::2], *near), expert_down)
+        cost_estimate=cost(14),
+    )(ix_arr, g_rows, og_all, pick_t, shid, dsg, dsu, wsd, after(ghid, gu_out[0], *two_parts[2::2], *near), expert_down)
 
     sgrad = jnp.concatenate(
         [sgu_grad[:, :fs].reshape(R, gr, fs), sgu_grad[:, fs:].reshape(R, gr, fs)]
@@ -881,12 +872,12 @@
             smem,
         ],
         out_specs=(
-            pl.BlockSpec((3, D, 128), lambda i: (0, 0, i)),
+            pl.BlockSpec((1, 3, D, 128), lambda i: (i, 0, 0, 0)),
             whole((chips, T, D)),
             whole((chips, T, D)),
             whole((8, D)),
         ),
-        out_shape=(shape((3, D, half)), shape((chips, T, D)), shape((chips, T, D)), shape((8, D), F32)),
+        out_shape=(shape((pairs, 3, D, 128)), shape((chips, T, D)), shape((chips, T, D)), shape((8, D), F32)),
         scratch_shapes=[
             pltpu.VMEM((D, kv_rows), BF),
             pltpu.VMEM((128, kv_rows), BF),
@@ -905,18 +896,24 @@
         og1_far, grads, gate_b, up_b, wo_got, sg_got = lax.optimization_barrier(
             (og1_far, grads, gate_b, up_b, wo_got, sg_got)
         )
-    lane = og1 + swap(og1_far)
+    far_got = swap(og1_far)
+    if square:
+        sg_mid = cross(sg_near + sg_got[1], 1)
+        sg_mid, far_got = lax.optimization_barrier((sg_mid, far_got))
+    lane = og1 + far_got
     one_parts = [lane[nb]] + [line(lane[nb - s], -s) for s in range(1, chips)]
-    lane_all = one_parts[1:]
-
-    def reduce_z(x):
-        total = lax.dynamic_index_in_dim(x, z, 0, keepdims=False).astype(F32)
-        for s in range(1, Z):
-            total += ring(lax.dynamic_index_in_dim(x, (z + s) % Z, 0, keepdims=False), s).astype(F32)
-        return total
+
+    n_chip = R * Z
+
+    def dense_pack(groups, ext):
+        rows = groups.reshape(-1, n_chip, hrow, 128).transpose(1, 0, 2, 3).reshape(n_chip, -1, 128)
+        ext = ext.astype(BF)
+        ext = jnp.pad(ext, ((0, 0), (0, -ext.shape[1] % 128))).reshape(n_chip, -1, 128)
+        rows = jnp.concatenate([rows, ext], axis=1)
+        return jnp.pad(rows, ((0, 0), (0, -rows.shape[1] % 8), (0, 0))).reshape(R, Z, -1, 128)
 
     wo_lane = wo_mine + wo_got
-    n_chip = R * Z
+    wo_groups = wo_lane.reshape(D, pairs, 128).transpose(1, 0, 2)
     ext = jnp.concatenate(
         [
             gain1_part[0].reshape(n_chip, hrow),
@@ -924,52 +921,40 @@
             rgrad[:experts].reshape(experts, n_chip, hrow).transpose(1, 0, 2).reshape(n_chip, experts * hrow),
         ],
         axis=1,
-    ).astype(BF)
-    ext = jnp.pad(ext, ((0, 0), (0, -ext.shape[1] % half))).reshape(n_chip, -1, half)
-    dense = jnp.concatenate([grads, wo_lane[None]]).reshape(4, n_chip, hrow, half).transpose(1, 0, 2, 3)
-    dense = jnp.concatenate([dense.reshape(n_chip, 4 * hrow, half), ext], axis=1)
-    dense = jnp.pad(dense, ((0, 0), (0, -dense.shape[1] % 8), (0, 0)))
-    dense_rep = direct(pieces(dense.reshape((R, Z) + dense.shape[1:])), *lane_all).astype(BF)
-    dense = reduce_z(dense_rep)
-    mats = dense[: 4 * hrow].reshape(4, 2, wrow, half)
-    mats_mine, mats_other = ordered(mats[:, 0], mats[:, 1])
-    ext = dense[4 * hrow :]
-    got = swap(jnp.concatenate([mats_other.reshape(4 * wrow, half), ext], axis=0).astype(BF)).astype(F32)
-    left, right = ordered(mats_mine, got[: 4 * wrow].reshape(4, wrow, half))
-    mats = jnp.concatenate([left, right], axis=2)
-    ext = (ext + got[4 * wrow :]).reshape(-1)[: (2 + experts) * hrow].reshape(2 + experts, 2, wrow)
-    ext = jnp.where(is0, ext[:, 0], ext[:, 1])
-
+    )
+
+    groups = 4 * pairs
+    pack_d = dense_pack(jnp.concatenate([grads.reshape(-1, D, 128), wo_groups]), ext)
+    send_d = pieces(pack_d)
+    got_d = [after(cross(send_d[s], s), *one_parts[1:]) for s in range(1, R)]
+    total_d = send_d[0].astype(F32)
+    for x in got_d:
+        total_d += x.astype(F32)
+    total_d = total_d.astype(BF)
     if square:
-        sg_mid = cross(after(sg_near + sg_got[1], *lane_all), 1)
-        sgrad = sg_own.astype(F32) + sg_got[0].astype(F32) + after(sg_mid, dense_rep).astype(F32)
+        sgrad = sg_own.astype(F32) + sg_got[0].astype(F32) + sg_mid.astype(F32)
     else:
         sgrad = lax.psum_scatter(sgrad.reshape(-1, fs), "rep", scatter_dimension=0, tiled=True).astype(F32)
     sd_sum = jnp.concatenate(
         [sgrad[2 * gr + k * drow : 2 * gr + (k + 1) * drow] for k in range(wide)], axis=1
     )
     sgu = jnp.concatenate([sgrad[:gr], sgrad[gr : 2 * gr]], axis=1).astype(BF)
-    sgu = after(sgu, dense_rep)
-    sgu = lax.all_to_all(sgu.reshape(E, wrow, 2 * fs), "ep", split_axis=0, concat_axis=0, tiled=True)
-
-    sgu = after(sgu, dense)
-
-    def units_back(x):
-        return x.astype(F32).reshape(E, wrow, R, drow).transpose(1, 2, 0, 3).reshape(wrow, FF)
-
-    sg_sum, su_sum = units_back(sgu[:, :, :fs]), units_back(sgu[:, :, fs:])
+    sgu = sgu.reshape(Z, hrow, -1, 128).transpose(0, 2, 1, 3).reshape(Z, -1, 128)
+    rows_d = total_d.shape[1]
+    to_z = jnp.concatenate([total_d, sgu], axis=1)
+    z_own = lax.dynamic_index_in_dim(to_z, z, 0, keepdims=False)
+    z_got = [ring(lax.dynamic_index_in_dim(to_z, (z + s) % Z, 0, keepdims=False), s) for s in range(1, Z)]
 
     if square:
-        gate_sum = gu_out[0][0].astype(F32) + (gate_a.astype(F32) + after(gate_b, dense_rep).astype(F32))
-        up_sum = gu_out[2][0].astype(F32) + (up_a.astype(F32) + after(up_b, dense_rep).astype(F32))
+        gate_sum = gu_out[0][0].astype(F32) + (gate_a.astype(F32) + after(gate_b, lane).astype(F32))
+        up_sum = gu_out[2][0].astype(F32) + (up_a.astype(F32) + after(up_b, lane).astype(F32))
     else:
-        gate_sum, up_sum = (direct(x, dense_rep) for x in gu_out)
-    dn_sum = after(dn_sum, dense_rep).T.astype(F32)
-    layer_out = (mid + after(mix_sum, dense_rep).astype(F32)).astype(BF)
-
-    done = [gate_sum, up_sum, dn_sum, layer_out, sd_sum, sg_sum, su_sum]
+        gate_sum, up_sum = (direct(x, lane) for x in gu_out)
+    dn_sum = after(dn_sum, lane).T.astype(F32)
+    layer_out = (mid + after(mix_sum, lane).astype(F32)).astype(BF)
+    done = [gate_sum, up_sum, dn_sum, layer_out, sd_sum, to_z]
     one_parts[0], *done = lax.optimization_barrier((one_parts[0], *done))
-    gate_sum, up_sum, dn_sum, layer_out, sd_sum, sg_sum, su_sum = done
+    gate_sum, up_sum, dn_sum, layer_out, sd_sum, to_z = done
     tokens_grad = pl.pallas_call(
         functools.partial(last_kernel, chips),
         in_specs=vmem(chips + 3),
@@ -980,16 +965,50 @@
         cost_estimate=cost(3),
     )(*one_parts, tokens, gain1, mid_grad)
 
+    z_got = [after(x, tokens_grad) for x in z_got]
+    total = z_own[:rows_d].astype(F32)
+    for x in z_got:
+        total += x[:rows_d].astype(F32)
+    sg_from = put(jnp.zeros((Z,) + sgu.shape[1:], BF), z_own[rows_d:], z)
+    for s in range(1, Z):
+        sg_from = put(sg_from, z_got[s - 1][rows_d:], (z - s) % Z)
+    sg_groups = Z * (2 * fs // 128)
+    mats_all, ext_all = total[: groups * hrow], total[groups * hrow :]
+    rows_all = jnp.concatenate([mats_all, sg_from.reshape(-1, 128).astype(F32)])
+    rows_all = rows_all.reshape(groups + sg_groups, 2, wrow, 128)
+    mine, other = ordered(rows_all[:, 0], rows_all[:, 1])
+    got = swap(jnp.concatenate([other.reshape(-1, 128), ext_all], axis=0).astype(BF)).astype(F32)
+    count_rows = (groups + sg_groups) * wrow
+    left, right = ordered(mine, got[:count_rows].reshape(-1, wrow, 128))
+    ext_all = ext_all + got[count_rows:]
+    ext_all = ext_all.reshape(-1)[: (2 + experts) * hrow].reshape(2 + experts, 2, wrow)
+    ext_all = jnp.where(is0, ext_all[:, 0], ext_all[:, 1])
+
+    def joined_mat(indices):
+        return jnp.concatenate([left[i] for i in indices] + [right[i] for i in indices], axis=1)
+
+    mats = [joined_mat([3 * p + m for p in range(pairs)]) for m in range(3)]
+    mats.append(joined_mat([3 * pairs + p for p in range(pairs)]))
+
+    sg = jnp.stack([left[groups:].reshape(Z, -1, wrow, 128), right[groups:].reshape(Z, -1, wrow, 128)], axis=1)
+    sg = sg.reshape(E, 2, fs // 128, wrow, 128)
+
+    def units_back(x):
+        x = x.transpose(0, 2, 1, 3).reshape(E, wrow, R, drow)
+        return x.transpose(1, 2, 0, 3).reshape(wrow, FF)
+
+    sg_sum, su_sum = units_back(sg[:, 0]), units_back(sg[:, 1])
+
     return (
         layer_out,
         tokens_grad,
-        ext[0],
+        ext_all[0],
         mats[0],
         mats[1],
         mats[2],
         mats[3],
-        ext[1],
-        ext[2:].T,
+        ext_all[1],
+        ext_all[2:].T,
         sg_sum,
         su_sum,
         sd_sum,

time: 426 us -> 384 us (0.901)
  waiting for transfers between devices: 88.1 us -> 61.3 us
  Pallas kernels: 151 us -> 141 us
  starting transfers between devices: 79 us -> 72.5 us
    ppermute x4, waiting for transfers between devices: 44 us -> 21.5 us  [line(): lax.ppermute(x, 'ep', [(i, i + 2 * s) for i in range(E) if 0 <= i + 2 * s...]
    pallas_call x1, Pallas kernels: 40 us -> 32.4 us  [shards(): pl.pallas_call(functools.partial(expert_kernel, E, T, experts), grid=(ste...]
    ppermute x12, waiting for transfers between devices: 24.4 us -> 17.8 us  [ring(): return lax.ppermute(x, 'ep', [(i, (i + 2 * s) % E) for i in range(E)])]
    ppermute x17, waiting for transfers between devices: 14.5 us -> 20.8 us  [cross(): return lax.ppermute(x, 'rep', [(i, i ^ s) for i in range(R)])]
    all_to_all x1 -> x0, waiting for transfers between devices: 5.13 us -> none  [shards(): lax.all_to_all(sgu.reshape(E, wrow, 2 * fs), 'ep', split_axis=0, concat_a...]
  transfers between devices with their start and end apart: 53 -> 52, of which waited for: 18 -> 17; matrix products, arithmetic and copies ran while one was open for 18% -> 20% of each run, Pallas kernels for 26% -> 29%
where the time goes in v3:
time: 384 us; the launch traced here: 378 us
  Pallas kernels  141 us (37%)
  starting transfers between devices  72.5 us (19%)
  waiting for transfers between devices  61.3 us (16%)
  other arithmetic  48 us (12%)
  local copies, waits for them, and re-layouts  39 us (10%)
  between operations  15.2 us (4%)
    pallas_call x1, Pallas kernels, shards(): pl.pallas_call(functools.partial(expert_kernel, E, T, experts), grid=(ste...  32.4 us
    pallas_call x1, Pallas kernels, shards(): pl.pallas_call(functools.partial(attend_back_kernel, first, count, T), gr...  30.9 us
    ppermute x15, starting transfers between devices, swap(): return lax.ppermute(x, 'ep', [(i, i ^ 1) for i in range(E)])  22.4 us
    ppermute x4, waiting for transfers between devices, line(): lax.ppermute(x, 'ep', [(i, i + 2 * s) for i in range(E) if 0 <= i + 2 * s...  21.5 us
    ppermute x17, waiting for transfers between devices, cross(): return lax.ppermute(x, 'rep', [(i, i ^ s) for i in range(R)])  20.8 us
    ppermute x12, starting transfers between devices, ring(): return lax.ppermute(x, 'ep', [(i, (i + 2 * s) % E) for i in range(E)])  20.5 us
    ppermute x12, waiting for transfers between devices, ring(): return lax.ppermute(x, 'ep', [(i, (i + 2 * s) % E) for i in range(E)])  17.8 us
    pallas_call x1, Pallas kernels, shards(): pl.pallas_call(functools.partial(result_kernel, E, T), grid=(steps,), in_...  16.3 us
  transfers between devices with their start and end apart: 52, of which 17 were waited for; matrix products, arithmetic and copies ran while one was open for 20% of the time, Pallas kernels for 29%

profile of v3, /device:TPU:9, one launch (start us, length us, event | category | flops | bytes accessed | tf_op | source)
XLA Modules:
  0.0 378.1 jit_solution(16605922696266902246)
XLA Ops:
  34.5 4.3 %multiply_sine_fusion = (f32[1536,128]{1,0:T(8,128)}, f32[1536,128]{1,0:T(8,128)}) fusion(f32[128]{0:T(128)S(1)} %mul.48, f32[1536]{0:T(1024)S(1)} %convert_element_type.217), kind=kLoop, calls=%fused_computation.19 | loop fusion | flops 196608 | bytes 1579520 | tf_op jit(solution)/shard_map/sin | solution.py:516
  40.0 5.4 %all-to-all-start = ((bf16[8,24,512]{2,1,0:T(8,128)(2,1)}), bf16[8,24,512]{2,1,0:T(8,128)(2,1)S(1)}, u32[]{:S(2)}, u32[]{:S(2)}) async-start(bf16[8,24,512]{2,1,0:T(8,128)(2,1)} %pad_maximum_fusion.8), calls=%async_computation | async-start | bytes 393216 | tf_op jit(solution)/shard_map/all_to_all | solution.py:550
  46.7 12.6 %collective-permute-done.2.refs_2_ = bf16[264,768]{1,0:T(8,128)(2,1)} collective-permute-done((bf16[264,768]{1,0:T(8,128)(2,1)}, bf16[264,768]{1,0:T(8,128)(2,1)}, u32[]{:S(2)}, u32[]{:S(2)}) %collective-permute-start.2) | collective-permute-done | bytes 405536 | tf_op jit(solution)/shard_map/ppermute | solution.py:443
  62.1 5.7 %collective-permute-done.10 = bf16[4,208,384]{2,1,0:T(8,128)(2,1)} collective-permute-done((bf16[4,208,384]{2,1,0:T(8,128)(2,1)S(1)}, bf16[4,208,384]{2,1,0:T(8,128)(2,1)}, u32[]{:S(2)}, u32[]{:S(2)}) %collective-permute-start.10) | collective-permute-done | bytes 639008 | tf_op jit(solution)/shard_map/ppermute | solution.py:446
  74.0 8.1 %qkv.1 = (bf16[6,256,768]{2,1,0:T(8,128)(2,1)}, bf16[3,6,256,128]{3,2,1,0:T(8,128)(2,1)}, bf16[3,6,256,128]{3,2,1,0:T(8,128)(2,1)}, bf16[3,2,256,128]{3,2,1,0:T(8,128)(2,1)}) custom-call(s32[1]{0:T(128)} %bitcast.c_ref, bf16[264,768]{1,0:T(8,128)(2,1)} %fusion.8.refs_0_, bf16[264,768]{1,0:T(8,128)(2,1)} %collective-permute-done.1.refs_1_, ...), custom_call_target="tpu_custom_call" | custom-call | flops 8800000000 | bytes 800000 | tf_op jit(solution)/shard_map/qkv/pallas_call | solution.py:519
  86.4 10.2 %attend.1 = (f32[3,512,128]{2,1,0:T(8,128)}, bf16[3,512,128]{2,1,0:T(8,128)(2,1)}, f32[3,8,512]{2,1,0:T(8,128)}) custom-call(bf16[3,512,128]{2,1,0:T(8,128)(2,1)} %bitcast.383, bf16[3,1536,128]{2,1,0:T(8,128)(2,1)} %bitcast.379, bf16[3,1536,128]{2,1,0:T(8,128)(2,1)} %bitcast.381, f32[512,128]{1,0:T(8,128)} %broadcast_in_dim.109.sq_ref, f32[1,1536]{1,0:T(1,128)} %bitcast.369), custom_call_target="tpu_custom_call" | custom-call | flops 11000000512 | bytes 1000000 | tf_op jit(solution)/shard_map/attend/pallas_call | solution.py:558
  110.6 5.9 %collective-permute-done.22 = bf16[576,256]{1,0:T(8,128)(2,1)S(1)} collective-permute-done((bf16[576,256]{1,0:T(8,128)(2,1)S(1)}, bf16[576,256]{1,0:T(8,128)(2,1)S(1)}, u32[]{:S(2)}, u32[]{:S(2)}) %collective-permute-start.22) | collective-permute-done | bytes 294944 | tf_op jit(solution)/shard_map/ppermute | solution.py:446
  121.4 10.6 %pre.1 = (bf16[1024,2048]{1,0:T(8,128)(2,1)}, bf16[768,1024]{1,0:T(8,128)(2,1)}) custom-call(s32[8]{0:T(128)} %stack.80.ix.ix_s, bf16[8,264,768]{2,1,0:T(8,128)(2,1)} %bitcast.374, bf16[8,128,256]{2,1,0:T(8,128)(2,1)} %compare_convert_fusion.1.p_ref.refs_8_, bf16[2048,768]{1,0:T(8,128)(2,1)} %bitcast.377), custom_call_target="tpu_custom_call" | custom-call | flops 13200000000 | bytes 1200000 | tf_op jit(solution)/shard_map/pre/pallas_call | solution.py:631
  131.9 5.6 %collective-permute-start.20 = (bf16[256,768]{1,0:T(8,128)(2,1)S(1)}, bf16[256,768]{1,0:T(8,128)(2,1)S(1)}, u32[]{:S(2)}, u32[]{:S(2)}) collective-permute-start(bf16[256,768]{1,0:T(8,128)(2,1)S(1)} %collective-permute-done.19.refs_6_), channel_id=1, source_target_pairs={{0,1},{1,0},{2,3},{3,2},{4,5},{5,4},{6,7},{7,6},{8,9},{9,8},{10,11... | collective-permute-start | bytes 1179656 | tf_op jit(solution)/shard_map/ppermute | solution.py:437
  137.7 3.8 %collective-permute-done.15.refs_2_ = bf16[256,768]{1,0:T(8,128)(2,1)} collective-permute-done((bf16[256,768]{1,0:T(8,128)(2,1)}, bf16[256,768]{1,0:T(8,128)(2,1)}, u32[]{:S(2)}, u32[]{:S(2)}) %collective-permute-start.15) | collective-permute-done | bytes 393248 | tf_op jit(solution)/shard_map/ppermute | solution.py:440
  146.1 32.4 %expert.1 = (bf16[1024,768]{1,0:T(8,128)(2,1)}, bf16[2048,768]{1,0:T(8,128)(2,1)}, bf16[1024,2048]{1,0:T(8,128)(2,1)}, bf16[1024,2048]{1,0:T(8,128)(2,1)}, bf16[...) custom-call(s32[1]{0:T(128)} %bitcast.29.e_ref, ...), custom_call_target="tpu_custom_call" | custom-call | flops 41799999488 | bytes 3800000 | tf_op jit(solution)/shard_map/expert/pallas_call | solution.py:645
  179.1 9.0 %dgrad.1 = bf16[768,2048]{1,0:T(8,128)(2,1)} custom-call(bf16[768,1024]{1,0:T(8,128)(2,1)} %get-tuple-element.142.ogx_t, bf16[1024,2048]{1,0:T(8,128)(2,1)} %get-tuple-element.156.ghid), custom_call_target="tpu_custom_call" | custom-call | flops 11000000512 | bytes 1000000 | tf_op jit(solution)/shard_map/dgrad/pallas_call | solution.py:713
  193.4 3.9 %collective-permute-start.29 = (bf16[256,768]{1,0:T(8,128)(2,1)S(1)}, bf16[256,768]{1,0:T(8,128)(2,1)S(1)}, u32[]{:S(2)}, u32[]{:S(2)}) collective-permute-start(bf16[256,768]{1,0:T(8,128)(2,1)S(1)} %get-tuple-element.219), channel_id=1, source_target_pairs={{0,2},{1,3},{2,4},{3,5},{4,6},{5,7},{6,0},{7,1},{8,10},{9,11},{10,... | collective-permute-start | bytes 1179656 | tf_op jit(solution)/shard_map/ppermute | solution.py:440
  197.8 13.4 %wgrad.1 = (bf16[2,768,512]{2,1,0:T(8,128)(2,1)}, bf16[2,768,512]{2,1,0:T(8,128)(2,1)}, bf16[2,768,512]{2,1,0:T(8,128)(2,1)}, bf16[2,768,512]{2,1,0:T(8,128)(2,1)}) custom-call(s32[1]{0:T(128)} %bitcast.55.r_ref, bf16[1024,768]{1,0:T(8,128)(2,1)} %get-tuple-element.146.x_ref, bf16[1024,2048]{1,0:T(8,128)(2,1)} %get-tuple-element.147.degate, ...), custom_call_target="tpu_custom_call" | custom-call | flops 14300000256 | bytes 1300000 | tf_op jit(solution)/shard_map/wgrad/pallas_call | solution.py:754
  215.1 16.3 %result.1 = (bf16[8,256,768]{2,1,0:T(8,128)(2,1)}, bf16[768,512]{1,0:T(8,128)(2,1)}, bf16[256,768]{1,0:T(8,128)(2,1)}) custom-call(s32[8]{0:T(128)} %stack.80.ix.ix_s, bf16[2048,768]{1,0:T(8,128)(2,1)} %get-tuple-element.150.g_ref, bf16[8,264,768]{2,1,0:T(8,128)(2,1)} %bitcast.376, bf16[8,256,128]{2,1,0:T(8,128)(2,1)} %compare_convert_fusion.refs_9_.pt_ref, ...), custom_call_target="tpu_custom_call" | custom-call | flops 15399999488 | bytes 1400000 | tf_op jit(solution)/shard_map/result/pallas_call | solution.py:783
  234.7 4.9 %collective-permute-done.27 = bf16[768,512]{1,0:T(8,128)(2,1)S(1)} collective-permute-done((bf16[768,512]{1,0:T(8,128)(2,1)S(1)}, bf16[768,512]{1,0:T(8,128)(2,1)S(1)}, u32[]{:S(2)}, u32[]{:S(2)}) %collective-permute-start.27) | collective-permute-done | bytes 786464 | tf_op jit(solution)/shard_map/ppermute | solution.py:446
  241.6 3.9 %mid_back.1 = (f32[256,768]{1,0:T(8,128)}, bf16[256,768]{1,0:T(8,128)(2,1)}, bf16[6,256,128]{2,1,0:T(8,128)(2,1)}, f32[8,768]{1,0:T(8,128)}) custom-call(bf16[256,768]{1,0:T(8,128)(2,1)} %get-tuple-element.161.refs_0_, bf16[256,768]{1,0:T(8,128)(2,1)} %copy-done.26, bf16[256,768]{1,0:T(8,128)(2,1)} %copy-done.24, bf16[256,768]{1,0:T(8,128)(2,1)} %copy-done.25, ...), custom_call_target="tpu_custom_call" | custom-call | flops 4400000000 | bytes 400000 | tf_op jit(solution)/shard_map/mid_back/pallas_call | solution.py:825
  263.7 30.9 %attend_back.1 = (bf16[3,3,768,128]{3,2,1,0:T(8,128)(2,1)}, bf16[3,256,768]{2,1,0:T(8,128)(2,1)}, bf16[3,256,768]{2,1,0:T(8,128)(2,1)}, f32[8,768]{1,0:T(8,128)}) custom-call(bf16[3,512,128]{2,1,0:T(8,128)(2,1)} %bitcast.384, bf16[3,1536,128]{2,1,0:T(8,128)(2,1)} %bitcast.380, bf16[3,1536,128]{2,1,0:T(8,128)(2,1)} %bitcast.382, ...), custom_call_target="tpu_custom_call" | custom-call | flops 32999999488 | bytes 3000000 | tf_op jit(solution)/shard_map/attend_back/pallas_call | solution.py:853
  313.2 4.7 %collective-permute-start.40 = (bf16[256,768]{1,0:T(8,128)(2,1)}, bf16[256,768]{1,0:T(8,128)(2,1)S(1)}, u32[]{:S(2)}, u32[]{:S(2)}) collective-permute-start(bf16[256,768]{1,0:T(8,128)(2,1)} %get-tuple-element.235), channel_id=1, source_target_pairs={{2,0},{3,1},{4,2},{5,3},{6,4},{7,5},{10,8},{11,9},{12,10},{13,11},... | collective-permute-start | bytes 1179656 | tf_op jit(solution)/shard_map/ppermute | solution.py:443
  320.9 4.6 %convert_add_fusion = (f32[768,512]{1,0:T(8,128)}, f32[768,512]{1,0:T(8,128)}) fusion(bf16[768,512]{1,0:T(8,128)(2,1)} %collective-permute-done.34, bf16[768,512]{1,0:T(8,128)(2,1)} %copy-done.9, bf16[2,768,512]{2,1,0:T(8,128)(2,1)} %get-tuple-element.168, bf16[768,512]{1,0:T(8,128)(2,1)} %collective-permute-done.33, ...), kind=kLoop, calls=%fused_computation.10 | loop fusion | flops 3932160 | bytes 7864320 | tf_op jit(solution)/shard_map/add | solution.py:950
  326.2 8.3 %collective-permute-done.41.refs_2_ = bf16[256,768]{1,0:T(8,128)(2,1)S(1)} collective-permute-done((bf16[256,768]{1,0:T(8,128)(2,1)}, bf16[256,768]{1,0:T(8,128)(2,1)S(1)}, u32[]{:S(2)}, u32[]{:S(2)}) %collective-permute-start.41) | collective-permute-done | bytes 393248 | tf_op jit(solution)/shard_map/ppermute | solution.py:443
  336.5 6.3 %collective-permute-start.44 = (bf16[776,128]{1,0:T(8,128)(2,1)S(1)}, bf16[776,128]{1,0:T(8,128)(2,1)S(1)}, u32[]{:S(2)}, u32[]{:S(2)}) collective-permute-start(bf16[776,128]{1,0:T(8,128)(2,1)S(1)} %get-tuple-element.254), channel_id=1, source_target_pairs={{0,2},{1,3},{2,4},{3,5},{4,6},{5,7},{6,0},{7,1},{8,10},{9,11},{10,... | collective-permute-start | bytes 595976 | tf_op jit(solution)/shard_map/ppermute | solution.py:440
  342.8 3.9 %collective-permute-start.45 = (bf16[776,128]{1,0:T(8,128)(2,1)S(1)}, bf16[776,128]{1,0:T(8,128)(2,1)S(1)}, u32[]{:S(2)}, u32[]{:S(2)}) collective-permute-start(bf16[776,128]{1,0:T(8,128)(2,1)S(1)} %get-tuple-element.255), channel_id=1, source_target_pairs={{0,4},{1,5},{2,6},{3,7},{4,0},{5,1},{6,2},{7,3},{8,12},{9,13},{10,... | collective-permute-start | bytes 595976 | tf_op jit(solution)/shard_map/ppermute | solution.py:440
  354.0 5.9 %collective-permute-done.45 = bf16[776,128]{1,0:T(8,128)(2,1)S(1)} collective-permute-done((bf16[776,128]{1,0:T(8,128)(2,1)S(1)}, bf16[776,128]{1,0:T(8,128)(2,1)S(1)}, u32[]{:S(2)}, u32[]{:S(2)}) %collective-permute-start.45) | collective-permute-done | bytes 198688 | tf_op jit(solution)/shard_map/ppermute | solution.py:440
  (352 shorter events, 142.4 us)
Async XLA Ops:
  20.4 40.4 %collective-permute-start.1 = (bf16[264,768]{1,0:T(8,128)(2,1)}, bf16[264,768]{1,0:T(8,128)(2,1)}, u32[]{:S(2)}, u32[]{:S(2)}) collective-permute-start(bf16[264,768]{1,0:T(8,128)(2,1)} %fusion.8.refs_0_), channel_id=1, source_target_pairs={{0,2},{1,3},{2,4},{3,5},{4,6},{5,7},{8,10},{9,11},{10,12},{11,13},... | collective-permute-start | bytes 1216520 | tf_op jit(solution)/shard_map/ppermute | solution.py:443
  22.5 36.8 %collective-permute-start.2 = (bf16[264,768]{1,0:T(8,128)(2,1)}, bf16[264,768]{1,0:T(8,128)(2,1)}, u32[]{:S(2)}, u32[]{:S(2)}) collective-permute-start(bf16[264,768]{1,0:T(8,128)(2,1)} %fusion.8.refs_0_), channel_id=1, source_target_pairs={{0,4},{1,5},{2,6},{3,7},{8,12},{9,13},{10,14},{11,15},{16,20},{17,... | collective-permute-start | bytes 1216520 | tf_op jit(solution)/shard_map/ppermute | solution.py:443
  33.2 27.8 %collective-permute-start.9 = (bf16[4,208,384]{2,1,0:T(8,128)(2,1)S(1)}, bf16[4,208,384]{2,1,0:T(8,128)(2,1)}, u32[]{:S(2)}, u32[]{:S(2)}) collective-permute-start(bf16[4,208,384]{2,1,0:T(8,128)(2,1)S(1)} %bitcast_dynamic-update-slice_fusion.8), channel_id=1, source_target_pairs={{0,8},{8,0},{16,24},{24,16},{1,9},{9,1},{17,25},{25,17},{2,10},{10... | collective-permute-start | bytes 1916936 | tf_op jit(solution)/shard_map/ppermute | solution.py:446
  38.7 29.1 %collective-permute-start.10 = (bf16[4,208,384]{2,1,0:T(8,128)(2,1)S(1)}, bf16[4,208,384]{2,1,0:T(8,128)(2,1)}, u32[]{:S(2)}, u32[]{:S(2)}) collective-permute-start(bf16[4,208,384]{2,1,0:T(8,128)(2,1)S(1)} %bitcast_dynamic-update-slice_fusion.8), channel_id=1, source_target_pairs={{0,16},{8,24},{16,0},{24,8},{1,17},{9,25},{17,1},{25,9},{2,18},{10... | collective-permute-start | bytes 1916936 | tf_op jit(solution)/shard_map/ppermute | solution.py:446
  40.0 42.2 %all-to-all-start = ((bf16[8,24,512]{2,1,0:T(8,128)(2,1)}), bf16[8,24,512]{2,1,0:T(8,128)(2,1)S(1)}, u32[]{:S(2)}, u32[]{:S(2)}) async-start(bf16[8,24,512]{2,1,0:T(8,128)(2,1)} %pad_maximum_fusion.8), calls=%async_computation | async-start | bytes 393216 | tf_op jit(solution)/shard_map/all_to_all | solution.py:550
  45.4 72.3 %all-gather.3.cloned.1.call-start = ((), (), s32[]{:S(2)}) async-start(), calls=%async_computation.5 | async-start | bytes 3649536 | tf_op jit(solution)/shard_map/all_gather | solution.py:541
  45.7 23.3 %collective-permute-start.11 = (bf16[4,208,384]{2,1,0:T(8,128)(2,1)S(1)}, bf16[4,208,384]{2,1,0:T(8,128)(2,1)}, u32[]{:S(2)}, u32[]{:S(2)}) collective-permute-start(bf16[4,208,384]{2,1,0:T(8,128)(2,1)S(1)} %bitcast_dynamic-update-slice_fusion.8), channel_id=1, source_target_pairs={{0,24},{8,16},{16,8},{24,0},{1,25},{9,17},{17,9},{25,1},{2,26},{10... | collective-permute-start | bytes 1916936 | tf_op jit(solution)/shard_map/ppermute | solution.py:446
  59.3 287.5 %reduce-scatter.3.cloned.1.call-start = ((), (), s32[]{:S(2)}) async-start(), calls=%async_computation.3 | async-start | bytes 3932160 | tf_op jit(solution)/shard_map/reduce_scatter | solution.py:723
  107.2 24.8 %collective-permute-start.19 = (bf16[256,768]{1,0:T(8,128)(2,1)}, bf16[256,768]{1,0:T(8,128)(2,1)S(1)}, u32[]{:S(2)}, u32[]{:S(2)}) collective-permute-start(bf16[256,768]{1,0:T(8,128)(2,1)} %get-tuple-element.132.refs_0_), channel_id=1, source_target_pairs={{0,6},{1,7},{2,0},{3,1},{4,2},{5,3},{6,4},{7,5},{8,14},{9,15},{10,... | collective-permute-start | bytes 1179656 | tf_op jit(solution)/shard_map/ppermute | solution.py:440
  107.2 30.4 %collective-permute-start.17 = (bf16[256,768]{1,0:T(8,128)(2,1)}, bf16[256,768]{1,0:T(8,128)(2,1)S(1)}, u32[]{:S(2)}, u32[]{:S(2)}) collective-permute-start(bf16[256,768]{1,0:T(8,128)(2,1)} %get-tuple-element.132.refs_0_), channel_id=1, source_target_pairs={{0,4},{1,5},{2,6},{3,7},{4,0},{5,1},{6,2},{7,3},{8,12},{9,13},{10,... | collective-permute-start | bytes 1179656 | tf_op jit(solution)/shard_map/ppermute | solution.py:440
  109.4 32.1 %collective-permute-start.15 = (bf16[256,768]{1,0:T(8,128)(2,1)}, bf16[256,768]{1,0:T(8,128)(2,1)}, u32[]{:S(2)}, u32[]{:S(2)}) collective-permute-start(bf16[256,768]{1,0:T(8,128)(2,1)} %get-tuple-element.132.refs_0_), channel_id=1, source_target_pairs={{0,2},{1,3},{2,4},{3,5},{4,6},{5,7},{6,0},{7,1},{8,10},{9,11},{10,... | collective-permute-start | bytes 1179656 | tf_op jit(solution)/shard_map/ppermute | solution.py:440
  188.1 161.1 %reduce-scatter.5.cloned.1.call-start = ((), (), s32[]{:S(2)}) async-start(), calls=%async_computation.4 | async-start | bytes 3538944 | tf_op jit(solution)/shard_map/reduce_scatter | solution.py:823
  193.4 38.1 %collective-permute-start.29 = (bf16[256,768]{1,0:T(8,128)(2,1)S(1)}, bf16[256,768]{1,0:T(8,128)(2,1)S(1)}, u32[]{:S(2)}, u32[]{:S(2)}) collective-permute-start(bf16[256,768]{1,0:T(8,128)(2,1)S(1)} %get-tuple-element.219), channel_id=1, source_target_pairs={{0,2},{1,3},{2,4},{3,5},{4,6},{5,7},{6,0},{7,1},{8,10},{9,11},{10,... | collective-permute-start | bytes 1179656 | tf_op jit(solution)/shard_map/ppermute | solution.py:440
  197.3 34.2 %collective-permute-start.28 = (bf16[256,768]{1,0:T(8,128)(2,1)S(1)}, bf16[256,768]{1,0:T(8,128)(2,1)S(1)}, u32[]{:S(2)}, u32[]{:S(2)}) collective-permute-start(bf16[256,768]{1,0:T(8,128)(2,1)S(1)} %get-tuple-element.221), channel_id=1, source_target_pairs={{0,6},{1,7},{2,0},{3,1},{4,2},{5,3},{6,4},{7,5},{8,14},{9,15},{10,... | collective-permute-start | bytes 1179656 | tf_op jit(solution)/shard_map/ppermute | solution.py:440
  212.7 26.9 %collective-permute-start.27 = (bf16[768,512]{1,0:T(8,128)(2,1)S(1)}, bf16[768,512]{1,0:T(8,128)(2,1)S(1)}, u32[]{:S(2)}, u32[]{:S(2)}) collective-permute-start(bf16[768,512]{1,0:T(8,128)(2,1)S(1)} %get-tuple-element.231), channel_id=1, source_target_pairs={{0,16},{8,24},{16,0},{24,8},{1,17},{9,25},{17,1},{25,9},{2,18},{10... | collective-permute-start | bytes 2359304 | tf_op jit(solution)/shard_map/ppermute | solution.py:446
  215.0 26.5 %collective-permute-start.25 = (bf16[768,512]{1,0:T(8,128)(2,1)S(1)}, bf16[768,512]{1,0:T(8,128)(2,1)}, u32[]{:S(2)}, u32[]{:S(2)}) collective-permute-start(bf16[768,512]{1,0:T(8,128)(2,1)S(1)} %get-tuple-element.233), channel_id=1, source_target_pairs={{0,8},{8,0},{16,24},{24,16},{1,9},{9,1},{17,25},{25,17},{2,10},{10... | collective-permute-start | bytes 2359304 | tf_op jit(solution)/shard_map/ppermute | solution.py:446
  231.5 26.3 %collective-permute-start.32 = (bf16[768,512]{1,0:T(8,128)(2,1)S(1)}, bf16[768,512]{1,0:T(8,128)(2,1)}, u32[]{:S(2)}, u32[]{:S(2)}) collective-permute-start(bf16[768,512]{1,0:T(8,128)(2,1)S(1)} %get-tuple-element.169), channel_id=1, source_target_pairs={{0,16},{8,24},{16,0},{24,8},{1,17},{9,25},{17,1},{25,9},{2,18},{10... | collective-permute-start | bytes 2359304 | tf_op jit(solution)/shard_map/ppermute | solution.py:446
  232.0 26.4 %collective-permute-start.31 = (bf16[768,512]{1,0:T(8,128)(2,1)}, bf16[768,512]{1,0:T(8,128)(2,1)}, u32[]{:S(2)}, u32[]{:S(2)}) collective-permute-start(bf16[768,512]{1,0:T(8,128)(2,1)} %get-tuple-element.166), channel_id=1, source_target_pairs={{0,8},{8,0},{16,24},{24,16},{1,9},{9,1},{17,25},{25,17},{2,10},{10... | collective-permute-start | bytes 2359304 | tf_op jit(solution)/shard_map/ppermute | solution.py:446
  253.0 42.4 %collective-permute-start.35 = (bf16[768,384]{1,0:T(8,128)(2,1)}, bf16[768,384]{1,0:T(8,128)(2,1)}, u32[]{:S(2)}, u32[]{:S(2)}) collective-permute-start(bf16[768,384]{1,0:T(8,128)(2,1)} %broadcast_select_fusion), channel_id=1, source_target_pairs={{0,1},{1,0},{2,3},{3,2},{4,5},{5,4},{6,7},{7,6},{8,9},{9,8},{10,11... | collective-permute-start | bytes 1769480 | tf_op jit(solution)/shard_map/ppermute | solution.py:437
  257.6 37.9 %collective-permute-start.36 = (bf16[2,576,256]{2,1,0:T(8,128)(2,1)}, bf16[2,576,256]{2,1,0:T(8,128)(2,1)}, u32[]{:S(2)}, u32[]{:S(2)}) collective-permute-start(bf16[2,576,256]{2,1,0:T(8,128)(2,1)} %pad_maximum_fusion.4), channel_id=1, source_target_pairs={{0,16},{8,24},{16,0},{24,8},{1,17},{9,25},{17,1},{25,9},{2,18},{10... | collective-permute-start | bytes 1769480 | tf_op jit(solution)/shard_map/ppermute | solution.py:446
  262.0 33.5 %collective-permute-start.34 = (bf16[768,512]{1,0:T(8,128)(2,1)}, bf16[768,512]{1,0:T(8,128)(2,1)}, u32[]{:S(2)}, u32[]{:S(2)}) collective-permute-start(bf16[768,512]{1,0:T(8,128)(2,1)} %bitcast_add_fusion), channel_id=1, source_target_pairs={{0,8},{8,0},{16,24},{24,16},{1,9},{9,1},{17,25},{25,17},{2,10},{10... | collective-permute-start | bytes 2359304 | tf_op jit(solution)/shard_map/ppermute | solution.py:446
  262.0 33.5 %collective-permute-start.33 = (bf16[768,512]{1,0:T(8,128)(2,1)S(1)}, bf16[768,512]{1,0:T(8,128)(2,1)}, u32[]{:S(2)}, u32[]{:S(2)}) collective-permute-start(bf16[768,512]{1,0:T(8,128)(2,1)S(1)} %bitcast_add_fusion.1), channel_id=1, source_target_pairs={{0,16},{8,24},{16,0},{24,8},{1,17},{9,25},{17,1},{25,9},{2,18},{10... | collective-permute-start | bytes 2359304 | tf_op jit(solution)/shard_map/ppermute | solution.py:446
  305.9 28.6 %collective-permute-start.42 = (bf16[4,584,128]{2,1,0:T(8,128)(2,1)}, bf16[4,584,128]{2,1,0:T(8,128)(2,1)}, u32[]{:S(2)}, u32[]{:S(2)}) collective-permute-start(bf16[4,584,128]{2,1,0:T(8,128)(2,1)} %get-tuple-element.229), channel_id=1, source_target_pairs={{0,16},{8,24},{16,0},{24,8},{1,17},{9,25},{17,1},{25,9},{2,18},{10... | collective-permute-start | bytes 1794056 | tf_op jit(solution)/shard_map/ppermute | solution.py:446
  307.2 27.7 %collective-permute-start.43 = (bf16[4,584,128]{2,1,0:T(8,128)(2,1)}, bf16[4,584,128]{2,1,0:T(8,128)(2,1)}, u32[]{:S(2)}, u32[]{:S(2)}) collective-permute-start(bf16[4,584,128]{2,1,0:T(8,128)(2,1)} %get-tuple-element.228), channel_id=1, source_target_pairs={{0,24},{8,16},{16,8},{24,0},{1,25},{9,17},{17,9},{25,1},{2,26},{10... | collective-permute-start | bytes 1794056 | tf_op jit(solution)/shard_map/ppermute | solution.py:446
  (61 other events, 555.8 us)
Sparse Core Ops, SparseCore 0:
  59.4 40.9 all-gather.2
  188.2 52.3 reduce-scatter.2
  254.0 36.9 reduce-scatter.4

commit v4 on v3

--- a/solution.py
+++ b/solution.py
@@ -316,25 +316,26 @@
         d1 = jnp.sum(jnp.where(low, 0.0, prod), axis=1, keepdims=True)
         delta = jnp.where(lanes((rows, 128)) == 0, d0, d1).T
         sq = sq_ref[0:1, at_q : at_q + rows]
-        halves = []
-        for hh in range(2):
-            keep = low if hh == 0 else jnp.logical_not(low)
-            q = jnp.where(keep, qpair, jnp.zeros_like(qpair))
-            do = jnp.where(keep, dopair, jnp.zeros_like(dopair))
-            lse_row = lse_ref[0, hh : hh + 1, at_q : at_q + rows]
-            delta_row = delta[hh : hh + 1, :]
-            dq = jnp.zeros((64, rows), F32)
-            for j in range(count):
-                at = (first + qi + j) * rows
-                same = sk_ref[at : at + rows, 0:1] == sq
-                s = nt(k_ref[0, at : at + rows, :], q)
-                p = jnp.where(same, jnp.exp(s - lse_row), 0.0)
-                dp = nt(v_ref[0, at : at + rows, :], do)
-                ds = (p * (dp - delta_row)).astype(BF)
-                dv[at : at + rows, :] += nn(p.astype(BF), do)
-                dk[at : at + rows, :] += nn(ds, q)
-                dq += nn(k_t[64 * hh : 64 * hh + 64, at : at + rows], ds)
-            halves.append(dq)
+        def masked(x):
+            zero = jnp.zeros_like(x)
+            return jnp.concatenate([jnp.where(low, x, zero), jnp.where(low, zero, x)], axis=0)
+
+        q, do = masked(qpair), masked(dopair)
+        lse_row = jnp.concatenate([lse_ref[0, h : h + 1, at_q : at_q + rows] for h in range(2)], axis=1)
+        delta_row = jnp.concatenate([delta[h : h + 1, :] for h in range(2)], axis=1)
+        sq = jnp.concatenate([sq, sq], axis=1)
+        halves = [jnp.zeros((64, rows), F32) for _ in range(2)]
+        for j in range(count):
+            at = (first + qi + j) * rows
+            same = sk_ref[at : at + rows, 0:1] == sq
+            s = nt(k_ref[0, at : at + rows, :], q)
+            p = jnp.where(same, jnp.exp(s - lse_row), 0.0)
+            dp = nt(v_ref[0, at : at + rows, :], do)
+            ds = (p * (dp - delta_row)).astype(BF)
+            dv[at : at + rows, :] += nn(p.astype(BF), do)
+            dk[at : at + rows, :] += nn(ds, q)
+            for h in range(2):
+                halves[h] += nn(k_t[64 * h : 64 * h + 64, at : at + rows], ds[:, h * rows : (h + 1) * rows])
         dq = jnp.concatenate(halves, axis=0).T * 0.125
         at = base + at_q
         dq = dq * cos[at : at + rows, :] - turned(dq) * sin[at : at + rows, :]
@@ -621,7 +622,7 @@
     pick_t = (rank[:, :, None] == slot_ids[None, None, :]).astype(BF)
 
     smem = pl.BlockSpec(memory_space=pltpu.SMEM)
-    ft = min(256, FF // R)
+    ft = min(512, FF // R)
     steps = FF // ft
     per = FF // R // ft
     col = lambda n: pl.BlockSpec((n, ft), lambda i: (0, i))
@@ -776,7 +777,7 @@
             total += (after(got, *deps) if deps else got).astype(F32)
         return total
 
-    two_parts[2::2] = [after(x, gu_out[0]) for x in two_parts[2::2]]
+    two_parts[1] = after(two_parts[1], gu_out[0])
     near = []
     if square:
         gate_a, up_a = cross(gu_out[1][0], 1), cross(gu_out[3][0], 2)
@@ -806,20 +807,20 @@
         compiler_params=params(),
         name="result",
         cost_estimate=cost(14),
-    )(ix_arr, g_rows, og_all, pick_t, shid, dsg, dsu, wsd, after(ghid, gu_out[0], *two_parts[2::2], *near), expert_down)
+    )(ix_arr, g_rows, og_all, pick_t, shid, dsg, dsu, wsd, after(ghid, gu_out[0], two_parts[1], *near), expert_down)
 
     sgrad = jnp.concatenate(
         [sgu_grad[:, :fs].reshape(R, gr, fs), sgu_grad[:, fs:].reshape(R, gr, fs)]
         + [sd_grad[:, k * fs : (k + 1) * fs].reshape(R, drow, fs) for k in range(wide)],
         axis=1,
     )
-    two_parts[1::2] = [after(x, mix) for x in two_parts[1::2]]
+    two_parts[2:] = [after(x, mix) for x in two_parts[2:]]
     if square:
         gate_a, up_a = after(gate_a, mix), after(up_a, mix)
         two_parts[0], gate_a, up_a = lax.optimization_barrier((two_parts[0], gate_a, up_a))
         gate_c, up_c = cross(after(gu_out[1][1], mix), 1), cross(after(gu_out[3][1], mix), 2)
 
-    mix_in = after(mix, two_parts[1], *((gate_a, up_a) if square else ()))
+    mix_in = after(mix, two_parts[2], *((gate_a, up_a) if square else ()))
     mix_sum = lax.psum_scatter(mix_in.reshape(E * T, D), "ep", scatter_dimension=0, tiled=True)
 
     mid_grad, attn_grad, att_grad, gain2_part = pl.pallas_call(
@@ -901,7 +902,10 @@
         sg_mid = cross(sg_near + sg_got[1], 1)
         sg_mid, far_got = lax.optimization_barrier((sg_mid, far_got))
     lane = og1 + far_got
-    one_parts = [lane[nb]] + [line(lane[nb - s], -s) for s in range(1, chips)]
+    one_moved = lane[0]
+    for i in range(1, nb):
+        one_moved = lane[i] + line(one_moved, -1)
+    one_parts = [lane[nb], line(one_moved, -1)]
 
     n_chip = R * Z
 
@@ -956,8 +960,8 @@
     one_parts[0], *done = lax.optimization_barrier((one_parts[0], *done))
     gate_sum, up_sum, dn_sum, layer_out, sd_sum, to_z = done
     tokens_grad = pl.pallas_call(
-        functools.partial(last_kernel, chips),
-        in_specs=vmem(chips + 3),
+        functools.partial(last_kernel, 2),
+        in_specs=vmem(5),
         out_specs=vmem(1)[0],
         out_shape=shape((T, D), F32),
         compiler_params=params(),

time: 384 us -> 370 us (0.964)
  Pallas kernels: 141 us -> 131 us
  starting transfers between devices: 72.5 us -> 63.3 us
  waiting for transfers between devices: 61.3 us -> 67.5 us
    ppermute x12, starting transfers between devices: 20.5 us -> 12.9 us  [ring(): return lax.ppermute(x, 'ep', [(i, (i + 2 * s) % E) for i in range(E)])]
    pallas_call x1, Pallas kernels: 30.9 us -> 27.1 us  [shards(): pl.pallas_call(functools.partial(attend_back_kernel, first, count, T), gr...]
  transfers between devices with their start and end apart: 52 -> 52, of which waited for: 17 -> 17; matrix products, arithmetic and copies ran while one was open for 20% -> 21% of each run, Pallas kernels for 29% -> 27%
where the time goes in v4:
time: 370 us; the launch traced here: 365 us
  Pallas kernels  131 us (35%)
  waiting for transfers between devices  67.5 us (18%)
  starting transfers between devices  63.3 us (17%)
  other arithmetic  48.4 us (13%)
  local copies, waits for them, and re-layouts  38.3 us (10%)
  between operations  15.2 us (4%)
    pallas_call x1, Pallas kernels, shards(): pl.pallas_call(functools.partial(expert_kernel, E, T, experts), grid=(ste...  32 us
    pallas_call x1, Pallas kernels, shards(): pl.pallas_call(functools.partial(attend_back_kernel, first, count, T), gr...  27.1 us
    ppermute x4, waiting for transfers between devices, line(): lax.ppermute(x, 'ep', [(i, i + 2 * s) for i in range(E) if 0 <= i + 2 * s...  24.4 us
    ppermute x15, starting transfers between devices, swap(): return lax.ppermute(x, 'ep', [(i, i ^ 1) for i in range(E)])  22.9 us
    ppermute x17, waiting for transfers between devices, cross(): return lax.ppermute(x, 'rep', [(i, i ^ s) for i in range(R)])  22 us
    ppermute x12, waiting for transfers between devices, ring(): return lax.ppermute(x, 'ep', [(i, (i + 2 * s) % E) for i in range(E)])  19.9 us
    pallas_call x1, Pallas kernels, shards(): pl.pallas_call(functools.partial(result_kernel, E, T), grid=(steps,), in_...  15 us
    ppermute x17, starting transfers between devices, cross(): return lax.ppermute(x, 'rep', [(i, i ^ s) for i in range(R)])  13.4 us
  transfers between devices with their start and end apart: 52, of which 17 were waited for; matrix products, arithmetic and copies ran while one was open for 21% of the time, Pallas kernels for 27%

profile of v4, /device:TPU:9, one launch (start us, length us, event | category | flops | bytes accessed | tf_op | source)
XLA Modules:
  0.0 365.2 jit_solution(3327450818955628219)
XLA Ops:
  24.6 3.8 %collective-permute-start.3 = (bf16[264,768]{1,0:T(8,128)(2,1)}, bf16[264,768]{1,0:T(8,128)(2,1)}, u32[]{:S(2)}, u32[]{:S(2)}) collective-permute-start(bf16[264,768]{1,0:T(8,128)(2,1)} %fusion.8.refs_0_), channel_id=1, source_target_pairs={{0,1},{1,0},{2,3},{3,2},{4,5},{5,4},{6,7},{7,6},{8,9},{9,8},{10,11... | collective-permute-start | bytes 1216520 | tf_op jit(solution)/shard_map/ppermute | solution.py:438
  34.5 4.2 %multiply_sine_fusion = (f32[1536,128]{1,0:T(8,128)}, f32[1536,128]{1,0:T(8,128)}) fusion(f32[128]{0:T(128)S(1)} %mul.48, f32[1536]{0:T(1024)S(1)} %convert_element_type.217), kind=kLoop, calls=%fused_computation.19 | loop fusion | flops 196608 | bytes 1579520 | tf_op jit(solution)/shard_map/sin | solution.py:517
  39.9 5.4 %all-to-all-start = ((bf16[8,24,512]{2,1,0:T(8,128)(2,1)}), bf16[8,24,512]{2,1,0:T(8,128)(2,1)S(1)}, u32[]{:S(2)}, u32[]{:S(2)}) async-start(bf16[8,24,512]{2,1,0:T(8,128)(2,1)} %pad_maximum_fusion.8), calls=%async_computation | async-start | bytes 393216 | tf_op jit(solution)/shard_map/all_to_all | solution.py:551
  46.7 12.6 %collective-permute-done.2.refs_2_ = bf16[264,768]{1,0:T(8,128)(2,1)} collective-permute-done((bf16[264,768]{1,0:T(8,128)(2,1)}, bf16[264,768]{1,0:T(8,128)(2,1)}, u32[]{:S(2)}, u32[]{:S(2)}) %collective-permute-start.2) | collective-permute-done | bytes 405536 | tf_op jit(solution)/shard_map/ppermute | solution.py:444
  62.2 5.6 %collective-permute-done.10 = bf16[4,208,384]{2,1,0:T(8,128)(2,1)} collective-permute-done((bf16[4,208,384]{2,1,0:T(8,128)(2,1)S(1)}, bf16[4,208,384]{2,1,0:T(8,128)(2,1)}, u32[]{:S(2)}, u32[]{:S(2)}) %collective-permute-start.10) | collective-permute-done | bytes 639008 | tf_op jit(solution)/shard_map/ppermute | solution.py:447
  73.9 8.1 %qkv.1 = (bf16[6,256,768]{2,1,0:T(8,128)(2,1)}, bf16[3,6,256,128]{3,2,1,0:T(8,128)(2,1)}, bf16[3,6,256,128]{3,2,1,0:T(8,128)(2,1)}, bf16[3,2,256,128]{3,2,1,0:T(8,128)(2,1)}) custom-call(s32[1]{0:T(128)} %bitcast.c_ref, bf16[264,768]{1,0:T(8,128)(2,1)} %fusion.8.refs_0_, bf16[264,768]{1,0:T(8,128)(2,1)} %collective-permute-done.1.refs_1_, ...), custom_call_target="tpu_custom_call" | custom-call | flops 8800000000 | bytes 800000 | tf_op jit(solution)/shard_map/qkv/pallas_call | solution.py:520
  86.3 10.2 %attend.1 = (f32[3,512,128]{2,1,0:T(8,128)}, bf16[3,512,128]{2,1,0:T(8,128)(2,1)}, f32[3,8,512]{2,1,0:T(8,128)}) custom-call(bf16[3,512,128]{2,1,0:T(8,128)(2,1)} %bitcast.385, bf16[3,1536,128]{2,1,0:T(8,128)(2,1)} %bitcast.381, bf16[3,1536,128]{2,1,0:T(8,128)(2,1)} %bitcast.383, f32[512,128]{1,0:T(8,128)} %broadcast_in_dim.109.sq_ref, f32[1,1536]{1,0:T(1,128)} %bitcast.371), custom_call_target="tpu_custom_call" | custom-call | flops 11000000512 | bytes 1000000 | tf_op jit(solution)/shard_map/attend/pallas_call | solution.py:559
  104.1 3.0 mid.1
  110.3 6.1 %collective-permute-done.22 = bf16[576,256]{1,0:T(8,128)(2,1)S(1)} collective-permute-done((bf16[576,256]{1,0:T(8,128)(2,1)S(1)}, bf16[576,256]{1,0:T(8,128)(2,1)S(1)}, u32[]{:S(2)}, u32[]{:S(2)}) %collective-permute-start.22) | collective-permute-done | bytes 294944 | tf_op jit(solution)/shard_map/ppermute | solution.py:447
  121.7 8.8 %pre.1 = (bf16[1024,2048]{1,0:T(8,128)(2,1)}, bf16[768,1024]{1,0:T(8,128)(2,1)}) custom-call(s32[8]{0:T(128)} %stack.80.ix.ix_s, bf16[8,264,768]{2,1,0:T(8,128)(2,1)} %bitcast.376, bf16[8,128,256]{2,1,0:T(8,128)(2,1)} %compare_convert_fusion.1.p_ref.refs_8_, bf16[2048,768]{1,0:T(8,128)(2,1)} %bitcast.379), custom_call_target="tpu_custom_call" | custom-call | flops 13200000000 | bytes 1200000 | tf_op jit(solution)/shard_map/pre/pallas_call | solution.py:632
  130.4 7.1 %collective-permute-start.20 = (bf16[256,768]{1,0:T(8,128)(2,1)S(1)}, bf16[256,768]{1,0:T(8,128)(2,1)S(1)}, u32[]{:S(2)}, u32[]{:S(2)}) collective-permute-start(bf16[256,768]{1,0:T(8,128)(2,1)S(1)} %collective-permute-done.19.refs_6_), channel_id=1, source_target_pairs={{0,1},{1,0},{2,3},{3,2},{4,5},{5,4},{6,7},{7,6},{8,9},{9,8},{10,11... | collective-permute-start | bytes 1179656 | tf_op jit(solution)/shard_map/ppermute | solution.py:438
  137.6 3.9 %collective-permute-done.15.refs_2_ = bf16[256,768]{1,0:T(8,128)(2,1)} collective-permute-done((bf16[256,768]{1,0:T(8,128)(2,1)}, bf16[256,768]{1,0:T(8,128)(2,1)}, u32[]{:S(2)}, u32[]{:S(2)}) %collective-permute-start.15) | collective-permute-done | bytes 393248 | tf_op jit(solution)/shard_map/ppermute | solution.py:441
  146.0 32.0 %expert.1 = (bf16[1024,768]{1,0:T(8,128)(2,1)}, bf16[2048,768]{1,0:T(8,128)(2,1)}, bf16[1024,2048]{1,0:T(8,128)(2,1)}, bf16[1024,2048]{1,0:T(8,128)(2,1)}, bf16[...) custom-call(s32[1]{0:T(128)} %bitcast.29.e_ref, ...), custom_call_target="tpu_custom_call" | custom-call | flops 41799999488 | bytes 3800000 | tf_op jit(solution)/shard_map/expert/pallas_call | solution.py:646
  178.6 7.2 %dgrad.1 = bf16[768,2048]{1,0:T(8,128)(2,1)} custom-call(bf16[768,1024]{1,0:T(8,128)(2,1)} %get-tuple-element.142.ogx_t, bf16[1024,2048]{1,0:T(8,128)(2,1)} %get-tuple-element.156.ghid), custom_call_target="tpu_custom_call" | custom-call | flops 11000000512 | bytes 1000000 | tf_op jit(solution)/shard_map/dgrad/pallas_call | solution.py:714
  196.1 12.7 %wgrad.1 = (bf16[2,768,512]{2,1,0:T(8,128)(2,1)}, bf16[2,768,512]{2,1,0:T(8,128)(2,1)}, bf16[2,768,512]{2,1,0:T(8,128)(2,1)}, bf16[2,768,512]{2,1,0:T(8,128)(2,1)}) custom-call(s32[1]{0:T(128)} %bitcast.55.r_ref, bf16[1024,768]{1,0:T(8,128)(2,1)} %get-tuple-element.146.x_ref, bf16[1024,2048]{1,0:T(8,128)(2,1)} %get-tuple-element.147.degate, ...), custom_call_target="tpu_custom_call" | custom-call | flops 14300000256 | bytes 1300000 | tf_op jit(solution)/shard_map/wgrad/pallas_call | solution.py:755
  212.8 15.0 %result.1 = (bf16[8,256,768]{2,1,0:T(8,128)(2,1)}, bf16[768,512]{1,0:T(8,128)(2,1)}, bf16[256,768]{1,0:T(8,128)(2,1)}) custom-call(s32[8]{0:T(128)} %stack.80.ix.ix_s, bf16[2048,768]{1,0:T(8,128)(2,1)} %get-tuple-element.150.g_ref, bf16[8,264,768]{2,1,0:T(8,128)(2,1)} %bitcast.378, bf16[8,256,128]{2,1,0:T(8,128)(2,1)} %compare_convert_fusion.refs_9_.pt_ref, ...), custom_call_target="tpu_custom_call" | custom-call | flops 15399999488 | bytes 1400000 | tf_op jit(solution)/shard_map/result/pallas_call | solution.py:784
  230.9 5.5 %collective-permute-done.27 = bf16[768,512]{1,0:T(8,128)(2,1)S(1)} collective-permute-done((bf16[768,512]{1,0:T(8,128)(2,1)S(1)}, bf16[768,512]{1,0:T(8,128)(2,1)S(1)}, u32[]{:S(2)}, u32[]{:S(2)}) %collective-permute-start.27) | collective-permute-done | bytes 786464 | tf_op jit(solution)/shard_map/ppermute | solution.py:447
  239.1 4.2 %mid_back.1 = (f32[256,768]{1,0:T(8,128)}, bf16[256,768]{1,0:T(8,128)(2,1)}, bf16[6,256,128]{2,1,0:T(8,128)(2,1)}, f32[8,768]{1,0:T(8,128)}) custom-call(bf16[256,768]{1,0:T(8,128)(2,1)} %get-tuple-element.161.refs_0_, bf16[256,768]{1,0:T(8,128)(2,1)} %copy-done.28, bf16[256,768]{1,0:T(8,128)(2,1)} %copy-done.30, bf16[256,768]{1,0:T(8,128)(2,1)} %copy-done.29, ...), custom_call_target="tpu_custom_call" | custom-call | flops 4400000000 | bytes 400000 | tf_op jit(solution)/shard_map/mid_back/pallas_call | solution.py:826
  245.0 3.5 collective-permute-start.30
  261.6 27.1 %attend_back.1 = (bf16[3,3,768,128]{3,2,1,0:T(8,128)(2,1)}, bf16[3,256,768]{2,1,0:T(8,128)(2,1)}, bf16[3,256,768]{2,1,0:T(8,128)(2,1)}, f32[8,768]{1,0:T(8,128)}) custom-call(bf16[3,512,128]{2,1,0:T(8,128)(2,1)} %bitcast.386, bf16[3,1536,128]{2,1,0:T(8,128)(2,1)} %bitcast.382, bf16[3,1536,128]{2,1,0:T(8,128)(2,1)} %bitcast.384, ...), custom_call_target="tpu_custom_call" | custom-call | flops 32999999488 | bytes 3000000 | tf_op jit(solution)/shard_map/attend_back/pallas_call | solution.py:854
  309.2 7.6 %collective-permute-done.40 = bf16[256,768]{1,0:T(8,128)(2,1)} collective-permute-done((bf16[256,768]{1,0:T(8,128)(2,1)}, bf16[256,768]{1,0:T(8,128)(2,1)}, u32[]{:S(2)}, u32[]{:S(2)}) %collective-permute-start.40) | collective-permute-done | bytes 393248 | tf_op jit(solution)/shard_map/ppermute | solution.py:444
  320.3 4.1 %convert_add_fusion = (f32[768,512]{1,0:T(8,128)}, f32[768,512]{1,0:T(8,128)}) fusion(bf16[768,512]{1,0:T(8,128)(2,1)} %collective-permute-done.34, bf16[768,512]{1,0:T(8,128)(2,1)S(1)} %copy-done.12, bf16[2,768,512]{2,1,0:T(8,128)(2,1)} %get-tuple-element.168, bf16[768,512]{1,0:T(8,128)(2,1)} %collective-permute-done.33, bf16[768,512]{1,0:T(8,128)(2,1)} %copy-done.13, ...), kind=kLoop, calls=%fused_computation.10 | loop fusion | flops 3932160 | bytes 7864320 | tf_op jit(solution)/shard_map/add | solution.py:954
  324.4 4.2 %collective-permute-done.41.refs_1_ = bf16[256,768]{1,0:T(8,128)(2,1)S(1)} collective-permute-done((bf16[256,768]{1,0:T(8,128)(2,1)S(1)}, bf16[256,768]{1,0:T(8,128)(2,1)S(1)}, u32[]{:S(2)}, u32[]{:S(2)}) %collective-permute-start.41) | collective-permute-done | bytes 393248 | tf_op jit(solution)/shard_map/ppermute | solution.py:444
  340.1 11.1 %collective-permute-done.46 = bf16[776,128]{1,0:T(8,128)(2,1)S(1)} collective-permute-done((bf16[776,128]{1,0:T(8,128)(2,1)S(1)}, bf16[776,128]{1,0:T(8,128)(2,1)S(1)}, u32[]{:S(2)}, u32[]{:S(2)}) %collective-permute-start.46) | collective-permute-done | bytes 198688 | tf_op jit(solution)/shard_map/ppermute | solution.py:441
  (359 shorter events, 136.9 us)
Async XLA Ops:
  20.4 40.5 %collective-permute-start.1 = (bf16[264,768]{1,0:T(8,128)(2,1)}, bf16[264,768]{1,0:T(8,128)(2,1)}, u32[]{:S(2)}, u32[]{:S(2)}) collective-permute-start(bf16[264,768]{1,0:T(8,128)(2,1)} %fusion.8.refs_0_), channel_id=1, source_target_pairs={{0,2},{1,3},{2,4},{3,5},{4,6},{5,7},{8,10},{9,11},{10,12},{11,13},... | collective-permute-start | bytes 1216520 | tf_op jit(solution)/shard_map/ppermute | solution.py:444
  22.4 36.9 %collective-permute-start.2 = (bf16[264,768]{1,0:T(8,128)(2,1)}, bf16[264,768]{1,0:T(8,128)(2,1)}, u32[]{:S(2)}, u32[]{:S(2)}) collective-permute-start(bf16[264,768]{1,0:T(8,128)(2,1)} %fusion.8.refs_0_), channel_id=1, source_target_pairs={{0,4},{1,5},{2,6},{3,7},{8,12},{9,13},{10,14},{11,15},{16,20},{17,... | collective-permute-start | bytes 1216520 | tf_op jit(solution)/shard_map/ppermute | solution.py:444
  33.2 27.8 %collective-permute-start.9 = (bf16[4,208,384]{2,1,0:T(8,128)(2,1)S(1)}, bf16[4,208,384]{2,1,0:T(8,128)(2,1)}, u32[]{:S(2)}, u32[]{:S(2)}) collective-permute-start(bf16[4,208,384]{2,1,0:T(8,128)(2,1)S(1)} %bitcast_dynamic-update-slice_fusion.8), channel_id=1, source_target_pairs={{0,8},{8,0},{16,24},{24,16},{1,9},{9,1},{17,25},{25,17},{2,10},{10... | collective-permute-start | bytes 1916936 | tf_op jit(solution)/shard_map/ppermute | solution.py:447
  38.7 29.1 %collective-permute-start.10 = (bf16[4,208,384]{2,1,0:T(8,128)(2,1)S(1)}, bf16[4,208,384]{2,1,0:T(8,128)(2,1)}, u32[]{:S(2)}, u32[]{:S(2)}) collective-permute-start(bf16[4,208,384]{2,1,0:T(8,128)(2,1)S(1)} %bitcast_dynamic-update-slice_fusion.8), channel_id=1, source_target_pairs={{0,16},{8,24},{16,0},{24,8},{1,17},{9,25},{17,1},{25,9},{2,18},{10... | collective-permute-start | bytes 1916936 | tf_op jit(solution)/shard_map/ppermute | solution.py:447
  39.9 42.1 %all-to-all-start = ((bf16[8,24,512]{2,1,0:T(8,128)(2,1)}), bf16[8,24,512]{2,1,0:T(8,128)(2,1)S(1)}, u32[]{:S(2)}, u32[]{:S(2)}) async-start(bf16[8,24,512]{2,1,0:T(8,128)(2,1)} %pad_maximum_fusion.8), calls=%async_computation | async-start | bytes 393216 | tf_op jit(solution)/shard_map/all_to_all | solution.py:551
  45.4 72.3 %all-gather.3.cloned.1.call-start = ((), (), s32[]{:S(2)}) async-start(), calls=%async_computation.5 | async-start | bytes 3649536 | tf_op jit(solution)/shard_map/all_gather | solution.py:542
  59.3 273.7 %reduce-scatter.3.cloned.1.call-start = ((), (), s32[]{:S(2)}) async-start(), calls=%async_computation.3 | async-start | bytes 3932160 | tf_op jit(solution)/shard_map/reduce_scatter | solution.py:724
  107.1 23.4 %collective-permute-start.19 = (bf16[256,768]{1,0:T(8,128)(2,1)}, bf16[256,768]{1,0:T(8,128)(2,1)S(1)}, u32[]{:S(2)}, u32[]{:S(2)}) collective-permute-start(bf16[256,768]{1,0:T(8,128)(2,1)} %get-tuple-element.132.refs_0_), channel_id=1, source_target_pairs={{0,6},{1,7},{2,0},{3,1},{4,2},{5,3},{6,4},{7,5},{8,14},{9,15},{10,... | collective-permute-start | bytes 1179656 | tf_op jit(solution)/shard_map/ppermute | solution.py:441
  107.1 30.4 %collective-permute-start.17 = (bf16[256,768]{1,0:T(8,128)(2,1)}, bf16[256,768]{1,0:T(8,128)(2,1)S(1)}, u32[]{:S(2)}, u32[]{:S(2)}) collective-permute-start(bf16[256,768]{1,0:T(8,128)(2,1)} %get-tuple-element.132.refs_0_), channel_id=1, source_target_pairs={{0,4},{1,5},{2,6},{3,7},{4,0},{5,1},{6,2},{7,3},{8,12},{9,13},{10,... | collective-permute-start | bytes 1179656 | tf_op jit(solution)/shard_map/ppermute | solution.py:441
  109.3 32.1 %collective-permute-start.15 = (bf16[256,768]{1,0:T(8,128)(2,1)}, bf16[256,768]{1,0:T(8,128)(2,1)}, u32[]{:S(2)}, u32[]{:S(2)}) collective-permute-start(bf16[256,768]{1,0:T(8,128)(2,1)} %get-tuple-element.132.refs_0_), channel_id=1, source_target_pairs={{0,2},{1,3},{2,4},{3,5},{4,6},{5,7},{6,0},{7,1},{8,10},{9,11},{10,... | collective-permute-start | bytes 1179656 | tf_op jit(solution)/shard_map/ppermute | solution.py:441
  185.9 149.6 %reduce-scatter.5.cloned.1.call-start = ((), (), s32[]{:S(2)}) async-start(), calls=%async_computation.4 | async-start | bytes 3538944 | tf_op jit(solution)/shard_map/reduce_scatter | solution.py:824
  194.0 33.9 %collective-permute-start.29 = (bf16[256,768]{1,0:T(8,128)(2,1)}, bf16[256,768]{1,0:T(8,128)(2,1)S(1)}, u32[]{:S(2)}, u32[]{:S(2)}) collective-permute-start(bf16[256,768]{1,0:T(8,128)(2,1)} %get-tuple-element.219), channel_id=1, source_target_pairs={{0,2},{1,3},{2,4},{3,5},{4,6},{5,7},{6,0},{7,1},{8,10},{9,11},{10,... | collective-permute-start | bytes 1179656 | tf_op jit(solution)/shard_map/ppermute | solution.py:441
  194.0 34.1 %collective-permute-start.28 = (bf16[256,768]{1,0:T(8,128)(2,1)S(1)}, bf16[256,768]{1,0:T(8,128)(2,1)S(1)}, u32[]{:S(2)}, u32[]{:S(2)}) collective-permute-start(bf16[256,768]{1,0:T(8,128)(2,1)S(1)} %get-tuple-element.220), channel_id=1, source_target_pairs={{0,4},{1,5},{2,6},{3,7},{4,0},{5,1},{6,2},{7,3},{8,12},{9,13},{10,... | collective-permute-start | bytes 1179656 | tf_op jit(solution)/shard_map/ppermute | solution.py:441
  210.4 26.0 %collective-permute-start.27 = (bf16[768,512]{1,0:T(8,128)(2,1)S(1)}, bf16[768,512]{1,0:T(8,128)(2,1)S(1)}, u32[]{:S(2)}, u32[]{:S(2)}) collective-permute-start(bf16[768,512]{1,0:T(8,128)(2,1)S(1)} %get-tuple-element.231), channel_id=1, source_target_pairs={{0,16},{8,24},{16,0},{24,8},{1,17},{9,25},{17,1},{25,9},{2,18},{10... | collective-permute-start | bytes 2359304 | tf_op jit(solution)/shard_map/ppermute | solution.py:447
  212.7 26.4 %collective-permute-start.25 = (bf16[768,512]{1,0:T(8,128)(2,1)S(1)}, bf16[768,512]{1,0:T(8,128)(2,1)S(1)}, u32[]{:S(2)}, u32[]{:S(2)}) collective-permute-start(bf16[768,512]{1,0:T(8,128)(2,1)S(1)} %get-tuple-element.233), channel_id=1, source_target_pairs={{0,8},{8,0},{16,24},{24,16},{1,9},{9,1},{17,25},{25,17},{2,10},{10... | collective-permute-start | bytes 2359304 | tf_op jit(solution)/shard_map/ppermute | solution.py:447
  228.1 27.6 %collective-permute-start.32 = (bf16[768,512]{1,0:T(8,128)(2,1)S(1)}, bf16[768,512]{1,0:T(8,128)(2,1)}, u32[]{:S(2)}, u32[]{:S(2)}) collective-permute-start(bf16[768,512]{1,0:T(8,128)(2,1)S(1)} %get-tuple-element.169), channel_id=1, source_target_pairs={{0,16},{8,24},{16,0},{24,8},{1,17},{9,25},{17,1},{25,9},{2,18},{10... | collective-permute-start | bytes 2359304 | tf_op jit(solution)/shard_map/ppermute | solution.py:447
  229.4 26.7 %collective-permute-start.31 = (bf16[768,512]{1,0:T(8,128)(2,1)}, bf16[768,512]{1,0:T(8,128)(2,1)}, u32[]{:S(2)}, u32[]{:S(2)}) collective-permute-start(bf16[768,512]{1,0:T(8,128)(2,1)} %get-tuple-element.166), channel_id=1, source_target_pairs={{0,8},{8,0},{16,24},{24,16},{1,9},{9,1},{17,25},{25,17},{2,10},{10... | collective-permute-start | bytes 2359304 | tf_op jit(solution)/shard_map/ppermute | solution.py:447
  250.9 38.6 %collective-permute-start.35 = (bf16[768,384]{1,0:T(8,128)(2,1)}, bf16[768,384]{1,0:T(8,128)(2,1)}, u32[]{:S(2)}, u32[]{:S(2)}) collective-permute-start(bf16[768,384]{1,0:T(8,128)(2,1)} %broadcast_select_fusion), channel_id=1, source_target_pairs={{0,1},{1,0},{2,3},{3,2},{4,5},{5,4},{6,7},{7,6},{8,9},{9,8},{10,11... | collective-permute-start | bytes 1769480 | tf_op jit(solution)/shard_map/ppermute | solution.py:438
  255.4 34.1 %collective-permute-start.36 = (bf16[2,576,256]{2,1,0:T(8,128)(2,1)}, bf16[2,576,256]{2,1,0:T(8,128)(2,1)}, u32[]{:S(2)}, u32[]{:S(2)}) collective-permute-start(bf16[2,576,256]{2,1,0:T(8,128)(2,1)} %pad_maximum_fusion.4), channel_id=1, source_target_pairs={{0,16},{8,24},{16,0},{24,8},{1,17},{9,25},{17,1},{25,9},{2,18},{10... | collective-permute-start | bytes 1769480 | tf_op jit(solution)/shard_map/ppermute | solution.py:447
  259.4 30.1 %collective-permute-start.34 = (bf16[768,512]{1,0:T(8,128)(2,1)}, bf16[768,512]{1,0:T(8,128)(2,1)}, u32[]{:S(2)}, u32[]{:S(2)}) collective-permute-start(bf16[768,512]{1,0:T(8,128)(2,1)} %bitcast_add_fusion), channel_id=1, source_target_pairs={{0,8},{8,0},{16,24},{24,16},{1,9},{9,1},{17,25},{25,17},{2,10},{10... | collective-permute-start | bytes 2359304 | tf_op jit(solution)/shard_map/ppermute | solution.py:447
  259.6 30.0 %collective-permute-start.33 = (bf16[768,512]{1,0:T(8,128)(2,1)S(1)}, bf16[768,512]{1,0:T(8,128)(2,1)}, u32[]{:S(2)}, u32[]{:S(2)}) collective-permute-start(bf16[768,512]{1,0:T(8,128)(2,1)S(1)} %bitcast_add_fusion.1), channel_id=1, source_target_pairs={{0,16},{8,24},{16,0},{24,8},{1,17},{9,25},{17,1},{25,9},{2,18},{10... | collective-permute-start | bytes 2359304 | tf_op jit(solution)/shard_map/ppermute | solution.py:447
  299.6 24.8 %collective-permute-start.39 = (bf16[4,584,128]{2,1,0:T(8,128)(2,1)}, bf16[4,584,128]{2,1,0:T(8,128)(2,1)}, u32[]{:S(2)}, u32[]{:S(2)}) collective-permute-start(bf16[4,584,128]{2,1,0:T(8,128)(2,1)} %get-tuple-element.227), channel_id=1, source_target_pairs={{0,8},{8,0},{16,24},{24,16},{1,9},{9,1},{17,25},{25,17},{2,10},{10... | collective-permute-start | bytes 1794056 | tf_op jit(solution)/shard_map/ppermute | solution.py:447
  299.8 28.8 %collective-permute-start.42 = (bf16[4,584,128]{2,1,0:T(8,128)(2,1)}, bf16[4,584,128]{2,1,0:T(8,128)(2,1)}, u32[]{:S(2)}, u32[]{:S(2)}) collective-permute-start(bf16[4,584,128]{2,1,0:T(8,128)(2,1)} %get-tuple-element.229), channel_id=1, source_target_pairs={{0,16},{8,24},{16,0},{24,8},{1,17},{9,25},{17,1},{25,9},{2,18},{10... | collective-permute-start | bytes 1794056 | tf_op jit(solution)/shard_map/ppermute | solution.py:447
  301.0 27.7 %collective-permute-start.43 = (bf16[4,584,128]{2,1,0:T(8,128)(2,1)}, bf16[4,584,128]{2,1,0:T(8,128)(2,1)}, u32[]{:S(2)}, u32[]{:S(2)}) collective-permute-start(bf16[4,584,128]{2,1,0:T(8,128)(2,1)} %get-tuple-element.228), channel_id=1, source_target_pairs={{0,24},{8,16},{16,8},{24,0},{1,25},{9,17},{17,9},{25,1},{2,26},{10... | collective-permute-start | bytes 1794056 | tf_op jit(solution)/shard_map/ppermute | solution.py:447
  (64 other events, 548.0 us)
Sparse Core Ops, SparseCore 0:
  59.4 40.9 all-gather.2
  186.0 53.3 reduce-scatter.2
  251.9 36.1 reduce-scatter.4

commit v5 on v4

--- a/solution.py
+++ b/solution.py
@@ -554,7 +554,6 @@
     shared = jnp.concatenate(
         [gu[:, :fs], gu[:, fs:]] + [shared_down[:, k * fs : (k + 1) * fs] for k in range(wide)], axis=0
     )
-    shared_got = [cross(shared, s) for s in range(1, R)]
     one = lambda *dims: pl.BlockSpec((1,) + dims, lambda i: (i, 0, 0))
     att, att_low, lse = pl.pallas_call(
         functools.partial(attend_kernel, first, count, T),
@@ -594,17 +593,10 @@
         cost_estimate=cost(3),
     )(attended, wo, tokens, gain2)
 
-    shared_got = [after(x, h2) for x in shared_got]
-    shared = put(jnp.zeros((R,) + shared.shape, BF), after(shared, h2), r)
-    for i in range(1, R):
-        shared = put(shared, shared_got[i - 1], r ^ i)
-    gr = E * wrow
-    wsg = shared[:, :gr].reshape(D, fs)
-    wsu = shared[:, gr : 2 * gr].reshape(D, fs)
-    wsd = jnp.concatenate(
-        [shared[:, 2 * gr + k * drow : 2 * gr + (k + 1) * drow].reshape(fs, fs) for k in range(wide)], axis=1
-    )
-    h2_lane = [h2] + [ring(h2, s) for s in range(1, Z)]
+    h2_lane = [h2] + [None] * (Z - 1)
+    h2_lane[1] = ring(h2, 1)
+    for s in range(Z - 1, Z // 2, -1):
+        h2_lane[s] = ring(h2 if s == Z - 1 else h2_lane[s + 1], -1)
 
     def both_cores(lane):
         blocks = []
@@ -642,7 +634,21 @@
         cost_estimate=cost(12),
     )(ix_arr, og_all, pick, expert_down.reshape(FF, D))
 
-    h2_blocks = both_cores([after(x, dehid) for x in h2_lane])
+    shared_part = after(shared, pick)
+    shared_got = [cross(shared_part, s) for s in range(1, R)]
+    shared = put(jnp.zeros((R,) + shared.shape, BF), after(shared_part, dehid), r)
+    for i in range(1, R):
+        shared = put(shared, after(shared_got[i - 1], dehid), r ^ i)
+    gr = E * wrow
+    wsg = shared[:, :gr].reshape(D, fs)
+    wsu = shared[:, gr : 2 * gr].reshape(D, fs)
+    wsd = jnp.concatenate(
+        [shared[:, 2 * gr + k * drow : 2 * gr + (k + 1) * drow].reshape(fs, fs) for k in range(wide)], axis=1
+    )
+    h2_lane[1] = after(h2_lane[1], dehid)
+    for s in range(2, Z // 2 + 1):
+        h2_lane[s] = ring(h2_lane[s - 1], 1)
+    h2_blocks = both_cores([h2_lane[s] if 0 < s <= Z // 2 else after(h2_lane[s], dehid) for s in range(Z)])
     (x_rows, g_rows, ghid, degate, deup, shid, dsg, dsu, tg, tg_far, rgrad) = pl.pallas_call(
         functools.partial(expert_kernel, E, T, experts),
         grid=(steps,),

time: 370 us -> 362 us (0.978)
  waiting for transfers between devices: 67.5 us -> 62.9 us
    ppermute x17, waiting for transfers between devices: 22 us -> 13.5 us  [cross(): return lax.ppermute(x, 'rep', [(i, i ^ s) for i in range(R)])]
    ppermute x15, starting transfers between devices: 22.9 us -> 18.1 us  [swap(): return lax.ppermute(x, 'ep', [(i, i ^ 1) for i in range(E)])]
    ppermute x12, waiting for transfers between devices: 19.9 us -> 23.9 us  [ring(): return lax.ppermute(x, 'ep', [(i, (i + 2 * s) % E) for i in range(E)])]
  transfers between devices with their start and end apart: 52 -> 52, of which waited for: 17 -> 15; matrix products, arithmetic and copies ran while one was open for 21% -> 22% of each run, Pallas kernels for 27% -> 28%
where the time goes in v5:
time: 362 us; the launch traced here: 357 us
  Pallas kernels  130 us (36%)
  waiting for transfers between devices  62.9 us (17%)
  starting transfers between devices  60.3 us (17%)
  other arithmetic  48.1 us (13%)
  local copies, waits for them, and re-layouts  38.4 us (11%)
  between operations  15.3 us (4%)
    pallas_call x1, Pallas kernels, shards(): pl.pallas_call(functools.partial(expert_kernel, E, T, experts), grid=(ste...  32 us
    pallas_call x1, Pallas kernels, shards(): pl.pallas_call(functools.partial(attend_back_kernel, first, count, T), gr...  27.1 us
    ppermute x4, waiting for transfers between devices, line(): lax.ppermute(x, 'ep', [(i, i + 2 * s) for i in range(E) if 0 <= i + 2 * s...  24.3 us
    ppermute x12, waiting for transfers between devices, ring(): return lax.ppermute(x, 'ep', [(i, (i + 2 * s) % E) for i in range(E)])  23.9 us
    ppermute x15, starting transfers between devices, swap(): return lax.ppermute(x, 'ep', [(i, i ^ 1) for i in range(E)])  18.1 us
    pallas_call x1, Pallas kernels, shards(): pl.pallas_call(functools.partial(result_kernel, E, T), grid=(steps,), in_...  15 us
    ppermute x12, starting transfers between devices, ring(): return lax.ppermute(x, 'ep', [(i, (i + 2 * s) % E) for i in range(E)])  14.3 us
    ppermute x17, starting transfers between devices, cross(): return lax.ppermute(x, 'rep', [(i, i ^ s) for i in range(R)])  13.8 us
  transfers between devices with their start and end apart: 52, of which 15 were waited for; matrix products, arithmetic and copies ran while one was open for 22% of the time, Pallas kernels for 28%

profile of v5, /device:TPU:9, one launch (start us, length us, event | category | flops | bytes accessed | tf_op | source)
XLA Modules:
  0.0 357.0 jit_solution(3525859933395320900)
XLA Ops:
  24.7 3.7 %collective-permute-start.3 = (bf16[264,768]{1,0:T(8,128)(2,1)}, bf16[264,768]{1,0:T(8,128)(2,1)}, u32[]{:S(2)}, u32[]{:S(2)}) collective-permute-start(bf16[264,768]{1,0:T(8,128)(2,1)} %fusion.8.refs_0_), channel_id=1, source_target_pairs={{0,1},{1,0},{2,3},{3,2},{4,5},{5,4},{6,7},{7,6},{8,9},{9,8},{10,11... | collective-permute-start | bytes 1216520 | tf_op jit(solution)/shard_map/ppermute | solution.py:438
  34.5 4.2 %multiply_sine_fusion = (f32[1536,128]{1,0:T(8,128)}, f32[1536,128]{1,0:T(8,128)}) fusion(f32[128]{0:T(128)S(1)} %mul.48, f32[1536]{0:T(1024)S(1)} %convert_element_type.217), kind=kLoop, calls=%fused_computation.19 | loop fusion | flops 196608 | bytes 1579520 | tf_op jit(solution)/shard_map/sin | solution.py:517
  39.9 5.4 %all-to-all-start = ((bf16[8,24,512]{2,1,0:T(8,128)(2,1)}), bf16[8,24,512]{2,1,0:T(8,128)(2,1)S(1)}, u32[]{:S(2)}, u32[]{:S(2)}) async-start(bf16[8,24,512]{2,1,0:T(8,128)(2,1)} %pad_maximum_fusion.8), calls=%async_computation | async-start | bytes 393216 | tf_op jit(solution)/shard_map/all_to_all | solution.py:551
  46.7 12.6 %collective-permute-done.2.refs_2_ = bf16[264,768]{1,0:T(8,128)(2,1)} collective-permute-done((bf16[264,768]{1,0:T(8,128)(2,1)}, bf16[264,768]{1,0:T(8,128)(2,1)}, u32[]{:S(2)}, u32[]{:S(2)}) %collective-permute-start.2) | collective-permute-done | bytes 405536 | tf_op jit(solution)/shard_map/ppermute | solution.py:444
  62.1 5.7 %collective-permute-done.10 = bf16[4,208,384]{2,1,0:T(8,128)(2,1)} collective-permute-done((bf16[4,208,384]{2,1,0:T(8,128)(2,1)S(1)}, bf16[4,208,384]{2,1,0:T(8,128)(2,1)}, u32[]{:S(2)}, u32[]{:S(2)}) %collective-permute-start.10) | collective-permute-done | bytes 639008 | tf_op jit(solution)/shard_map/ppermute | solution.py:447
  73.9 8.1 %qkv.1 = (bf16[6,256,768]{2,1,0:T(8,128)(2,1)}, bf16[3,6,256,128]{3,2,1,0:T(8,128)(2,1)}, bf16[3,6,256,128]{3,2,1,0:T(8,128)(2,1)}, bf16[3,2,256,128]{3,2,1,0:T(8,128)(2,1)}) custom-call(s32[1]{0:T(128)} %bitcast.c_ref, bf16[264,768]{1,0:T(8,128)(2,1)} %fusion.8.refs_0_, bf16[264,768]{1,0:T(8,128)(2,1)} %collective-permute-done.1.refs_1_, ...), custom_call_target="tpu_custom_call" | custom-call | flops 8800000000 | bytes 800000 | tf_op jit(solution)/shard_map/qkv/pallas_call | solution.py:520
  86.3 10.2 %attend.1 = (f32[3,512,128]{2,1,0:T(8,128)}, bf16[3,512,128]{2,1,0:T(8,128)(2,1)}, f32[3,8,512]{2,1,0:T(8,128)}) custom-call(bf16[3,512,128]{2,1,0:T(8,128)(2,1)} %bitcast.385, bf16[3,1536,128]{2,1,0:T(8,128)(2,1)} %bitcast.381, bf16[3,1536,128]{2,1,0:T(8,128)(2,1)} %bitcast.383, f32[512,128]{1,0:T(8,128)} %broadcast_in_dim.109.sq_ref, f32[1,1536]{1,0:T(1,128)} %bitcast.371), custom_call_target="tpu_custom_call" | custom-call | flops 11000000512 | bytes 1000000 | tf_op jit(solution)/shard_map/attend/pallas_call | solution.py:558
  101.4 3.0 mid.1
  112.3 8.7 %pre.1 = (bf16[1024,2048]{1,0:T(8,128)(2,1)}, bf16[768,1024]{1,0:T(8,128)(2,1)}) custom-call(s32[8]{0:T(128)} %stack.80.ix.ix_s, bf16[8,264,768]{2,1,0:T(8,128)(2,1)} %bitcast.376, bf16[8,128,256]{2,1,0:T(8,128)(2,1)} %compare_convert_fusion.1.p_ref.refs_8_, bf16[2048,768]{1,0:T(8,128)(2,1)} %bitcast.379), custom_call_target="tpu_custom_call" | custom-call | flops 13200000000 | bytes 1200000 | tf_op jit(solution)/shard_map/pre/pallas_call | solution.py:624
  127.4 6.0 %collective-permute-done.17.refs_4_ = bf16[256,768]{1,0:T(8,128)(2,1)S(1)} collective-permute-done((bf16[256,768]{1,0:T(8,128)(2,1)S(1)}, bf16[256,768]{1,0:T(8,128)(2,1)S(1)}, u32[]{:S(2)}, u32[]{:S(2)}) %collective-permute-start.17) | collective-permute-done | bytes 393248 | tf_op jit(solution)/shard_map/ppermute | solution.py:441
  138.6 32.0 %expert.1 = (bf16[1024,768]{1,0:T(8,128)(2,1)}, bf16[2048,768]{1,0:T(8,128)(2,1)}, bf16[1024,2048]{1,0:T(8,128)(2,1)}, bf16[1024,2048]{1,0:T(8,128)(2,1)}, bf16[...) custom-call(s32[1]{0:T(128)} %bitcast.29.e_ref, ...), custom_call_target="tpu_custom_call" | custom-call | flops 41799999488 | bytes 3800000 | tf_op jit(solution)/shard_map/expert/pallas_call | solution.py:652
  170.8 7.2 %dgrad.1 = bf16[768,2048]{1,0:T(8,128)(2,1)} custom-call(bf16[768,1024]{1,0:T(8,128)(2,1)} %get-tuple-element.142.ogx_t, bf16[1024,2048]{1,0:T(8,128)(2,1)} %get-tuple-element.156.ghid), custom_call_target="tpu_custom_call" | custom-call | flops 11000000512 | bytes 1000000 | tf_op jit(solution)/shard_map/dgrad/pallas_call | solution.py:720
  188.1 12.2 %wgrad.1 = (bf16[2,768,512]{2,1,0:T(8,128)(2,1)}, bf16[2,768,512]{2,1,0:T(8,128)(2,1)}, bf16[2,768,512]{2,1,0:T(8,128)(2,1)}, bf16[2,768,512]{2,1,0:T(8,128)(2,1)}) custom-call(s32[1]{0:T(128)} %bitcast.55.r_ref, bf16[1024,768]{1,0:T(8,128)(2,1)} %get-tuple-element.146.x_ref, bf16[1024,2048]{1,0:T(8,128)(2,1)} %get-tuple-element.147.degate, ...), custom_call_target="tpu_custom_call" | custom-call | flops 14300000256 | bytes 1300000 | tf_op jit(solution)/shard_map/wgrad/pallas_call | solution.py:761
  204.4 15.0 %result.1 = (bf16[8,256,768]{2,1,0:T(8,128)(2,1)}, bf16[768,512]{1,0:T(8,128)(2,1)}, bf16[256,768]{1,0:T(8,128)(2,1)}) custom-call(s32[8]{0:T(128)} %stack.80.ix.ix_s, bf16[2048,768]{1,0:T(8,128)(2,1)} %get-tuple-element.150.g_ref, bf16[8,264,768]{2,1,0:T(8,128)(2,1)} %bitcast.378, bf16[8,256,128]{2,1,0:T(8,128)(2,1)} %compare_convert_fusion.refs_9_.pt_ref, ...), custom_call_target="tpu_custom_call" | custom-call | flops 15399999488 | bytes 1400000 | tf_op jit(solution)/shard_map/result/pallas_call | solution.py:790
  222.5 4.5 %collective-permute-done.27 = bf16[768,512]{1,0:T(8,128)(2,1)S(1)} collective-permute-done((bf16[768,512]{1,0:T(8,128)(2,1)S(1)}, bf16[768,512]{1,0:T(8,128)(2,1)S(1)}, u32[]{:S(2)}, u32[]{:S(2)}) %collective-permute-start.27) | collective-permute-done | bytes 786464 | tf_op jit(solution)/shard_map/ppermute | solution.py:447
  227.0 3.3 collective-permute-done.25
  230.3 4.2 %mid_back.1 = (f32[256,768]{1,0:T(8,128)}, bf16[256,768]{1,0:T(8,128)(2,1)}, bf16[6,256,128]{2,1,0:T(8,128)(2,1)}, f32[8,768]{1,0:T(8,128)}) custom-call(bf16[256,768]{1,0:T(8,128)(2,1)} %get-tuple-element.161.refs_0_, bf16[256,768]{1,0:T(8,128)(2,1)} %copy-done.28, bf16[256,768]{1,0:T(8,128)(2,1)} %copy-done.30, bf16[256,768]{1,0:T(8,128)(2,1)} %copy-done.29, ...), custom_call_target="tpu_custom_call" | custom-call | flops 4400000000 | bytes 400000 | tf_op jit(solution)/shard_map/mid_back/pallas_call | solution.py:832
  236.2 4.4 %collective-permute-start.30 = (bf16[3,256,128]{2,1,0:T(8,128)(2,1)}, bf16[3,256,128]{2,1,0:T(8,128)(2,1)}, u32[]{:S(2)}, u32[]{:S(2)}) collective-permute-start(bf16[3,256,128]{2,1,0:T(8,128)(2,1)} %broadcast_select_fusion.5), channel_id=1, source_target_pairs={{0,1},{1,0},{2,3},{3,2},{4,5},{5,4},{6,7},{7,6},{8,9},{9,8},{10,11... | collective-permute-start | bytes 589832 | tf_op jit(solution)/shard_map/ppermute | solution.py:438
  253.6 27.1 %attend_back.1 = (bf16[3,3,768,128]{3,2,1,0:T(8,128)(2,1)}, bf16[3,256,768]{2,1,0:T(8,128)(2,1)}, bf16[3,256,768]{2,1,0:T(8,128)(2,1)}, f32[8,768]{1,0:T(8,128)}) custom-call(bf16[3,512,128]{2,1,0:T(8,128)(2,1)} %bitcast.386, bf16[3,1536,128]{2,1,0:T(8,128)(2,1)} %bitcast.382, bf16[3,1536,128]{2,1,0:T(8,128)(2,1)} %bitcast.384, ...), custom_call_target="tpu_custom_call" | custom-call | flops 32999999488 | bytes 3000000 | tf_op jit(solution)/shard_map/attend_back/pallas_call | solution.py:860
  300.6 7.7 %collective-permute-done.40 = bf16[256,768]{1,0:T(8,128)(2,1)} collective-permute-done((bf16[256,768]{1,0:T(8,128)(2,1)}, bf16[256,768]{1,0:T(8,128)(2,1)}, u32[]{:S(2)}, u32[]{:S(2)}) %collective-permute-start.40) | collective-permute-done | bytes 393248 | tf_op jit(solution)/shard_map/ppermute | solution.py:444
  311.9 4.1 %convert_add_fusion = (f32[768,512]{1,0:T(8,128)}, f32[768,512]{1,0:T(8,128)}) fusion(bf16[768,512]{1,0:T(8,128)(2,1)} %collective-permute-done.34, bf16[768,512]{1,0:T(8,128)(2,1)S(1)} %copy-done.12, bf16[2,768,512]{2,1,0:T(8,128)(2,1)} %get-tuple-element.168, bf16[768,512]{1,0:T(8,128)(2,1)} %collective-permute-done.33, bf16[768,512]{1,0:T(8,128)(2,1)} %copy-done.13, ...), kind=kLoop, calls=%fused_computation.10 | loop fusion | flops 3932160 | bytes 7864320 | tf_op jit(solution)/shard_map/add | solution.py:960
  316.0 4.0 %collective-permute-done.41.refs_1_ = bf16[256,768]{1,0:T(8,128)(2,1)S(1)} collective-permute-done((bf16[256,768]{1,0:T(8,128)(2,1)S(1)}, bf16[256,768]{1,0:T(8,128)(2,1)S(1)}, u32[]{:S(2)}, u32[]{:S(2)}) %collective-permute-start.41) | collective-permute-done | bytes 393248 | tf_op jit(solution)/shard_map/ppermute | solution.py:444
  331.9 5.2 %collective-permute-done.45 = bf16[776,128]{1,0:T(8,128)(2,1)S(1)} collective-permute-done((bf16[776,128]{1,0:T(8,128)(2,1)S(1)}, bf16[776,128]{1,0:T(8,128)(2,1)S(1)}, u32[]{:S(2)}, u32[]{:S(2)}) %collective-permute-start.45) | collective-permute-done | bytes 198688 | tf_op jit(solution)/shard_map/ppermute | solution.py:441
  337.1 5.9 %collective-permute-done.46 = bf16[776,128]{1,0:T(8,128)(2,1)S(1)} collective-permute-done((bf16[776,128]{1,0:T(8,128)(2,1)S(1)}, bf16[776,128]{1,0:T(8,128)(2,1)S(1)}, u32[]{:S(2)}, u32[]{:S(2)}) %collective-permute-start.46) | collective-permute-done | bytes 198688 | tf_op jit(solution)/shard_map/ppermute | solution.py:441
  (361 shorter events, 137.3 us)
Async XLA Ops:
  20.4 40.4 %collective-permute-start.1 = (bf16[264,768]{1,0:T(8,128)(2,1)}, bf16[264,768]{1,0:T(8,128)(2,1)}, u32[]{:S(2)}, u32[]{:S(2)}) collective-permute-start(bf16[264,768]{1,0:T(8,128)(2,1)} %fusion.8.refs_0_), channel_id=1, source_target_pairs={{0,2},{1,3},{2,4},{3,5},{4,6},{5,7},{8,10},{9,11},{10,12},{11,13},... | collective-permute-start | bytes 1216520 | tf_op jit(solution)/shard_map/ppermute | solution.py:444
  22.5 36.8 %collective-permute-start.2 = (bf16[264,768]{1,0:T(8,128)(2,1)}, bf16[264,768]{1,0:T(8,128)(2,1)}, u32[]{:S(2)}, u32[]{:S(2)}) collective-permute-start(bf16[264,768]{1,0:T(8,128)(2,1)} %fusion.8.refs_0_), channel_id=1, source_target_pairs={{0,4},{1,5},{2,6},{3,7},{8,12},{9,13},{10,14},{11,15},{16,20},{17,... | collective-permute-start | bytes 1216520 | tf_op jit(solution)/shard_map/ppermute | solution.py:444
  24.7 21.0 %collective-permute-start.3 = (bf16[264,768]{1,0:T(8,128)(2,1)}, bf16[264,768]{1,0:T(8,128)(2,1)}, u32[]{:S(2)}, u32[]{:S(2)}) collective-permute-start(bf16[264,768]{1,0:T(8,128)(2,1)} %fusion.8.refs_0_), channel_id=1, source_target_pairs={{0,1},{1,0},{2,3},{3,2},{4,5},{5,4},{6,7},{7,6},{8,9},{9,8},{10,11... | collective-permute-start | bytes 1216520 | tf_op jit(solution)/shard_map/ppermute | solution.py:438
  33.2 27.8 %collective-permute-start.9 = (bf16[4,208,384]{2,1,0:T(8,128)(2,1)S(1)}, bf16[4,208,384]{2,1,0:T(8,128)(2,1)}, u32[]{:S(2)}, u32[]{:S(2)}) collective-permute-start(bf16[4,208,384]{2,1,0:T(8,128)(2,1)S(1)} %bitcast_dynamic-update-slice_fusion.8), channel_id=1, source_target_pairs={{0,8},{8,0},{16,24},{24,16},{1,9},{9,1},{17,25},{25,17},{2,10},{10... | collective-permute-start | bytes 1916936 | tf_op jit(solution)/shard_map/ppermute | solution.py:447
  38.7 29.1 %collective-permute-start.10 = (bf16[4,208,384]{2,1,0:T(8,128)(2,1)S(1)}, bf16[4,208,384]{2,1,0:T(8,128)(2,1)}, u32[]{:S(2)}, u32[]{:S(2)}) collective-permute-start(bf16[4,208,384]{2,1,0:T(8,128)(2,1)S(1)} %bitcast_dynamic-update-slice_fusion.8), channel_id=1, source_target_pairs={{0,16},{8,24},{16,0},{24,8},{1,17},{9,25},{17,1},{25,9},{2,18},{10... | collective-permute-start | bytes 1916936 | tf_op jit(solution)/shard_map/ppermute | solution.py:447
  39.9 42.1 %all-to-all-start = ((bf16[8,24,512]{2,1,0:T(8,128)(2,1)}), bf16[8,24,512]{2,1,0:T(8,128)(2,1)S(1)}, u32[]{:S(2)}, u32[]{:S(2)}) async-start(bf16[8,24,512]{2,1,0:T(8,128)(2,1)} %pad_maximum_fusion.8), calls=%async_computation | async-start | bytes 393216 | tf_op jit(solution)/shard_map/all_to_all | solution.py:551
  45.4 60.5 %all-gather.3.cloned.1.call-start = ((), (), s32[]{:S(2)}) async-start(), calls=%async_computation.5 | async-start | bytes 3649536 | tf_op jit(solution)/shard_map/all_gather | solution.py:542
  45.7 23.3 %collective-permute-start.11 = (bf16[4,208,384]{2,1,0:T(8,128)(2,1)S(1)}, bf16[4,208,384]{2,1,0:T(8,128)(2,1)}, u32[]{:S(2)}, u32[]{:S(2)}) collective-permute-start(bf16[4,208,384]{2,1,0:T(8,128)(2,1)S(1)} %bitcast_dynamic-update-slice_fusion.8), channel_id=1, source_target_pairs={{0,24},{8,16},{16,8},{24,0},{1,25},{9,17},{17,9},{25,1},{2,26},{10... | collective-permute-start | bytes 1916936 | tf_op jit(solution)/shard_map/ppermute | solution.py:447
  59.3 265.5 %reduce-scatter.3.cloned.1.call-start = ((), (), s32[]{:S(2)}) async-start(), calls=%async_computation.3 | async-start | bytes 3932160 | tf_op jit(solution)/shard_map/reduce_scatter | solution.py:730
  104.4 21.0 %collective-permute-start.19 = (bf16[256,768]{1,0:T(8,128)(2,1)}, bf16[256,768]{1,0:T(8,128)(2,1)S(1)}, u32[]{:S(2)}, u32[]{:S(2)}) collective-permute-start(bf16[256,768]{1,0:T(8,128)(2,1)} %get-tuple-element.132.refs_0_), channel_id=1, source_target_pairs={{0,6},{1,7},{2,0},{3,1},{4,2},{5,3},{6,4},{7,5},{8,14},{9,15},{10,... | collective-permute-start | bytes 1179656 | tf_op jit(solution)/shard_map/ppermute | solution.py:441
  178.0 149.3 %reduce-scatter.5.cloned.1.call-start = ((), (), s32[]{:S(2)}) async-start(), calls=%async_computation.4 | async-start | bytes 3538944 | tf_op jit(solution)/shard_map/reduce_scatter | solution.py:830
  185.5 33.9 %collective-permute-start.29 = (bf16[256,768]{1,0:T(8,128)(2,1)}, bf16[256,768]{1,0:T(8,128)(2,1)S(1)}, u32[]{:S(2)}, u32[]{:S(2)}) collective-permute-start(bf16[256,768]{1,0:T(8,128)(2,1)} %get-tuple-element.219), channel_id=1, source_target_pairs={{0,2},{1,3},{2,4},{3,5},{4,6},{5,7},{6,0},{7,1},{8,10},{9,11},{10,... | collective-permute-start | bytes 1179656 | tf_op jit(solution)/shard_map/ppermute | solution.py:441
  186.0 33.7 %collective-permute-start.28 = (bf16[256,768]{1,0:T(8,128)(2,1)S(1)}, bf16[256,768]{1,0:T(8,128)(2,1)S(1)}, u32[]{:S(2)}, u32[]{:S(2)}) collective-permute-start(bf16[256,768]{1,0:T(8,128)(2,1)S(1)} %get-tuple-element.220), channel_id=1, source_target_pairs={{0,4},{1,5},{2,6},{3,7},{4,0},{5,1},{6,2},{7,3},{8,12},{9,13},{10,... | collective-permute-start | bytes 1179656 | tf_op jit(solution)/shard_map/ppermute | solution.py:441
  201.9 25.1 %collective-permute-start.27 = (bf16[768,512]{1,0:T(8,128)(2,1)S(1)}, bf16[768,512]{1,0:T(8,128)(2,1)S(1)}, u32[]{:S(2)}, u32[]{:S(2)}) collective-permute-start(bf16[768,512]{1,0:T(8,128)(2,1)S(1)} %get-tuple-element.231), channel_id=1, source_target_pairs={{0,16},{8,24},{16,0},{24,8},{1,17},{9,25},{17,1},{25,9},{2,18},{10... | collective-permute-start | bytes 2359304 | tf_op jit(solution)/shard_map/ppermute | solution.py:447
  204.3 26.0 %collective-permute-start.25 = (bf16[768,512]{1,0:T(8,128)(2,1)S(1)}, bf16[768,512]{1,0:T(8,128)(2,1)S(1)}, u32[]{:S(2)}, u32[]{:S(2)}) collective-permute-start(bf16[768,512]{1,0:T(8,128)(2,1)S(1)} %get-tuple-element.233), channel_id=1, source_target_pairs={{0,8},{8,0},{16,24},{24,16},{1,9},{9,1},{17,25},{25,17},{2,10},{10... | collective-permute-start | bytes 2359304 | tf_op jit(solution)/shard_map/ppermute | solution.py:447
  219.7 28.0 %collective-permute-start.32 = (bf16[768,512]{1,0:T(8,128)(2,1)S(1)}, bf16[768,512]{1,0:T(8,128)(2,1)}, u32[]{:S(2)}, u32[]{:S(2)}) collective-permute-start(bf16[768,512]{1,0:T(8,128)(2,1)S(1)} %get-tuple-element.169), channel_id=1, source_target_pairs={{0,16},{8,24},{16,0},{24,8},{1,17},{9,25},{17,1},{25,9},{2,18},{10... | collective-permute-start | bytes 2359304 | tf_op jit(solution)/shard_map/ppermute | solution.py:447
  221.0 26.7 %collective-permute-start.31 = (bf16[768,512]{1,0:T(8,128)(2,1)}, bf16[768,512]{1,0:T(8,128)(2,1)}, u32[]{:S(2)}, u32[]{:S(2)}) collective-permute-start(bf16[768,512]{1,0:T(8,128)(2,1)} %get-tuple-element.166), channel_id=1, source_target_pairs={{0,8},{8,0},{16,24},{24,16},{1,9},{9,1},{17,25},{25,17},{2,10},{10... | collective-permute-start | bytes 2359304 | tf_op jit(solution)/shard_map/ppermute | solution.py:447
  243.0 38.6 %collective-permute-start.35 = (bf16[768,384]{1,0:T(8,128)(2,1)}, bf16[768,384]{1,0:T(8,128)(2,1)}, u32[]{:S(2)}, u32[]{:S(2)}) collective-permute-start(bf16[768,384]{1,0:T(8,128)(2,1)} %broadcast_select_fusion), channel_id=1, source_target_pairs={{0,1},{1,0},{2,3},{3,2},{4,5},{5,4},{6,7},{7,6},{8,9},{9,8},{10,11... | collective-permute-start | bytes 1769480 | tf_op jit(solution)/shard_map/ppermute | solution.py:438
  247.5 34.0 %collective-permute-start.36 = (bf16[2,576,256]{2,1,0:T(8,128)(2,1)}, bf16[2,576,256]{2,1,0:T(8,128)(2,1)}, u32[]{:S(2)}, u32[]{:S(2)}) collective-permute-start(bf16[2,576,256]{2,1,0:T(8,128)(2,1)} %pad_maximum_fusion.4), channel_id=1, source_target_pairs={{0,16},{8,24},{16,0},{24,8},{1,17},{9,25},{17,1},{25,9},{2,18},{10... | collective-permute-start | bytes 1769480 | tf_op jit(solution)/shard_map/ppermute | solution.py:447
  251.1 30.5 %collective-permute-start.34 = (bf16[768,512]{1,0:T(8,128)(2,1)}, bf16[768,512]{1,0:T(8,128)(2,1)}, u32[]{:S(2)}, u32[]{:S(2)}) collective-permute-start(bf16[768,512]{1,0:T(8,128)(2,1)} %bitcast_add_fusion), channel_id=1, source_target_pairs={{0,8},{8,0},{16,24},{24,16},{1,9},{9,1},{17,25},{25,17},{2,10},{10... | collective-permute-start | bytes 2359304 | tf_op jit(solution)/shard_map/ppermute | solution.py:447
  251.1 30.5 %collective-permute-start.33 = (bf16[768,512]{1,0:T(8,128)(2,1)S(1)}, bf16[768,512]{1,0:T(8,128)(2,1)}, u32[]{:S(2)}, u32[]{:S(2)}) collective-permute-start(bf16[768,512]{1,0:T(8,128)(2,1)S(1)} %bitcast_add_fusion.1), channel_id=1, source_target_pairs={{0,16},{8,24},{16,0},{24,8},{1,17},{9,25},{17,1},{25,9},{2,18},{10... | collective-permute-start | bytes 2359304 | tf_op jit(solution)/shard_map/ppermute | solution.py:447
  291.2 24.8 %collective-permute-start.39 = (bf16[4,584,128]{2,1,0:T(8,128)(2,1)}, bf16[4,584,128]{2,1,0:T(8,128)(2,1)}, u32[]{:S(2)}, u32[]{:S(2)}) collective-permute-start(bf16[4,584,128]{2,1,0:T(8,128)(2,1)} %get-tuple-element.227), channel_id=1, source_target_pairs={{0,8},{8,0},{16,24},{24,16},{1,9},{9,1},{17,25},{25,17},{2,10},{10... | collective-permute-start | bytes 1794056 | tf_op jit(solution)/shard_map/ppermute | solution.py:447
  291.4 28.7 %collective-permute-start.42 = (bf16[4,584,128]{2,1,0:T(8,128)(2,1)}, bf16[4,584,128]{2,1,0:T(8,128)(2,1)}, u32[]{:S(2)}, u32[]{:S(2)}) collective-permute-start(bf16[4,584,128]{2,1,0:T(8,128)(2,1)} %get-tuple-element.229), channel_id=1, source_target_pairs={{0,16},{8,24},{16,0},{24,8},{1,17},{9,25},{17,1},{25,9},{2,18},{10... | collective-permute-start | bytes 1794056 | tf_op jit(solution)/shard_map/ppermute | solution.py:447
  292.5 27.6 %collective-permute-start.43 = (bf16[4,584,128]{2,1,0:T(8,128)(2,1)}, bf16[4,584,128]{2,1,0:T(8,128)(2,1)}, u32[]{:S(2)}, u32[]{:S(2)}) collective-permute-start(bf16[4,584,128]{2,1,0:T(8,128)(2,1)} %get-tuple-element.228), channel_id=1, source_target_pairs={{0,24},{8,16},{16,8},{24,0},{1,25},{9,17},{17,9},{25,1},{2,26},{10... | collective-permute-start | bytes 1794056 | tf_op jit(solution)/shard_map/ppermute | solution.py:447
  (65 other events, 528.7 us)
Sparse Core Ops, SparseCore 0:
  59.4 40.9 all-gather.2
  178.1 52.8 reduce-scatter.2
  244.0 35.8 reduce-scatter.4

commit v6 on v5

--- a/solution.py
+++ b/solution.py
@@ -496,7 +496,9 @@
 
     seg_row = jnp.pad(segment_ids.reshape(1, T).astype(BF), ((0, 7), (0, D - T)))
     tok_pack = after(jnp.concatenate([tokens, seg_row], axis=0), pack)
-    own_tok = [tok_pack] + [line(tok_pack, s) for s in range(1, chips)]
+    own_tok = [tok_pack]
+    for s in range(1, chips):
+        own_tok.append(line(own_tok[-1], 1))
     par_tok = [swap(x) for x in own_tok]
 
     seg_blocks = [None] * kvb

time: 362 us -> 364 us (level)
  waiting for transfers between devices: 62.9 us -> 67.4 us
    ppermute x12, waiting for transfers between devices: 23.9 us -> 30.9 us  [ring(): return lax.ppermute(x, 'ep', [(i, (i + 2 * s) % E) for i in range(E)])]
    ppermute x4, waiting for transfers between devices: 24.3 us -> 18.8 us  [line(): lax.ppermute(x, 'ep', [(i, i + 2 * s) for i in range(E) if 0 <= i + 2 * s...]
    ppermute x15, starting transfers between devices: 18.1 us -> 14.3 us  [swap(): return lax.ppermute(x, 'ep', [(i, i ^ 1) for i in range(E)])]
  transfers between devices with their start and end apart: 52 -> 52, of which waited for: 15 -> 16; matrix products, arithmetic and copies ran while one was open for 22% -> 21% of each run, Pallas kernels for 28% -> 27%
where the time goes in v6:
time: 364 us; the launch traced here: 359 us
  Pallas kernels  130 us (36%)
  waiting for transfers between devices  67.4 us (19%)
  starting transfers between devices  57 us (16%)
  other arithmetic  48 us (13%)
  local copies, waits for them, and re-layouts  39.2 us (11%)
  between operations  15.3 us (4%)
    pallas_call x1, Pallas kernels, shards(): pl.pallas_call(functools.partial(expert_kernel, E, T, experts), grid=(ste...  32 us
    ppermute x12, waiting for transfers between devices, ring(): return lax.ppermute(x, 'ep', [(i, (i + 2 * s) % E) for i in range(E)])  30.9 us
    pallas_call x1, Pallas kernels, shards(): pl.pallas_call(functools.partial(attend_back_kernel, first, count, T), gr...  27.1 us
    ppermute x4, waiting for transfers between devices, line(): lax.ppermute(x, 'ep', [(i, i + 2 * s) for i in range(E) if 0 <= i + 2 * s...  18.8 us
    ppermute x17, waiting for transfers between devices, cross(): return lax.ppermute(x, 'rep', [(i, i ^ s) for i in range(R)])  16.5 us
    pallas_call x1, Pallas kernels, shards(): pl.pallas_call(functools.partial(result_kernel, E, T), grid=(steps,), in_...  14.8 us
    ppermute x15, starting transfers between devices, swap(): return lax.ppermute(x, 'ep', [(i, i ^ 1) for i in range(E)])  14.3 us
    ppermute x17, starting transfers between devices, cross(): return lax.ppermute(x, 'rep', [(i, i ^ s) for i in range(R)])  13.7 us
  transfers between devices with their start and end apart: 52, of which 16 were waited for; matrix products, arithmetic and copies ran while one was open for 21% of the time, Pallas kernels for 27%

profile of v6, /device:TPU:9, one launch (start us, length us, event | category | flops | bytes accessed | tf_op | source)
XLA Modules:
  0.0 358.6 jit_solution(7887372093775481494)
XLA Ops:
  23.6 7.4 %collective-permute-done.7 = bf16[208,384]{1,0:T(8,128)(2,1)S(1)} collective-permute-done((bf16[208,384]{1,0:T(8,128)(2,1)S(1)}, bf16[208,384]{1,0:T(8,128)(2,1)S(1)}, u32[]{:S(2)}, u32[]{:S(2)}) %collective-permute-start.7) | collective-permute-done | bytes 159776 | tf_op jit(solution)/shard_map/ppermute | solution.py:441
  34.5 4.2 %multiply_sine_fusion = (f32[1536,128]{1,0:T(8,128)}, f32[1536,128]{1,0:T(8,128)}) fusion(f32[128]{0:T(128)S(1)} %mul.48, f32[1536]{0:T(1024)S(1)} %convert_element_type.217), kind=kLoop, calls=%fused_computation.19 | loop fusion | flops 196608 | bytes 1579520 | tf_op jit(solution)/shard_map/sin | solution.py:519
  40.1 5.7 %all-to-all-start = ((bf16[8,24,512]{2,1,0:T(8,128)(2,1)}), bf16[8,24,512]{2,1,0:T(8,128)(2,1)S(1)}, u32[]{:S(2)}, u32[]{:S(2)}) async-start(bf16[8,24,512]{2,1,0:T(8,128)(2,1)} %pad_maximum_fusion.8), calls=%async_computation | async-start | bytes 393216 | tf_op jit(solution)/shard_map/all_to_all | solution.py:553
  46.2 3.1 collective-permute-start.2
  52.0 7.1 %collective-permute-done.2.refs_2_ = bf16[264,768]{1,0:T(8,128)(2,1)} collective-permute-done((bf16[264,768]{1,0:T(8,128)(2,1)}, bf16[264,768]{1,0:T(8,128)(2,1)}, u32[]{:S(2)}, u32[]{:S(2)}) %collective-permute-start.2) | collective-permute-done | bytes 405536 | tf_op jit(solution)/shard_map/ppermute | solution.py:444
  59.3 8.5 %collective-permute-done.10 = bf16[4,208,384]{2,1,0:T(8,128)(2,1)} collective-permute-done((bf16[4,208,384]{2,1,0:T(8,128)(2,1)S(1)}, bf16[4,208,384]{2,1,0:T(8,128)(2,1)}, u32[]{:S(2)}, u32[]{:S(2)}) %collective-permute-start.10) | collective-permute-done | bytes 639008 | tf_op jit(solution)/shard_map/ppermute | solution.py:447
  75.3 8.1 %qkv.1 = (bf16[6,256,768]{2,1,0:T(8,128)(2,1)}, bf16[3,6,256,128]{3,2,1,0:T(8,128)(2,1)}, bf16[3,6,256,128]{3,2,1,0:T(8,128)(2,1)}, bf16[3,2,256,128]{3,2,1,0:T(8,128)(2,1)}) custom-call(s32[1]{0:T(128)} %bitcast.c_ref, bf16[264,768]{1,0:T(8,128)(2,1)} %fusion.8.refs_0_, bf16[264,768]{1,0:T(8,128)(2,1)} %collective-permute-done.1.refs_1_, ...), custom_call_target="tpu_custom_call" | custom-call | flops 8800000000 | bytes 800000 | tf_op jit(solution)/shard_map/qkv/pallas_call | solution.py:522
  87.0 10.2 %attend.1 = (f32[3,512,128]{2,1,0:T(8,128)}, bf16[3,512,128]{2,1,0:T(8,128)(2,1)}, f32[3,8,512]{2,1,0:T(8,128)}) custom-call(bf16[3,512,128]{2,1,0:T(8,128)(2,1)} %bitcast.385, bf16[3,1536,128]{2,1,0:T(8,128)(2,1)} %bitcast.381, bf16[3,1536,128]{2,1,0:T(8,128)(2,1)} %bitcast.383, f32[512,128]{1,0:T(8,128)} %broadcast_in_dim.109.sq_ref, f32[1,1536]{1,0:T(1,128)} %bitcast.371), custom_call_target="tpu_custom_call" | custom-call | flops 11000000512 | bytes 1000000 | tf_op jit(solution)/shard_map/attend/pallas_call | solution.py:560
  102.6 3.0 mid.1
  113.4 8.7 %pre.1 = (bf16[1024,2048]{1,0:T(8,128)(2,1)}, bf16[768,1024]{1,0:T(8,128)(2,1)}) custom-call(s32[8]{0:T(128)} %stack.80.ix.ix_s, bf16[8,264,768]{2,1,0:T(8,128)(2,1)} %bitcast.376, bf16[8,128,256]{2,1,0:T(8,128)(2,1)} %compare_convert_fusion.1.p_ref.refs_8_, bf16[2048,768]{1,0:T(8,128)(2,1)} %bitcast.379), custom_call_target="tpu_custom_call" | custom-call | flops 13200000000 | bytes 1200000 | tf_op jit(solution)/shard_map/pre/pallas_call | solution.py:626
  128.5 7.2 %collective-permute-done.17.refs_4_ = bf16[256,768]{1,0:T(8,128)(2,1)S(1)} collective-permute-done((bf16[256,768]{1,0:T(8,128)(2,1)S(1)}, bf16[256,768]{1,0:T(8,128)(2,1)S(1)}, u32[]{:S(2)}, u32[]{:S(2)}) %collective-permute-start.17) | collective-permute-done | bytes 393248 | tf_op jit(solution)/shard_map/ppermute | solution.py:441
  140.4 32.0 %expert.1 = (bf16[1024,768]{1,0:T(8,128)(2,1)}, bf16[2048,768]{1,0:T(8,128)(2,1)}, bf16[1024,2048]{1,0:T(8,128)(2,1)}, bf16[1024,2048]{1,0:T(8,128)(2,1)}, bf16[...) custom-call(s32[1]{0:T(128)} %bitcast.29.e_ref, ...), custom_call_target="tpu_custom_call" | custom-call | flops 41799999488 | bytes 3800000 | tf_op jit(solution)/shard_map/expert/pallas_call | solution.py:654
  172.5 7.2 %dgrad.1 = bf16[768,2048]{1,0:T(8,128)(2,1)} custom-call(bf16[768,1024]{1,0:T(8,128)(2,1)} %get-tuple-element.142.ogx_t, bf16[1024,2048]{1,0:T(8,128)(2,1)} %get-tuple-element.156.ghid), custom_call_target="tpu_custom_call" | custom-call | flops 11000000512 | bytes 1000000 | tf_op jit(solution)/shard_map/dgrad/pallas_call | solution.py:722
  189.9 12.1 %wgrad.1 = (bf16[2,768,512]{2,1,0:T(8,128)(2,1)}, bf16[2,768,512]{2,1,0:T(8,128)(2,1)}, bf16[2,768,512]{2,1,0:T(8,128)(2,1)}, bf16[2,768,512]{2,1,0:T(8,128)(2,1)}) custom-call(s32[1]{0:T(128)} %bitcast.55.r_ref, bf16[1024,768]{1,0:T(8,128)(2,1)} %get-tuple-element.146.x_ref, bf16[1024,2048]{1,0:T(8,128)(2,1)} %get-tuple-element.147.degate, ...), custom_call_target="tpu_custom_call" | custom-call | flops 14300000256 | bytes 1300000 | tf_op jit(solution)/shard_map/wgrad/pallas_call | solution.py:763
  206.0 14.8 %result.1 = (bf16[8,256,768]{2,1,0:T(8,128)(2,1)}, bf16[768,512]{1,0:T(8,128)(2,1)}, bf16[256,768]{1,0:T(8,128)(2,1)}) custom-call(s32[8]{0:T(128)} %stack.80.ix.ix_s, bf16[2048,768]{1,0:T(8,128)(2,1)} %get-tuple-element.150.g_ref, bf16[8,264,768]{2,1,0:T(8,128)(2,1)} %bitcast.378, bf16[8,256,128]{2,1,0:T(8,128)(2,1)} %compare_convert_fusion.refs_9_.pt_ref, ...), custom_call_target="tpu_custom_call" | custom-call | flops 15399999488 | bytes 1400000 | tf_op jit(solution)/shard_map/result/pallas_call | solution.py:792
  224.2 5.1 %collective-permute-done.27 = bf16[768,512]{1,0:T(8,128)(2,1)S(1)} collective-permute-done((bf16[768,512]{1,0:T(8,128)(2,1)S(1)}, bf16[768,512]{1,0:T(8,128)(2,1)S(1)}, u32[]{:S(2)}, u32[]{:S(2)}) %collective-permute-start.27) | collective-permute-done | bytes 786464 | tf_op jit(solution)/shard_map/ppermute | solution.py:447
  231.9 4.2 %mid_back.1 = (f32[256,768]{1,0:T(8,128)}, bf16[256,768]{1,0:T(8,128)(2,1)}, bf16[6,256,128]{2,1,0:T(8,128)(2,1)}, f32[8,768]{1,0:T(8,128)}) custom-call(bf16[256,768]{1,0:T(8,128)(2,1)} %get-tuple-element.161.refs_0_, bf16[256,768]{1,0:T(8,128)(2,1)} %copy-done.29, bf16[256,768]{1,0:T(8,128)(2,1)} %copy-done.31, bf16[256,768]{1,0:T(8,128)(2,1)} %copy-done.30, ...), custom_call_target="tpu_custom_call" | custom-call | flops 4400000000 | bytes 400000 | tf_op jit(solution)/shard_map/mid_back/pallas_call | solution.py:834
  237.8 4.0 %collective-permute-start.30 = (bf16[3,256,128]{2,1,0:T(8,128)(2,1)}, bf16[3,256,128]{2,1,0:T(8,128)(2,1)}, u32[]{:S(2)}, u32[]{:S(2)}) collective-permute-start(bf16[3,256,128]{2,1,0:T(8,128)(2,1)} %broadcast_select_fusion.5), channel_id=1, source_target_pairs={{0,1},{1,0},{2,3},{3,2},{4,5},{5,4},{6,7},{7,6},{8,9},{9,8},{10,11... | collective-permute-start | bytes 589832 | tf_op jit(solution)/shard_map/ppermute | solution.py:438
  255.0 27.1 %attend_back.1 = (bf16[3,3,768,128]{3,2,1,0:T(8,128)(2,1)}, bf16[3,256,768]{2,1,0:T(8,128)(2,1)}, bf16[3,256,768]{2,1,0:T(8,128)(2,1)}, f32[8,768]{1,0:T(8,128)}) custom-call(bf16[3,512,128]{2,1,0:T(8,128)(2,1)} %bitcast.386, bf16[3,1536,128]{2,1,0:T(8,128)(2,1)} %bitcast.382, bf16[3,1536,128]{2,1,0:T(8,128)(2,1)} %bitcast.384, ...), custom_call_target="tpu_custom_call" | custom-call | flops 32999999488 | bytes 3000000 | tf_op jit(solution)/shard_map/attend_back/pallas_call | solution.py:862
  302.3 7.7 %collective-permute-done.40 = bf16[256,768]{1,0:T(8,128)(2,1)} collective-permute-done((bf16[256,768]{1,0:T(8,128)(2,1)}, bf16[256,768]{1,0:T(8,128)(2,1)}, u32[]{:S(2)}, u32[]{:S(2)}) %collective-permute-start.40) | collective-permute-done | bytes 393248 | tf_op jit(solution)/shard_map/ppermute | solution.py:444
  313.6 4.1 %convert_add_fusion = (f32[768,512]{1,0:T(8,128)}, f32[768,512]{1,0:T(8,128)}) fusion(bf16[768,512]{1,0:T(8,128)(2,1)} %collective-permute-done.34, bf16[768,512]{1,0:T(8,128)(2,1)S(1)} %copy-done.12, bf16[2,768,512]{2,1,0:T(8,128)(2,1)} %get-tuple-element.168, bf16[768,512]{1,0:T(8,128)(2,1)} %collective-permute-done.33, bf16[768,512]{1,0:T(8,128)(2,1)} %copy-done.13, ...), kind=kLoop, calls=%fused_computation.10 | loop fusion | flops 3932160 | bytes 7864320 | tf_op jit(solution)/shard_map/add | solution.py:962
  317.7 4.1 %collective-permute-done.41.refs_1_ = bf16[256,768]{1,0:T(8,128)(2,1)S(1)} collective-permute-done((bf16[256,768]{1,0:T(8,128)(2,1)S(1)}, bf16[256,768]{1,0:T(8,128)(2,1)S(1)}, u32[]{:S(2)}, u32[]{:S(2)}) %collective-permute-start.41) | collective-permute-done | bytes 393248 | tf_op jit(solution)/shard_map/ppermute | solution.py:444
  333.5 5.7 %collective-permute-done.45 = bf16[776,128]{1,0:T(8,128)(2,1)S(1)} collective-permute-done((bf16[776,128]{1,0:T(8,128)(2,1)S(1)}, bf16[776,128]{1,0:T(8,128)(2,1)S(1)}, u32[]{:S(2)}, u32[]{:S(2)}) %collective-permute-start.45) | collective-permute-done | bytes 198688 | tf_op jit(solution)/shard_map/ppermute | solution.py:441
  339.2 5.4 %collective-permute-done.46 = bf16[776,128]{1,0:T(8,128)(2,1)S(1)} collective-permute-done((bf16[776,128]{1,0:T(8,128)(2,1)S(1)}, bf16[776,128]{1,0:T(8,128)(2,1)S(1)}, u32[]{:S(2)}, u32[]{:S(2)}) %collective-permute-start.46) | collective-permute-done | bytes 198688 | tf_op jit(solution)/shard_map/ppermute | solution.py:441
  (363 shorter events, 136.6 us)
Async XLA Ops:
  20.4 25.8 %collective-permute-start.1 = (bf16[264,768]{1,0:T(8,128)(2,1)}, bf16[264,768]{1,0:T(8,128)(2,1)}, u32[]{:S(2)}, u32[]{:S(2)}) collective-permute-start(bf16[264,768]{1,0:T(8,128)(2,1)} %fusion.8.refs_0_), channel_id=1, source_target_pairs={{0,2},{1,3},{2,4},{3,5},{4,6},{5,7},{8,10},{9,11},{10,12},{11,13},... | collective-permute-start | bytes 1216520 | tf_op jit(solution)/shard_map/ppermute | solution.py:444
  22.5 26.8 %collective-permute-start.3 = (bf16[264,768]{1,0:T(8,128)(2,1)}, bf16[264,768]{1,0:T(8,128)(2,1)}, u32[]{:S(2)}, u32[]{:S(2)}) collective-permute-start(bf16[264,768]{1,0:T(8,128)(2,1)} %fusion.8.refs_0_), channel_id=1, source_target_pairs={{0,1},{1,0},{2,3},{3,2},{4,5},{5,4},{6,7},{7,6},{8,9},{9,8},{10,11... | collective-permute-start | bytes 1216520 | tf_op jit(solution)/shard_map/ppermute | solution.py:438
  38.7 29.1 %collective-permute-start.10 = (bf16[4,208,384]{2,1,0:T(8,128)(2,1)S(1)}, bf16[4,208,384]{2,1,0:T(8,128)(2,1)}, u32[]{:S(2)}, u32[]{:S(2)}) collective-permute-start(bf16[4,208,384]{2,1,0:T(8,128)(2,1)S(1)} %bitcast_dynamic-update-slice_fusion.8), channel_id=1, source_target_pairs={{0,16},{8,24},{16,0},{24,8},{1,17},{9,25},{17,1},{25,9},{2,18},{10... | collective-permute-start | bytes 1916936 | tf_op jit(solution)/shard_map/ppermute | solution.py:447
  39.9 29.1 %collective-permute-start.11 = (bf16[4,208,384]{2,1,0:T(8,128)(2,1)S(1)}, bf16[4,208,384]{2,1,0:T(8,128)(2,1)}, u32[]{:S(2)}, u32[]{:S(2)}) collective-permute-start(bf16[4,208,384]{2,1,0:T(8,128)(2,1)S(1)} %bitcast_dynamic-update-slice_fusion.8), channel_id=1, source_target_pairs={{0,24},{8,16},{16,8},{24,0},{1,25},{9,17},{17,9},{25,1},{2,26},{10... | collective-permute-start | bytes 1916936 | tf_op jit(solution)/shard_map/ppermute | solution.py:447
  40.1 43.3 %all-to-all-start = ((bf16[8,24,512]{2,1,0:T(8,128)(2,1)}), bf16[8,24,512]{2,1,0:T(8,128)(2,1)S(1)}, u32[]{:S(2)}, u32[]{:S(2)}) async-start(bf16[8,24,512]{2,1,0:T(8,128)(2,1)} %pad_maximum_fusion.8), calls=%async_computation | async-start | bytes 393216 | tf_op jit(solution)/shard_map/all_to_all | solution.py:553
  45.8 61.2 %all-gather.3.cloned.1.call-start = ((), (), s32[]{:S(2)}) async-start(), calls=%async_computation.5 | async-start | bytes 3649536 | tf_op jit(solution)/shard_map/all_gather | solution.py:544
  50.0 23.8 %collective-permute-start.4 = (bf16[264,768]{1,0:T(8,128)(2,1)}, bf16[264,768]{1,0:T(8,128)(2,1)}, u32[]{:S(2)}, u32[]{:S(2)}) collective-permute-start(bf16[264,768]{1,0:T(8,128)(2,1)} %collective-permute-done.1.refs_1_), channel_id=1, source_target_pairs={{0,1},{1,0},{2,3},{3,2},{4,5},{5,4},{6,7},{7,6},{8,9},{9,8},{10,11... | collective-permute-start | bytes 1216520 | tf_op jit(solution)/shard_map/ppermute | solution.py:438
  59.0 267.4 %reduce-scatter.3.cloned.1.call-start = ((), (), s32[]{:S(2)}) async-start(), calls=%async_computation.3 | async-start | bytes 3932160 | tf_op jit(solution)/shard_map/reduce_scatter | solution.py:732
  105.6 21.0 %collective-permute-start.19 = (bf16[256,768]{1,0:T(8,128)(2,1)}, bf16[256,768]{1,0:T(8,128)(2,1)S(1)}, u32[]{:S(2)}, u32[]{:S(2)}) collective-permute-start(bf16[256,768]{1,0:T(8,128)(2,1)} %get-tuple-element.132.refs_0_), channel_id=1, source_target_pairs={{0,6},{1,7},{2,0},{3,1},{4,2},{5,3},{6,4},{7,5},{8,14},{9,15},{10,... | collective-permute-start | bytes 1179656 | tf_op jit(solution)/shard_map/ppermute | solution.py:441
  179.8 149.1 %reduce-scatter.5.cloned.1.call-start = ((), (), s32[]{:S(2)}) async-start(), calls=%async_computation.4 | async-start | bytes 3538944 | tf_op jit(solution)/shard_map/reduce_scatter | solution.py:832
  185.2 20.8 %collective-permute-start.26 = (bf16[256,768]{1,0:T(8,128)(2,1)}, bf16[256,768]{1,0:T(8,128)(2,1)S(1)}, u32[]{:S(2)}, u32[]{:S(2)}) collective-permute-start(bf16[256,768]{1,0:T(8,128)(2,1)} %get-tuple-element.221), channel_id=1, source_target_pairs={{0,6},{1,7},{2,0},{3,1},{4,2},{5,3},{6,4},{7,5},{8,14},{9,15},{10,... | collective-permute-start | bytes 1179656 | tf_op jit(solution)/shard_map/ppermute | solution.py:441
  187.4 33.4 %collective-permute-start.29 = (bf16[256,768]{1,0:T(8,128)(2,1)}, bf16[256,768]{1,0:T(8,128)(2,1)S(1)}, u32[]{:S(2)}, u32[]{:S(2)}) collective-permute-start(bf16[256,768]{1,0:T(8,128)(2,1)} %get-tuple-element.219), channel_id=1, source_target_pairs={{0,2},{1,3},{2,4},{3,5},{4,6},{5,7},{6,0},{7,1},{8,10},{9,11},{10,... | collective-permute-start | bytes 1179656 | tf_op jit(solution)/shard_map/ppermute | solution.py:441
  187.8 33.6 %collective-permute-start.28 = (bf16[256,768]{1,0:T(8,128)(2,1)S(1)}, bf16[256,768]{1,0:T(8,128)(2,1)S(1)}, u32[]{:S(2)}, u32[]{:S(2)}) collective-permute-start(bf16[256,768]{1,0:T(8,128)(2,1)S(1)} %get-tuple-element.220), channel_id=1, source_target_pairs={{0,4},{1,5},{2,6},{3,7},{4,0},{5,1},{6,2},{7,3},{8,12},{9,13},{10,... | collective-permute-start | bytes 1179656 | tf_op jit(solution)/shard_map/ppermute | solution.py:441
  203.6 25.7 %collective-permute-start.27 = (bf16[768,512]{1,0:T(8,128)(2,1)S(1)}, bf16[768,512]{1,0:T(8,128)(2,1)S(1)}, u32[]{:S(2)}, u32[]{:S(2)}) collective-permute-start(bf16[768,512]{1,0:T(8,128)(2,1)S(1)} %get-tuple-element.231), channel_id=1, source_target_pairs={{0,16},{8,24},{16,0},{24,8},{1,17},{9,25},{17,1},{25,9},{2,18},{10... | collective-permute-start | bytes 2359304 | tf_op jit(solution)/shard_map/ppermute | solution.py:447
  205.7 26.2 %collective-permute-start.25 = (bf16[768,512]{1,0:T(8,128)(2,1)S(1)}, bf16[768,512]{1,0:T(8,128)(2,1)S(1)}, u32[]{:S(2)}, u32[]{:S(2)}) collective-permute-start(bf16[768,512]{1,0:T(8,128)(2,1)S(1)} %get-tuple-element.233), channel_id=1, source_target_pairs={{0,8},{8,0},{16,24},{24,16},{1,9},{9,1},{17,25},{25,17},{2,10},{10... | collective-permute-start | bytes 2359304 | tf_op jit(solution)/shard_map/ppermute | solution.py:447
  221.4 27.9 %collective-permute-start.32 = (bf16[768,512]{1,0:T(8,128)(2,1)S(1)}, bf16[768,512]{1,0:T(8,128)(2,1)}, u32[]{:S(2)}, u32[]{:S(2)}) collective-permute-start(bf16[768,512]{1,0:T(8,128)(2,1)S(1)} %get-tuple-element.169), channel_id=1, source_target_pairs={{0,16},{8,24},{16,0},{24,8},{1,17},{9,25},{17,1},{25,9},{2,18},{10... | collective-permute-start | bytes 2359304 | tf_op jit(solution)/shard_map/ppermute | solution.py:447
  222.4 26.9 %collective-permute-start.31 = (bf16[768,512]{1,0:T(8,128)(2,1)}, bf16[768,512]{1,0:T(8,128)(2,1)}, u32[]{:S(2)}, u32[]{:S(2)}) collective-permute-start(bf16[768,512]{1,0:T(8,128)(2,1)} %get-tuple-element.166), channel_id=1, source_target_pairs={{0,8},{8,0},{16,24},{24,16},{1,9},{9,1},{17,25},{25,17},{2,10},{10... | collective-permute-start | bytes 2359304 | tf_op jit(solution)/shard_map/ppermute | solution.py:447
  244.2 38.8 %collective-permute-start.35 = (bf16[768,384]{1,0:T(8,128)(2,1)}, bf16[768,384]{1,0:T(8,128)(2,1)}, u32[]{:S(2)}, u32[]{:S(2)}) collective-permute-start(bf16[768,384]{1,0:T(8,128)(2,1)} %broadcast_select_fusion), channel_id=1, source_target_pairs={{0,1},{1,0},{2,3},{3,2},{4,5},{5,4},{6,7},{7,6},{8,9},{9,8},{10,11... | collective-permute-start | bytes 1769480 | tf_op jit(solution)/shard_map/ppermute | solution.py:438
  248.7 34.3 %collective-permute-start.36 = (bf16[2,576,256]{2,1,0:T(8,128)(2,1)}, bf16[2,576,256]{2,1,0:T(8,128)(2,1)}, u32[]{:S(2)}, u32[]{:S(2)}) collective-permute-start(bf16[2,576,256]{2,1,0:T(8,128)(2,1)} %pad_maximum_fusion.4), channel_id=1, source_target_pairs={{0,16},{8,24},{16,0},{24,8},{1,17},{9,25},{17,1},{25,9},{2,18},{10... | collective-permute-start | bytes 1769480 | tf_op jit(solution)/shard_map/ppermute | solution.py:447
  252.7 30.3 %collective-permute-start.34 = (bf16[768,512]{1,0:T(8,128)(2,1)}, bf16[768,512]{1,0:T(8,128)(2,1)}, u32[]{:S(2)}, u32[]{:S(2)}) collective-permute-start(bf16[768,512]{1,0:T(8,128)(2,1)} %bitcast_add_fusion), channel_id=1, source_target_pairs={{0,8},{8,0},{16,24},{24,16},{1,9},{9,1},{17,25},{25,17},{2,10},{10... | collective-permute-start | bytes 2359304 | tf_op jit(solution)/shard_map/ppermute | solution.py:447
  252.7 30.3 %collective-permute-start.33 = (bf16[768,512]{1,0:T(8,128)(2,1)S(1)}, bf16[768,512]{1,0:T(8,128)(2,1)}, u32[]{:S(2)}, u32[]{:S(2)}) collective-permute-start(bf16[768,512]{1,0:T(8,128)(2,1)S(1)} %bitcast_add_fusion.1), channel_id=1, source_target_pairs={{0,16},{8,24},{16,0},{24,8},{1,17},{9,25},{17,1},{25,9},{2,18},{10... | collective-permute-start | bytes 2359304 | tf_op jit(solution)/shard_map/ppermute | solution.py:447
  292.8 24.9 %collective-permute-start.39 = (bf16[4,584,128]{2,1,0:T(8,128)(2,1)}, bf16[4,584,128]{2,1,0:T(8,128)(2,1)}, u32[]{:S(2)}, u32[]{:S(2)}) collective-permute-start(bf16[4,584,128]{2,1,0:T(8,128)(2,1)} %get-tuple-element.227), channel_id=1, source_target_pairs={{0,8},{8,0},{16,24},{24,16},{1,9},{9,1},{17,25},{25,17},{2,10},{10... | collective-permute-start | bytes 1794056 | tf_op jit(solution)/shard_map/ppermute | solution.py:447
  293.0 28.8 %collective-permute-start.42 = (bf16[4,584,128]{2,1,0:T(8,128)(2,1)}, bf16[4,584,128]{2,1,0:T(8,128)(2,1)}, u32[]{:S(2)}, u32[]{:S(2)}) collective-permute-start(bf16[4,584,128]{2,1,0:T(8,128)(2,1)} %get-tuple-element.229), channel_id=1, source_target_pairs={{0,16},{8,24},{16,0},{24,8},{1,17},{9,25},{17,1},{25,9},{2,18},{10... | collective-permute-start | bytes 1794056 | tf_op jit(solution)/shard_map/ppermute | solution.py:447
  294.1 27.8 %collective-permute-start.43 = (bf16[4,584,128]{2,1,0:T(8,128)(2,1)}, bf16[4,584,128]{2,1,0:T(8,128)(2,1)}, u32[]{:S(2)}, u32[]{:S(2)}) collective-permute-start(bf16[4,584,128]{2,1,0:T(8,128)(2,1)} %get-tuple-element.228), channel_id=1, source_target_pairs={{0,24},{8,16},{16,8},{24,0},{1,25},{9,17},{17,9},{25,1},{2,26},{10... | collective-permute-start | bytes 1794056 | tf_op jit(solution)/shard_map/ppermute | solution.py:447
  (66 other events, 513.6 us)
Sparse Core Ops, SparseCore 0:
  59.2 40.5 all-gather.2
  179.9 52.1 reduce-scatter.2
  245.2 36.4 reduce-scatter.4
